TPU v7x, 32 devices: a whole 2x2x4 slice. The times are simulated.
32 devices in a mesh: members: 2 (over x), lon: 16 (over z, y, core).
Axes of the slice: x: 2, y: 2, z: 4, core: 2. Of those that a mesh axis runs over, the one named last changes fastest.
Arguments:
- analysis_grad: bfloat16 [32768, 450], P(('members', 'lon')), parts along dimension 0, may hold values from -6 to 6
- requests: int32 [48, 256], P('lon'), may hold values from 0 to 1023
- slot_pos: int32 [32768, 16], P('lon'), may hold values from 0 to 767
- slot_weight: float32 [32768, 16], P('lon'), may hold values from 0.05 to 1
- slot_count: int32 [32768], P('lon'), may hold values from 1 to 16
- fold_src: int32 [1024], P('lon'), may hold values from 0 to 63
Outputs:
- ocean_grad: bfloat16 [65536, 450], P(('members', 'lon')), parts along dimension 0
There are 2 independent parts, one for each index of `members`. A program takes and returns all parts, laid end to end along the dimension named above; an argument that names none is the same for every part. Nothing has to cross between parts.
Inputs may be any that keep to these rules, and one draw needn't show every extreme that they name: `requests`: local row numbers within the owner's block of 1024 analysis cells.
All inputs are finite; a program needn't handle non-finite values.
Results may differ from a plain program's by a relative error of at most 0.0041.
Values may be sent and summed in bfloat16 or wider, within the bound.
No kernel may reach another device: no remote copies, remote signals or barrier semaphores. Data moves between devices by JAX's collectives and lax.ppermute only.
A program may use at most 64 MiB of HBM per device.

v0:
```python
import math

import jax
import jax.numpy as jnp
from jax import lax
from jax.sharding import PartitionSpec as P


def passed_along(block, axis, distance):
    devices = range(lax.axis_size(axis))
    route = [((i - distance) % len(devices), i) for i in devices]
    return lax.ppermute(block, axis, route)


def swapped(value, axis, bit):
    mask = 2**bit
    pairs = [(source, source ^ mask) for source in range(lax.axis_size(axis))]
    return lax.ppermute(value, axis, pairs)


def normalized(slot_weight, slot_count):
    slots = slot_weight.shape[1]
    valid = jnp.arange(slots, dtype=jnp.int32)[None, :] < slot_count[:, None]
    masked = jnp.where(valid, slot_weight, jnp.float32(0.0))
    return masked / jnp.sum(masked, axis=1, keepdims=True)


def pull_rows(fetched, slot_pos, weights):
    rows, slots = slot_pos.shape
    block = math.gcd(rows, 512)
    count = rows // block
    places = slot_pos.reshape(count, block, slots)
    scales = weights.reshape(count, block, slots)

    def one_block(pair):
        taken = fetched[pair[0]]
        return jnp.einsum("ok,okc->oc", pair[1], taken, preferred_element_type=jnp.float32)

    return lax.map(one_block, (places, scales)).reshape(rows, fetched.shape[1])


def local(analysis_grad, requests, slot_pos, slot_weight, slot_count, fold_src):
    lanes = lax.axis_size("lon")
    pieces = []
    for offset in (-1, 0, 1):
        wanted = requests[offset + 1]
        if offset == 0:
            pieces.append(analysis_grad[wanted])
        else:
            asked = passed_along(wanted, "lon", offset)
            picked = analysis_grad[asked]
            pieces.append(passed_along(picked, "lon", -offset))
    fetched = jnp.concatenate(pieces, axis=0)
    weights = normalized(slot_weight, slot_count).astype(jnp.bfloat16)
    pulled = pull_rows(fetched, slot_pos, weights)
    rows = pulled.shape[0]
    fold = fold_src.shape[0]
    edge = pulled[rows - fold :]
    mirror = swapped(edge.astype(jnp.bfloat16), "lon", lanes.bit_length() - 2).astype(edge.dtype)
    folded = edge + mirror[fold_src]
    return jnp.concatenate([pulled[: rows - fold], folded], axis=0).astype(jnp.bfloat16)


def solution(mesh):
    in_specs = (
        P(("members", "lon"), None),
        P("lon", None),
        P("lon", None),
        P("lon", None),
        P("lon"),
        P("lon"),
    )
    out_specs = P(("members", "lon"), None)
    return jax.shard_map(local, mesh=mesh, in_specs=in_specs, out_specs=out_specs, check_vma=False)
```

profile of v0, /device:TPU:0, one launch (start us, length us, event | category | flops | bytes accessed | tf_op | source)
XLA Modules:
  0.0 192.4 jit_solution(7405122760111322928)
XLA Ops:
  0.0 0.8 fusion.2
  0.8 5.4 %collective-permute-start = (s32[256]{0:T(256)S(1)}, s32[256]{0:T(256)S(1)}, u32[]{:S(2)}, u32[]{:S(2)}) collective-permute-start(s32[256]{0:T(256)S(1)} %bitcast.42), channel_id=1, source_target_pairs={{1,0},{2,1},{3,2},{4,3},{5,4},{6,5},{7,6},{8,7},{9,8},{10,9},{11,1... | collective-permute-start | bytes 3080 | tf_op jit(solution)/shard_map/ppermute | solution.py:12
  6.2 0.9 fusion.1
  7.2 0.9 divide_convert_fusion
  8.1 0.7 compare_select_fusion.1
  8.8 1.5 copy.11
  10.3 1.2 gather_fusion.1
  11.9 1.2 gather_fusion.3
  13.1 4.2 %collective-permute-start.3 = (bf16[256,450]{1,0:T(8,128)(2,1)S(1)}, bf16[256,450]{1,0:T(8,128)(2,1)S(1)}, u32[]{:S(2)}, u32[]{:S(2)}) collective-permute-start(bf16[256,450]{1,0:T(8,128)(2,1)S(1)} %gather_fusion.3), channel_id=1, source_target_pairs={{1,0},{2,1},{3,2},{4,3},{5,4},{6,5},{7,6},{8,7},{9,8},{10,9},{11,1... | collective-permute-start | bytes 691208 | tf_op jit(solution)/shard_map/ppermute | solution.py:12
  17.2 1.2 gather_fusion.2
  18.8 1.3 collective-permute-done.1
  20.0 1.1 collective-permute-done.3
  21.2 159.3 %while.10 = (s32[]{:T(128)}, f32[4,512,450]{2,1,0:T(8,128)}, bf16[4,512,16]{1,2,0:T(8,128)(2,1)S(1)}, s32[4,512,16]{2,1,0:T(8,128)S(1)}, bf16[768,450]{1,0:T(8,128)(2,1)S(1)}, /*index=5*/s32[]{:T(128)}) while((s32[]{:T(128)}, f32[4,512,450]{2,1,0:T(8,128)}, bf16[4,512,16]{1,2,0:T(8,128)(2,1)S(1)}, s32[4,512,16]{2,1,0:T(8,128)S(1)}, ...), condition=%wide.region_2.3_spmd, body=%wide.region_1.2_spmd.sunk | while | flops 7405570 | bytes 25322060 | solution.py:39
  21.4 33.8 %gather_fusion = bf16[8192,450]{1,0:T(8,128)(2,1)} fusion(bf16[768,450]{1,0:T(8,128)(2,1)S(1)} %get-tuple-element.97, s32[8192]{0:T(1024)S(1)} %broadcast_clamp_fusion.2), kind=kCustom, calls=%fused_computation.clone.1 | custom fusion | bytes 14778368 | tf_op jit(solution)/shard_map/while/body/eval_jaxpr/gather | solution.py:36
  55.4 4.6 %fusion.11 = f32[512,1,450]{2,1,0:T(1,128)S(1)} fusion(bf16[512,16,1]{1,2,0:T(2,128)(2,1)S(1)} %copy.27, bf16[512,16,450]{2,1,0:T(8,128)(2,1)} %bitcast.36), kind=kOutput, calls=%fused_computation.28.clone.1 | convolution fusion | flops 7372800 | bytes 8310784 | tf_op jit(solution)/shard_map/while/body/eval_jaxpr/ok,okc->oc/dot_general | solution.py:37
  60.0 1.1 bitcast_dynamic-update-slice_fusion.2
  61.3 33.8 %gather_fusion = bf16[8192,450]{1,0:T(8,128)(2,1)} fusion(bf16[768,450]{1,0:T(8,128)(2,1)S(1)} %get-tuple-element.97, s32[8192]{0:T(1024)S(1)} %broadcast_clamp_fusion.2), kind=kCustom, calls=%fused_computation.clone.1 | custom fusion | bytes 14778368 | tf_op jit(solution)/shard_map/while/body/eval_jaxpr/gather | solution.py:36
  95.3 4.6 %fusion.11 = f32[512,1,450]{2,1,0:T(1,128)S(1)} fusion(bf16[512,16,1]{1,2,0:T(2,128)(2,1)S(1)} %copy.27, bf16[512,16,450]{2,1,0:T(8,128)(2,1)} %bitcast.36), kind=kOutput, calls=%fused_computation.28.clone.1 | convolution fusion | flops 7372800 | bytes 8310784 | tf_op jit(solution)/shard_map/while/body/eval_jaxpr/ok,okc->oc/dot_general | solution.py:37
  99.9 1.0 bitcast_dynamic-update-slice_fusion.2
  101.1 33.8 %gather_fusion = bf16[8192,450]{1,0:T(8,128)(2,1)} fusion(bf16[768,450]{1,0:T(8,128)(2,1)S(1)} %get-tuple-element.97, s32[8192]{0:T(1024)S(1)} %broadcast_clamp_fusion.2), kind=kCustom, calls=%fused_computation.clone.1 | custom fusion | bytes 14778368 | tf_op jit(solution)/shard_map/while/body/eval_jaxpr/gather | solution.py:36
  135.1 4.6 %fusion.11 = f32[512,1,450]{2,1,0:T(1,128)S(1)} fusion(bf16[512,16,1]{1,2,0:T(2,128)(2,1)S(1)} %copy.27, bf16[512,16,450]{2,1,0:T(8,128)(2,1)} %bitcast.36), kind=kOutput, calls=%fused_computation.28.clone.1 | convolution fusion | flops 7372800 | bytes 8310784 | tf_op jit(solution)/shard_map/while/body/eval_jaxpr/ok,okc->oc/dot_general | solution.py:37
  139.7 1.0 bitcast_dynamic-update-slice_fusion.2
  140.9 33.8 %gather_fusion = bf16[8192,450]{1,0:T(8,128)(2,1)} fusion(bf16[768,450]{1,0:T(8,128)(2,1)S(1)} %get-tuple-element.97, s32[8192]{0:T(1024)S(1)} %broadcast_clamp_fusion.2), kind=kCustom, calls=%fused_computation.clone.1 | custom fusion | bytes 14778368 | tf_op jit(solution)/shard_map/while/body/eval_jaxpr/gather | solution.py:36
  174.9 4.6 %fusion.11 = f32[512,1,450]{2,1,0:T(1,128)S(1)} fusion(bf16[512,16,1]{1,2,0:T(2,128)(2,1)S(1)} %copy.27, bf16[512,16,450]{2,1,0:T(8,128)(2,1)} %bitcast.36), kind=kOutput, calls=%fused_computation.28.clone.1 | convolution fusion | flops 7372800 | bytes 8310784 | tf_op jit(solution)/shard_map/while/body/eval_jaxpr/ok,okc->oc/dot_general | solution.py:37
  179.5 1.1 bitcast_dynamic-update-slice_fusion.2
  180.5 0.9 slice.38
  181.6 3.7 %slice.37 = bf16[1984,450]{1,0:T(8,128)(2,1)} slice(f32[2048,450]{1,0:T(8,128)} %bitcast.11), slice={[0:1984], [0:450]} | slice | bytes 3571200 | tf_op jit(solution)/shard_map/slice | solution.py:61
  185.3 1.4 collective-permute-done.4
  186.7 0.7 gather_fusion.4
  187.4 0.9 add_convert_fusion
  188.3 1.8 pad_maximum_fusion
  190.1 2.3 %copy.16 = bf16[2048,450]{0,1:T(8,128)(2,1)} copy(bf16[2048,450]{1,0:T(8,128)(2,1)S(1)} %pad_maximum_fusion) | data formatting | bytes 3686400 | tf_op jit(solution)/shard_map/concatenate | solution.py:61
  (41 shorter events, 2.3 us)
Async XLA Ops:
  0.8 9.5 %collective-permute-start = (s32[256]{0:T(256)S(1)}, s32[256]{0:T(256)S(1)}, u32[]{:S(2)}, u32[]{:S(2)}) collective-permute-start(s32[256]{0:T(256)S(1)} %bitcast.42), channel_id=1, source_target_pairs={{1,0},{2,1},{3,2},{4,3},{5,4},{6,5},{7,6},{8,7},{9,8},{10,9},{11,1... | collective-permute-start | bytes 3080 | tf_op jit(solution)/shard_map/ppermute | solution.py:12
  6.2 5.7 %collective-permute-start.2 = (s32[256]{0:T(256)S(1)}, s32[256]{0:T(256)S(1)}, u32[]{:S(2)}, u32[]{:S(2)}) collective-permute-start(s32[256]{0:T(256)S(1)} %bitcast.41), channel_id=1, source_target_pairs={{15,0},{0,1},{1,2},{2,3},{3,4},{4,5},{5,6},{6,7},{7,8},{8,9},{9,10... | collective-permute-start | bytes 3080 | tf_op jit(solution)/shard_map/ppermute | solution.py:12
  8.8 9.6 %copy-start = (s32[2048,16]{0,1:T(8,128)S(1)}, s32[2048,16]{0,1:T(8,128)}, u32[]{:S(2)}) copy-start(s32[2048,16]{0,1:T(8,128)} %param.10) | copy-start | bytes 393220
  10.3 8.4 %copy-start.1 = (s32[64]{0:T(128)S(1)}, s32[64]{0:T(128)}, u32[]{:S(2)}) copy-start(s32[64]{0:T(128)} %param.13) | copy-start | bytes 772
  11.5 8.5 %collective-permute-start.1 = (bf16[256,450]{1,0:T(8,128)(2,1)S(1)}, bf16[256,450]{1,0:T(8,128)(2,1)S(1)}, u32[]{:S(2)}, u32[]{:S(2)}) collective-permute-start(bf16[256,450]{1,0:T(8,128)(2,1)S(1)} %gather_fusion.1), channel_id=1, source_target_pairs={{15,0},{0,1},{1,2},{2,3},{3,4},{4,5},{5,6},{6,7},{7,8},{8,9},{9,10... | collective-permute-start | bytes 691208 | tf_op jit(solution)/shard_map/ppermute | solution.py:12
  13.1 8.1 %collective-permute-start.3 = (bf16[256,450]{1,0:T(8,128)(2,1)S(1)}, bf16[256,450]{1,0:T(8,128)(2,1)S(1)}, u32[]{:S(2)}, u32[]{:S(2)}) collective-permute-start(bf16[256,450]{1,0:T(8,128)(2,1)S(1)} %gather_fusion.3), channel_id=1, source_target_pairs={{1,0},{2,1},{3,2},{4,3},{5,4},{6,5},{7,6},{8,7},{9,8},{10,9},{11,1... | collective-permute-start | bytes 691208 | tf_op jit(solution)/shard_map/ppermute | solution.py:12
  181.5 5.2 %collective-permute-start.4 = (bf16[64,450]{1,0:T(8,128)(2,1)S(1)}, bf16[64,450]{1,0:T(8,128)(2,1)S(1)}, u32[]{:S(2)}, u32[]{:S(2)}) collective-permute-start(bf16[64,450]{1,0:T(8,128)(2,1)S(1)} %slice.38), channel_id=1, source_target_pairs={{0,8},{1,9},{2,10},{3,11},{4,12},{5,13},{6,14},{7,15},{8,0},{9,1},... | collective-permute-start | bytes 172808 | tf_op jit(solution)/shard_map/ppermute | solution.py:18
where the time goes:
time: 193 us; the launch traced here: 192 us
  local copies, waits for them, and re-layouts  154 us (80%)
  matrix products  18.4 us (10%)
  starting transfers between devices  9.75 us (5%)
  other arithmetic  5.62 us (3%)
  waiting for transfers between devices  4.11 us (2%)
    gather x4, local copies, waits for them, and re-layouts, one_block(): taken = fetched[pair[0]]  135 us
    dot_general x4, matrix products, one_block(): jnp.einsum('ok,okc->oc', pair[1], taken, preferred_element_type=jnp.float32)  18.4 us
    ppermute x4, starting transfers between devices, passed_along(): return lax.ppermute(block, axis, route)  9.68 us
    dynamic_update_slice x4, local copies, waits for them, and re-layouts, pull_rows(): return lax.map(one_block, (places, scales)).reshape(rows, fetched.shape[1])  4.29 us
  transfers between devices with their start and end apart: 5, of which 4 were waited for; matrix products, arithmetic and copies ran while one was open for 6% of the time, Pallas kernels for 0%

commit v1 on v0

v1 whole, which is shorter than its diff:
```python
import functools

import jax
import jax.numpy as jnp
from jax import lax
from jax.experimental import pallas as pl
from jax.experimental.pallas import tpu as pltpu
from jax.sharding import PartitionSpec as P

LANES = 128
PACK = 16
VMEM = pl.BlockSpec(memory_space=pltpu.VMEM)


def passed_along(block, axis, distance):
    count = lax.axis_size(axis)
    route = [((i - distance) % count, i) for i in range(count)]
    return lax.ppermute(block, axis, route)


def row_ids(shape):
    return lax.broadcasted_iota(jnp.int32, shape, 0)


def weights_kernel(pos_ref, weight_ref, count_ref, w_ref, *, near, cap):
    slots, cells = pos_ref.shape

    def one_tile(tile, carry):
        lanes = pl.ds(pl.multiple_of(tile * LANES, LANES), LANES)
        pos = pos_ref[:, lanes]
        valid = row_ids((slots, LANES)) < count_ref[:, lanes]
        masked = jnp.where(valid, weight_ref[:, lanes], jnp.float32(0.0))
        scale = masked / jnp.sum(masked, axis=0, keepdims=True)
        scale = scale.astype(jnp.bfloat16).astype(jnp.float32)
        merged = jnp.zeros((slots, LANES), jnp.float32)
        for k in range(slots):
            merged += jnp.where(pos == pos[k : k + 1], scale[k : k + 1], jnp.float32(0.0))
        spread = [jnp.broadcast_to(merged[k : k + 1], (PACK, LANES)).astype(jnp.bfloat16) for k in range(slots)]
        row = row_ids((PACK, LANES)).astype(jnp.float32).astype(jnp.bfloat16)
        for piece in range(near):
            local = pos - piece * cap
            local = jnp.where((local >= 0) & (local < cap), local, -1).astype(jnp.float32)
            place = [jnp.broadcast_to(local[k : k + 1], (PACK, LANES)).astype(jnp.bfloat16) for k in range(slots)]
            for group in range(cap // PACK):
                here = row + jnp.bfloat16(group * PACK)
                acc = jnp.zeros((PACK, LANES), jnp.bfloat16)
                for k in range(slots):
                    acc = jnp.where(place[k] == here, spread[k], acc)
                w_ref[pl.ds(piece * cap + group * PACK, PACK), lanes] = acc
        return carry

    lax.fori_loop(0, cells // LANES, one_tile, 0)


def dense_weights(pos, weight, count, near, cap):
    slots, cells = pos.shape
    return pl.pallas_call(
        functools.partial(weights_kernel, near=near, cap=cap),
        out_shape=jax.ShapeDtypeStruct((near * cap, cells), jnp.bfloat16),
        in_specs=[VMEM] * 3,
        out_specs=VMEM,
        compiler_params=pltpu.CompilerParams(vmem_limit_bytes=16 * 2**20),
        cost_estimate=pl.CostEstimate(flops=near * cap * cells * slots * 2, bytes_accessed=near * cap * cells * 2, transcendentals=0),
    )(pos, weight, count)


def chosen(grad, wanted):
    hit = row_ids((grad.shape[1], wanted.shape[1])) == wanted
    onehot = jnp.where(hit, jnp.float32(1.0), jnp.float32(0.0)).astype(jnp.bfloat16)
    return jnp.dot(grad, onehot, preferred_element_type=jnp.float32).astype(jnp.bfloat16)


def pick_kernel(grad_ref, own_ref, west_ref, east_ref, own_out, west_out, east_out):
    grad = grad_ref[...]
    own_out[...] = chosen(grad, own_ref[1:2, :])
    west_out[...] = chosen(grad, west_ref[2:3, :])
    east_out[...] = chosen(grad, east_ref[0:1, :])


def picked(grad, own, west, east):
    cols, cap = grad.shape[0], own.shape[1]
    shape = jax.ShapeDtypeStruct((cols, cap), jnp.bfloat16)
    return pl.pallas_call(
        pick_kernel,
        out_shape=(shape,) * 3,
        in_specs=[VMEM] * 4,
        out_specs=(VMEM,) * 3,
        compiler_params=pltpu.CompilerParams(vmem_limit_bytes=16 * 2**20),
    )(grad, own, west, east)


def mixed(parts, w_ref, lanes):
    cap = parts[0].shape[1]
    acc = None
    for i, part in enumerate(parts):
        term = jnp.dot(part[...], w_ref[pl.ds(i * cap, cap), lanes], preferred_element_type=jnp.float32)
        acc = term if acc is None else acc + term
    return acc


def edge_kernel(west_ref, own_ref, east_ref, w_ref, sum_ref, edge_ref):
    cells = w_ref.shape[1]
    total = mixed((west_ref, own_ref, east_ref), w_ref, pl.ds(cells - LANES, LANES))
    sum_ref[...] = total
    edge_ref[...] = total.astype(jnp.bfloat16)


def edge_sums(west, own, east, dense):
    cols = own.shape[0]
    return pl.pallas_call(
        edge_kernel,
        out_shape=(jax.ShapeDtypeStruct((cols, LANES), jnp.float32), jax.ShapeDtypeStruct((cols, LANES), jnp.bfloat16)),
        in_specs=[VMEM] * 4,
        out_specs=(VMEM,) * 2,
        compiler_params=pltpu.CompilerParams(vmem_limit_bytes=16 * 2**20),
    )(west, own, east, dense)


def body_kernel(west_ref, own_ref, east_ref, w_ref, out_ref):
    width = out_ref.shape[1]
    lanes = pl.ds(pl.multiple_of(pl.program_id(0) * width, width), width)
    out_ref[...] = mixed((west_ref, own_ref, east_ref), w_ref, lanes).astype(jnp.bfloat16)


def body_sums(west, own, east, dense):
    cols, cells = own.shape[0], dense.shape[1]
    width = 2 * LANES
    return pl.pallas_call(
        body_kernel,
        grid=(cells // width,),
        out_shape=jax.ShapeDtypeStruct((cols, cells), jnp.bfloat16),
        in_specs=[VMEM] * 4,
        out_specs=pl.BlockSpec((cols, width), lambda i: (0, i)),
        compiler_params=pltpu.CompilerParams(vmem_limit_bytes=16 * 2**20),
        cost_estimate=pl.CostEstimate(flops=2 * cols * dense.shape[0] * cells, bytes_accessed=cols * cells * 2, transcendentals=0),
    )(west, own, east, dense)


def fold_kernel(whole_ref, sum_ref, mirror_ref, src_ref, out_ref):
    del whole_ref
    fold = src_ref.shape[1]
    first = LANES - fold
    source = jnp.concatenate([jnp.full((1, first), -1, jnp.int32), src_ref[...] + first], axis=1)
    hit = row_ids((LANES, LANES)) == source
    onehot = jnp.where(hit, jnp.float32(1.0), jnp.float32(0.0)).astype(jnp.bfloat16)
    other = jnp.dot(mirror_ref[...], onehot, preferred_element_type=jnp.float32)
    out_ref[...] = (sum_ref[...] + other).astype(jnp.bfloat16)


def folded(whole, sums, mirror, fold_src):
    cols, cells = whole.shape
    last = cells // LANES - 1
    return pl.pallas_call(
        fold_kernel,
        grid=(1,),
        out_shape=jax.ShapeDtypeStruct((cols, cells), jnp.bfloat16),
        in_specs=[pl.BlockSpec(memory_space=pl.ANY), VMEM, VMEM, VMEM],
        out_specs=pl.BlockSpec((cols, LANES), lambda i: (0, last)),
        input_output_aliases={0: 0},
        compiler_params=pltpu.CompilerParams(vmem_limit_bytes=8 * 2**20),
    )(whole, sums, mirror, fold_src)


def local(analysis_grad, requests, slot_pos, slot_weight, slot_count, fold_src):
    near, cap = requests.shape
    around = lax.axis_size("lon")
    to_west = passed_along(requests, "lon", -1)
    to_east = passed_along(requests, "lon", 1)
    dense = dense_weights(slot_pos.T, slot_weight.T, slot_count[None, :], near, cap)
    own, for_west, for_east = picked(analysis_grad.T, requests, to_east, to_west)
    from_east = passed_along(for_west, "lon", -1)
    from_west = passed_along(for_east, "lon", 1)
    sums, edge = edge_sums(from_west, own, from_east, dense)
    mirror = passed_along(edge, "lon", around // 2)
    whole = body_sums(from_west, own, from_east, dense)
    return folded(whole, sums, mirror, fold_src[None, :]).T


def solution(mesh):
    in_specs = (
        P(("members", "lon"), None),
        P("lon", None),
        P("lon", None),
        P("lon", None),
        P("lon"),
        P("lon"),
    )
    out_specs = P(("members", "lon"), None)
    return jax.shard_map(local, mesh=mesh, in_specs=in_specs, out_specs=out_specs, check_vma=False)
```

time: 193 us -> 28.6 us (0.15)
  local copies, waits for them, and re-layouts: 154 us -> 4.38 us
  matrix products: 18.4 us -> 0 us
  Pallas kernels: 0 us -> 11.2 us
  other arithmetic: 5.62 us -> 0 us
    gather x8 -> x0, local copies, waits for them, and re-layouts: 139 us -> none  [the longest x4 135 us: one_block(): taken = fetched[pair[0]]]
    dot_general x4 -> x0, matrix products: 18.4 us -> none  [one_block(): jnp.einsum('ok,okc->oc', pair[1], taken, preferred_element_type=jnp.float32)]
    pallas_call x0 -> x5, Pallas kernels: none -> 11.2 us  [the longest x1 4.62 us: body_sums(): pl.pallas_call(body_kernel, grid=(cells // width,), out_shape=jax.ShapeDt...]
    slice x3 -> x0, local copies, waits for them, and re-layouts: 5.41 us -> none  [the longest x1 3.73 us: local(): pulled[:rows - fold]]
    dynamic_update_slice x4 -> x0, local copies, waits for them, and re-layouts: 4.29 us -> none  [pull_rows(): return lax.map(one_block, (places, scales)).reshape(rows, fetched.shape[1])]
    unnamed x5 -> x12, local copies, waits for them, and re-layouts: 1.51 us -> 4.38 us
    concatenate x1 -> x0, local copies, waits for them, and re-layouts: 2.3 us -> none  [local(): jnp.concatenate([pulled[:rows - fold], folded], axis=0).astype(jnp.bfloat16)]
    concatenate x2 -> x0, other arithmetic: 1.94 us -> none  [the longest x1 1.84 us: local(): jnp.concatenate([pulled[:rows - fold], folded], axis=0).astype(jnp.bfloat16)]
  transfers between devices with their start and end apart: 5 -> 5, of which waited for: 4 -> 2; matrix products, arithmetic and copies ran while one was open for 6% -> 0% of each run, Pallas kernels for 0% -> 32%
where the time goes in v1:
time: 28.6 us; the launch traced here: 28.3 us
  Pallas kernels  11.2 us (39%)
  starting transfers between devices  10 us (35%)
  local copies, waits for them, and re-layouts  4.38 us (15%)
  waiting for transfers between devices  2.62 us (9%)
    ppermute x5, starting transfers between devices, passed_along(): return lax.ppermute(block, axis, route)  10 us
    pallas_call x1, Pallas kernels, body_sums(): pl.pallas_call(body_kernel, grid=(cells // width,), out_shape=jax.ShapeDt...  4.62 us
    pallas_call x1, Pallas kernels, dense_weights(): pl.pallas_call(functools.partial(weights_kernel, near=near, cap=cap), out...  4.42 us
    unnamed x12, local copies, waits for them, and re-layouts  4.38 us
    ppermute x5, waiting for transfers between devices, passed_along(): return lax.ppermute(block, axis, route)  2.62 us
    pallas_call x1, Pallas kernels, folded(): pl.pallas_call(fold_kernel, grid=(1,), out_shape=jax.ShapeDtypeStruct((co...  0.93 us
    pallas_call x1, Pallas kernels, picked(): pl.pallas_call(pick_kernel, out_shape=(shape,) * 3, in_specs=[VMEM] * 4,...  0.91 us
  transfers between devices with their start and end apart: 5, of which 2 were waited for; matrix products, arithmetic and copies ran while one was open for 0% of the time, Pallas kernels for 32%

profile of v1, /device:TPU:0, one launch (start us, length us, event | category | flops | bytes accessed | tf_op | source)
XLA Modules:
  0.0 28.3 jit_solution(7929316185789842576)
XLA Ops:
  0.0 0.5 %collective-permute-start = (s32[3,256]{1,0:T(4,128)}, s32[3,256]{1,0:T(4,128)S(1)}, u32[]{:S(2)}, u32[]{:S(2)}) collective-permute-start(s32[3,256]{1,0:T(4,128)} %own_ref.1), channel_id=1, source_target_pairs={{15,0},{0,1},{1,2},{2,3},{3,4},{4,5},{5,6},{6,7},{7,8},{8,9},{9,10... | collective-permute-start | bytes 9224 | tf_op jit(solution)/shard_map/ppermute | solution.py:18
  0.5 5.0 %collective-permute-start.1 = (s32[3,256]{1,0:T(4,128)}, s32[3,256]{1,0:T(4,128)S(1)}, u32[]{:S(2)}, u32[]{:S(2)}) collective-permute-start(s32[3,256]{1,0:T(4,128)} %own_ref.1), channel_id=1, source_target_pairs={{1,0},{2,1},{3,2},{4,3},{5,4},{6,5},{7,6},{8,7},{9,8},{10,9},{11,1... | collective-permute-start | bytes 9224 | tf_op jit(solution)/shard_map/ppermute | solution.py:18
  5.4 1.5 %collective-permute-done.west_ref = s32[3,256]{1,0:T(4,128)S(1)} collective-permute-done((s32[3,256]{1,0:T(4,128)}, s32[3,256]{1,0:T(4,128)S(1)}, u32[]{:S(2)}, u32[]{:S(2)}) %collective-permute-start) | collective-permute-done | bytes 3104 | tf_op jit(solution)/shard_map/ppermute | solution.py:18
  6.9 0.0 collective-permute-done.1.east_ref
  7.0 0.0 copy-start
  7.0 1.2 %copy-done = bf16[1024,450]{0,1:T(8,128)(2,1)S(1)} copy-done((bf16[1024,450]{0,1:T(8,128)(2,1)S(1)}, bf16[1024,450]{0,1:T(8,128)(2,1)}, u32[]{:S(2)}) %copy-start) | copy-done | bytes 921624
  8.2 0.0 copy-start.4
  8.2 0.7 %copy-done.4 = s32[3,256]{1,0:T(4,128)S(1)} copy-done((s32[3,256]{1,0:T(4,128)S(1)}, s32[3,256]{1,0:T(4,128)}, u32[]{:S(2)}) %copy-start.4) | copy-done | bytes 3096
  8.9 0.9 %shard_map.64 = (bf16[450,256]{1,0:T(8,128)(2,1)S(1)}, bf16[450,256]{1,0:T(8,128)(2,1)S(1)}, bf16[450,256]{1,0:T(8,128)(2,1)S(1)}) custom-call(bf16[450,1024]{1,0:T(8,128)(2,1)S(1)} %bitcast.6, s32[3,256]{1,0:T(4,128)S(1)} %copy-done.4, s32[3,256]{1,0:T(4,128)S(1)} %collective-permute-done.west_ref, s32[3,256]{1,0:T(4,128)S(1)} %collective-permute-done.1.east_ref), custom_call_target="tpu_custom_call" | custom-call | tf_op jit(solution)/shard_map/pallas_call | solution.py:83
  9.8 0.1 collective-permute-start.2
  9.8 4.5 %collective-permute-start.3 = (bf16[450,256]{1,0:T(8,128)(2,1)S(1)}, bf16[450,256]{1,0:T(8,128)(2,1)S(1)}, u32[]{:S(2)}, u32[]{:S(2)}) collective-permute-start(bf16[450,256]{1,0:T(8,128)(2,1)S(1)} %get-tuple-element.12), channel_id=1, source_target_pairs={{1,0},{2,1},{3,2},{4,3},{5,4},{6,5},{7,6},{8,7},{9,8},{10,9},{11,1... | collective-permute-start | bytes 691208 | tf_op jit(solution)/shard_map/ppermute | solution.py:18
  14.3 0.0 copy-start.1
  14.3 0.9 %copy-done.1 = s32[2048,16]{0,1:T(8,128)S(1)} copy-done((s32[2048,16]{0,1:T(8,128)S(1)}, s32[2048,16]{0,1:T(8,128)}, u32[]{:S(2)}) %copy-start.1) | copy-done | bytes 131096
  15.2 0.0 copy-start.2
  15.2 0.9 %copy-done.2 = f32[2048,16]{0,1:T(8,128)S(1)} copy-done((f32[2048,16]{0,1:T(8,128)S(1)}, f32[2048,16]{0,1:T(8,128)}, u32[]{:S(2)}) %copy-start.2) | copy-done | bytes 131096
  16.1 0.0 copy-start.3
  16.1 0.7 %copy-done.3 = s32[2048]{0:T(1024)S(1)} copy-done((s32[2048]{0:T(1024)S(1)}, s32[2048]{0:T(1024)}, u32[]{:S(2)}) %copy-start.3) | copy-done | bytes 8216
  16.8 4.4 %shard_map.65.w_ref = bf16[768,2048]{1,0:T(8,128)(2,1)S(1)} custom-call(s32[16,2048]{1,0:T(8,128)S(1)} %bitcast.7, f32[16,2048]{1,0:T(8,128)S(1)} %bitcast.8, s32[1,2048]{1,0:T(1,128)S(1)} %bitcast.9), custom_call_target="tpu_custom_call" | custom-call | flops 50331648 | bytes 3145728 | tf_op jit(solution)/shard_map/pallas_call | solution.py:57
  21.2 0.0 collective-permute-done.2.west_ref
  21.2 0.0 collective-permute-done.3.east_ref
  21.3 0.4 %shard_map.67 = (f32[450,128]{1,0:T(8,128)S(1)}, bf16[450,128]{1,0:T(8,128)(2,1)S(1)}) custom-call(bf16[450,256]{1,0:T(8,128)(2,1)S(1)} %collective-permute-done.2.west_ref, bf16[450,256]{1,0:T(8,128)(2,1)S(1)} %get-tuple-element.11.own_ref, bf16[450,256]{1,0:T(8,128)(2,1)S(1)} %collective-permute-done.3.east_ref, bf16[768,2048]{1,0:T(8,128)(2,1)S(1)} %shard_map.65.w_ref), custom_call_target="tpu_custom_call" | custom-call | tf_op jit(solution)/shard_map/pallas_call | solution.py:110
  21.6 0.0 copy-start.5
  21.6 0.1 collective-permute-start.4
  21.7 4.6 %shard_map.66.whole_ref = bf16[450,2048]{1,0:T(8,128)(2,1)} custom-call(bf16[450,256]{1,0:T(8,128)(2,1)S(1)} %collective-permute-done.2.west_ref, bf16[450,256]{1,0:T(8,128)(2,1)S(1)} %get-tuple-element.11.own_ref, bf16[450,256]{1,0:T(8,128)(2,1)S(1)} %collective-permute-done.3.east_ref, bf16[768,2048]{1,0:T(8,128)(2,1)S(1)} %shard_map.65.w_ref), custom_call_target="tpu_custom_call" | custom-call | flops 1415577600 | bytes 1843200 | tf_op jit(solution)/shard_map/pallas_call | solution.py:128
  26.3 1.1 %collective-permute-done.4.mirror_ref = bf16[450,128]{1,0:T(8,128)(2,1)S(1)} collective-permute-done((bf16[450,128]{1,0:T(8,128)(2,1)S(1)}, bf16[450,128]{1,0:T(8,128)(2,1)S(1)}, u32[]{:S(2)}, u32[]{:S(2)}) %collective-permute-start.4) | collective-permute-done | bytes 115232 | tf_op jit(solution)/shard_map/ppermute | solution.py:18
  27.4 0.0 copy-done.5
  27.4 0.9 %shard_map.68 = bf16[450,2048]{1,0:T(8,128)(2,1)} custom-call(bf16[450,2048]{1,0:T(8,128)(2,1)} %shard_map.66.whole_ref, f32[450,128]{1,0:T(8,128)S(1)} %get-tuple-element.13.sum_ref, bf16[450,128]{1,0:T(8,128)(2,1)S(1)} %collective-permute-done.4.mirror_ref, s32[1,64]{1,0:T(1,128)S(1)} %bitcast.10), custom_call_target="tpu_custom_call", output_to_operand_aliasing={{}: (0, {})} | custom-call | tf_op jit(solution)/shard_map/pallas_call | solution.py:153
Async XLA Ops:
  0.0 6.9 %collective-permute-start = (s32[3,256]{1,0:T(4,128)}, s32[3,256]{1,0:T(4,128)S(1)}, u32[]{:S(2)}, u32[]{:S(2)}) collective-permute-start(s32[3,256]{1,0:T(4,128)} %own_ref.1), channel_id=1, source_target_pairs={{15,0},{0,1},{1,2},{2,3},{3,4},{4,5},{5,6},{6,7},{7,8},{8,9},{9,10... | collective-permute-start | bytes 9224 | tf_op jit(solution)/shard_map/ppermute | solution.py:18
  0.5 6.5 %collective-permute-start.1 = (s32[3,256]{1,0:T(4,128)}, s32[3,256]{1,0:T(4,128)S(1)}, u32[]{:S(2)}, u32[]{:S(2)}) collective-permute-start(s32[3,256]{1,0:T(4,128)} %own_ref.1), channel_id=1, source_target_pairs={{1,0},{2,1},{3,2},{4,3},{5,4},{6,5},{7,6},{8,7},{9,8},{10,9},{11,1... | collective-permute-start | bytes 9224 | tf_op jit(solution)/shard_map/ppermute | solution.py:18
  7.0 1.2 %copy-start = (bf16[1024,450]{0,1:T(8,128)(2,1)S(1)}, bf16[1024,450]{0,1:T(8,128)(2,1)}, u32[]{:S(2)}) copy-start(bf16[1024,450]{0,1:T(8,128)(2,1)} %param.6) | copy-start | bytes 2764804
  8.2 0.7 %copy-start.4 = (s32[3,256]{1,0:T(4,128)S(1)}, s32[3,256]{1,0:T(4,128)}, u32[]{:S(2)}) copy-start(s32[3,256]{1,0:T(4,128)} %own_ref.1) | copy-start | bytes 9220
  9.8 11.5 %collective-permute-start.2 = (bf16[450,256]{1,0:T(8,128)(2,1)S(1)}, bf16[450,256]{1,0:T(8,128)(2,1)S(1)}, u32[]{:S(2)}, u32[]{:S(2)}) collective-permute-start(bf16[450,256]{1,0:T(8,128)(2,1)S(1)} %get-tuple-element.10), channel_id=1, source_target_pairs={{15,0},{0,1},{1,2},{2,3},{3,4},{4,5},{5,6},{6,7},{7,8},{8,9},{9,10... | collective-permute-start | bytes 691208 | tf_op jit(solution)/shard_map/ppermute | solution.py:18
  9.8 11.4 %collective-permute-start.3 = (bf16[450,256]{1,0:T(8,128)(2,1)S(1)}, bf16[450,256]{1,0:T(8,128)(2,1)S(1)}, u32[]{:S(2)}, u32[]{:S(2)}) collective-permute-start(bf16[450,256]{1,0:T(8,128)(2,1)S(1)} %get-tuple-element.12), channel_id=1, source_target_pairs={{1,0},{2,1},{3,2},{4,3},{5,4},{6,5},{7,6},{8,7},{9,8},{10,9},{11,1... | collective-permute-start | bytes 691208 | tf_op jit(solution)/shard_map/ppermute | solution.py:18
  14.3 0.9 %copy-start.1 = (s32[2048,16]{0,1:T(8,128)S(1)}, s32[2048,16]{0,1:T(8,128)}, u32[]{:S(2)}) copy-start(s32[2048,16]{0,1:T(8,128)} %param.8) | copy-start | bytes 393220
  15.2 0.9 %copy-start.2 = (f32[2048,16]{0,1:T(8,128)S(1)}, f32[2048,16]{0,1:T(8,128)}, u32[]{:S(2)}) copy-start(f32[2048,16]{0,1:T(8,128)} %param.9) | copy-start | bytes 393220
  16.1 0.7 %copy-start.3 = (s32[2048]{0:T(1024)S(1)}, s32[2048]{0:T(1024)}, u32[]{:S(2)}) copy-start(s32[2048]{0:T(1024)} %param.10) | copy-start | bytes 24580
  21.6 5.8 %copy-start.5 = (s32[64]{0:T(128)S(1)}, s32[64]{0:T(128)}, u32[]{:S(2)}) copy-start(s32[64]{0:T(128)} %param.11) | copy-start | bytes 772
  21.6 5.8 %collective-permute-start.4 = (bf16[450,128]{1,0:T(8,128)(2,1)S(1)}, bf16[450,128]{1,0:T(8,128)(2,1)S(1)}, u32[]{:S(2)}, u32[]{:S(2)}) collective-permute-start(bf16[450,128]{1,0:T(8,128)(2,1)S(1)} %get-tuple-element.14), channel_id=1, source_target_pairs={{8,0},{9,1},{10,2},{11,3},{12,4},{13,5},{14,6},{15,7},{0,8},{1,9},... | collective-permute-start | bytes 345608 | tf_op jit(solution)/shard_map/ppermute | solution.py:18

commit v2 on v1

v2 whole, which is shorter than its diff:
```python
import functools

import jax
import jax.numpy as jnp
from jax import lax
from jax.experimental import pallas as pl
from jax.experimental.pallas import tpu as pltpu
from jax.sharding import PartitionSpec as P

LANES = 128
PACK = 16
EARLY_TILES = 4
MIB = 2**20
VMEM = pl.BlockSpec(memory_space=pltpu.VMEM)
HBM = pl.BlockSpec(memory_space=pltpu.HBM)


def even_place():
    return lax.rem(lax.axis_index("lon"), 2) == 0


def row_ids(shape):
    return lax.broadcasted_iota(jnp.int32, shape, 0)


def lane_ids(shape):
    return lax.broadcasted_iota(jnp.int32, shape, 1)


def inner_swap(block):
    count = lax.axis_size("lon")
    return lax.ppermute(block, "lon", [(i, i ^ 1) for i in range(count)])


def outer_swap(block):
    count = lax.axis_size("lon")
    return lax.ppermute(block, "lon", [(i, (i - 1) % count if i % 2 == 0 else (i + 1) % count) for i in range(count)])


def half_away(block):
    count = lax.axis_size("lon")
    return lax.ppermute(block, "lon", [(i, (i + count // 2) % count) for i in range(count)])


def in_hbm(block):
    return pltpu.with_memory_space_constraint(block, pltpu.HBM)


def fill_tiles(pos_ref, weight_ref, count_ref, w_ref, first, tiles, near, cap):
    slots = pos_ref.shape[0]
    flip = jnp.where(even_place(), 0, near - 1)

    def one_tile(tile, carry):
        taken = pl.ds(pl.multiple_of((first + tile) * LANES, LANES), LANES)
        given = pl.ds(pl.multiple_of(tile * LANES, LANES), LANES)
        pos = pos_ref[:, taken]
        valid = row_ids((slots, LANES)) < count_ref[:, taken]
        masked = jnp.where(valid, weight_ref[:, taken], jnp.float32(0.0))
        scale = masked / jnp.sum(masked, axis=0, keepdims=True)
        scale = scale.astype(jnp.bfloat16).astype(jnp.float32)
        merged = jnp.zeros((slots, LANES), jnp.float32)
        for k in range(slots):
            merged += jnp.where(pos == pos[k : k + 1], scale[k : k + 1], jnp.float32(0.0))
        spread = [jnp.broadcast_to(merged[k : k + 1], (PACK, LANES)).astype(jnp.bfloat16) for k in range(slots)]
        row = row_ids((PACK, LANES)).astype(jnp.float32).astype(jnp.bfloat16)
        for piece in range(near):
            source = jnp.where(flip == 0, piece, near - 1 - piece)
            local = pos - source * cap
            local = jnp.where((local >= 0) & (local < cap), local, -1).astype(jnp.float32)
            place = [jnp.broadcast_to(local[k : k + 1], (PACK, LANES)).astype(jnp.bfloat16) for k in range(slots)]
            for group in range(cap // PACK):
                here = row + jnp.bfloat16(group * PACK)
                acc = jnp.zeros((PACK, LANES), jnp.bfloat16)
                for k in range(slots):
                    acc = jnp.where(place[k] == here, spread[k], acc)
                w_ref[pl.ds(piece * cap + group * PACK, PACK), given] = acc
        return carry

    lax.fori_loop(0, tiles, one_tile, 0)


def early_kernel(grad_hbm, pos_hbm, weight_hbm, count_hbm, own_hbm, grad_ref, pos_ref, weight_ref, count_ref, own_ref, w_ref, sems, *, near, cap):
    pairs = ((pos_hbm, pos_ref), (weight_hbm, weight_ref), (count_hbm, count_ref), (own_hbm, own_ref), (grad_hbm, grad_ref))
    copies = [pltpu.make_async_copy(source, target, sems.at[i]) for i, (source, target) in enumerate(pairs)]
    for copy in copies:
        copy.start()
    for copy in copies[:3]:
        copy.wait()
    tiles = w_ref.shape[1] // LANES
    fill_tiles(pos_ref, weight_ref, count_ref, w_ref, pos_ref.shape[1] // LANES - tiles, tiles, near, cap)
    for copy in copies[3:]:
        copy.wait()


def early(grad, pos, weight, count, own, tiles):
    near, cap = own.shape
    held = [jax.ShapeDtypeStruct(x.shape, x.dtype) for x in (grad, pos, weight, count, own)]
    return pl.pallas_call(
        functools.partial(early_kernel, near=near, cap=cap),
        out_shape=(*held, jax.ShapeDtypeStruct((near * cap, tiles * LANES), jnp.bfloat16)),
        in_specs=[HBM] * 5,
        out_specs=(VMEM,) * 6,
        scratch_shapes=[pltpu.SemaphoreType.DMA((5,))],
        compiler_params=pltpu.CompilerParams(vmem_limit_bytes=16 * MIB),
    )(grad, pos, weight, count, own)


def late_kernel(pos_ref, weight_ref, count_ref, w_ref, *, near, cap):
    fill_tiles(pos_ref, weight_ref, count_ref, w_ref, 0, w_ref.shape[1] // LANES, near, cap)


def late(pos, weight, count, near, cap, tiles):
    cells, slots = tiles * LANES, pos.shape[0]
    return pl.pallas_call(
        functools.partial(late_kernel, near=near, cap=cap),
        out_shape=jax.ShapeDtypeStruct((near * cap, cells), jnp.bfloat16),
        in_specs=[VMEM] * 3,
        out_specs=VMEM,
        compiler_params=pltpu.CompilerParams(vmem_limit_bytes=16 * MIB),
        cost_estimate=pl.CostEstimate(flops=near * cap * cells * slots * 2, bytes_accessed=near * cap * cells * 2, transcendentals=0),
    )(pos, weight, count)


def chosen(grad, wanted):
    hit = row_ids((grad.shape[1], wanted.shape[1])) == wanted
    onehot = jnp.where(hit, jnp.float32(1.0), jnp.float32(0.0)).astype(jnp.bfloat16)
    return jnp.dot(grad, onehot, preferred_element_type=jnp.float32).astype(jnp.bfloat16)


def outer_pick_kernel(grad_ref, asked_ref, out_ref):
    near = asked_ref.shape[0]
    wanted = jnp.where(even_place(), asked_ref[near - 1 : near, :], asked_ref[0:1, :])
    out_ref[...] = chosen(grad_ref[...], wanted)


def inner_pick_kernel(grad_ref, asked_ref, own_ref, out_ref, own_out):
    near = asked_ref.shape[0]
    wanted = jnp.where(even_place(), asked_ref[0:1, :], asked_ref[near - 1 : near, :])
    out_ref[...] = chosen(grad_ref[...], wanted)
    own_out[...] = chosen(grad_ref[...], own_ref[near // 2 : near // 2 + 1, :])


def picked(kernel, outputs, grad, *asked):
    shape = jax.ShapeDtypeStruct((grad.shape[0], asked[0].shape[1]), grad.dtype)
    return pl.pallas_call(
        kernel,
        out_shape=(shape,) * outputs,
        in_specs=[VMEM] * (1 + len(asked)),
        out_specs=(VMEM,) * outputs,
        compiler_params=pltpu.CompilerParams(vmem_limit_bytes=16 * MIB),
    )(grad, *asked)


def mixed(parts, w_ref, lanes):
    cap = parts[0].shape[1]
    acc = None
    for i, part in enumerate(parts):
        term = jnp.dot(part[...], w_ref[pl.ds(i * cap, cap), lanes], preferred_element_type=jnp.float32)
        acc = term if acc is None else acc + term
    return acc


def edge_kernel(outer_ref, own_ref, inner_ref, w_ref, sum_ref, edge_ref):
    cells, cols, half = w_ref.shape[1], own_ref.shape[0], edge_ref.shape[0]
    total = mixed((outer_ref, own_ref, inner_ref), w_ref, pl.ds(cells - LANES, LANES))
    sum_ref[pl.ds(cols // 8 * 8, 2 * half - cols // 8 * 8), :] = jnp.zeros((2 * half - cols // 8 * 8, LANES), jnp.float32)
    sum_ref[0:cols, :] = total
    upper = pltpu.roll(sum_ref[0:half, :], LANES // 2, 1)
    packed = jnp.where(lane_ids((half, LANES)) < LANES // 2, upper, sum_ref[half : 2 * half, :])
    edge_ref[...] = packed.astype(jnp.bfloat16)


def edge_sums(outer, own, inner, dense):
    cols = own.shape[0]
    half = -(-cols // (2 * PACK)) * PACK
    return pl.pallas_call(
        edge_kernel,
        out_shape=(jax.ShapeDtypeStruct((2 * half, LANES), jnp.float32), jax.ShapeDtypeStruct((half, LANES), jnp.bfloat16)),
        in_specs=[VMEM] * 4,
        out_specs=(VMEM,) * 2,
        compiler_params=pltpu.CompilerParams(vmem_limit_bytes=16 * MIB),
    )(outer, own, inner, dense)


def body_kernel(outer_ref, own_ref, inner_ref, late_ref, early_ref, out_hbm, buffer, sems, *, steps):
    for i, (start, width) in enumerate(steps):
        ahead = late_ref.shape[1]
        w_ref, inside = (late_ref, start) if start < ahead else (early_ref, start - ahead)
        buffer[:, pl.ds(start, width)] = mixed((outer_ref, own_ref, inner_ref), w_ref, pl.ds(inside, width)).astype(jnp.bfloat16)
        pltpu.make_async_copy(buffer.at[:, pl.ds(start, width)], out_hbm.at[:, pl.ds(start, width)], sems.at[i]).start()
    for i, (start, width) in enumerate(steps):
        pltpu.make_async_copy(buffer.at[:, pl.ds(start, width)], out_hbm.at[:, pl.ds(start, width)], sems.at[i]).wait()


def cuts(first, last, width):
    return [(start, min(width, last - start)) for start in range(first, last, width)]


def body_sums(outer, own, inner, late_w, early_w):
    cols, ahead = own.shape[0], late_w.shape[1]
    cells = ahead + early_w.shape[1]
    steps = cuts(0, ahead, 4 * LANES) + cuts(ahead, cells - LANES, 4 * LANES)
    return pl.pallas_call(
        functools.partial(body_kernel, steps=steps),
        out_shape=jax.ShapeDtypeStruct((cols, cells), jnp.bfloat16),
        in_specs=[VMEM] * 5,
        out_specs=HBM,
        scratch_shapes=[pltpu.VMEM((cols, cells), jnp.bfloat16), pltpu.SemaphoreType.DMA((len(steps),))],
        compiler_params=pltpu.CompilerParams(vmem_limit_bytes=24 * MIB),
        cost_estimate=pl.CostEstimate(flops=2 * cols * late_w.shape[0] * cells, bytes_accessed=cols * cells * 2, transcendentals=0),
    )(outer, own, inner, late_w, early_w)


def fold_kernel(whole_ref, sum_ref, mirror_ref, src_ref, out_ref):
    del whole_ref
    cols, half, fold = out_ref.shape[0], mirror_ref.shape[0], src_ref.shape[1]
    unused = jnp.full((1, LANES - fold), -1, jnp.int32)
    others = []
    for shift in (0, LANES // 2):
        source = jnp.concatenate([unused, src_ref[...] + shift], axis=1)
        hit = row_ids((LANES, LANES)) == source
        onehot = jnp.where(hit, jnp.float32(1.0), jnp.float32(0.0)).astype(jnp.bfloat16)
        others.append(jnp.dot(mirror_ref[...], onehot, preferred_element_type=jnp.float32))
    other = jnp.concatenate(others, axis=0)[0:cols]
    out_ref[...] = (sum_ref[0:cols, :] + other).astype(jnp.bfloat16)


def folded(whole, sums, mirror, fold_src):
    cols, cells = whole.shape
    last = cells // LANES - 1
    return pl.pallas_call(
        fold_kernel,
        grid=(1,),
        out_shape=jax.ShapeDtypeStruct((cols, cells), jnp.bfloat16),
        in_specs=[HBM, VMEM, VMEM, VMEM],
        out_specs=pl.BlockSpec((cols, LANES), lambda i: (0, last)),
        input_output_aliases={0: 0},
        compiler_params=pltpu.CompilerParams(vmem_limit_bytes=8 * MIB),
    )(whole, sums, mirror, fold_src)


def local(analysis_grad, requests, slot_pos, slot_weight, slot_count, fold_src):
    near, cap = requests.shape
    tiles = slot_pos.shape[0] // LANES
    asked_outer = outer_swap(requests)
    asked_inner = inner_swap(requests)
    placed = [in_hbm(x) for x in (analysis_grad.T, slot_pos.T, slot_weight.T, slot_count[None, :], requests)]
    grad, pos, weight, count, own_asks, early_w = early(*placed, EARLY_TILES)
    (for_outer,) = picked(outer_pick_kernel, 1, grad, asked_outer)
    outer = outer_swap(for_outer)
    for_inner, own = picked(inner_pick_kernel, 2, grad, asked_inner, own_asks)
    inner = inner_swap(for_inner)
    late_w = late(pos, weight, count, near, cap, tiles - EARLY_TILES)
    sums, edge = edge_sums(outer, own, inner, early_w)
    mirror = half_away(edge)
    whole = body_sums(outer, own, inner, late_w, early_w)
    return folded(whole, sums, mirror, fold_src[None, :]).T


def solution(mesh):
    in_specs = (
        P(("members", "lon"), None),
        P("lon", None),
        P("lon", None),
        P("lon", None),
        P("lon"),
        P("lon"),
    )
    out_specs = P(("members", "lon"), None)
    return jax.shard_map(local, mesh=mesh, in_specs=in_specs, out_specs=out_specs, check_vma=False)
```

time: 28.6 us -> 23 us (0.80)
  local copies, waits for them, and re-layouts: 4.38 us -> 0.01 us
  Pallas kernels: 11.2 us -> 10.2 us
  starting transfers between devices: 10 us -> 9.45 us
  waiting for transfers between devices: 2.62 us -> 3.11 us
    unnamed x12 -> x2, local copies, waits for them, and re-layouts: 4.38 us -> 0.01 us
    pallas_call x4 -> x6, Pallas kernels: 10.3 us -> 9.31 us  [the longest x1 3.32 us: late(): pl.pallas_call(functools.partial(late_kernel, near=near, cap=cap), out_sh...]
    ppermute x5, starting transfers between devices: 10 us -> 9.45 us  [the longest x2 9.3 us: outer_swap(): lax.ppermute(block, 'lon', [(i, (i - 1) % count if i % 2 == 0 else (i + 1...]
    ppermute x5, waiting for transfers between devices: 2.62 us -> 3.11 us  [the longest x1 2.69 us: half_away(): lax.ppermute(block, 'lon', [(i, (i + count // 2) % count) for i in range(...]
  transfers between devices with their start and end apart: 5 -> 5, of which waited for: 2 -> 2; matrix products, arithmetic and copies ran while one was open for 0% -> 0% of each run, Pallas kernels for 32% -> 39%
where the time goes in v2:
time: 23 us; the launch traced here: 22.9 us
  Pallas kernels  10.2 us (44%)
  starting transfers between devices  9.45 us (41%)
  waiting for transfers between devices  3.11 us (14%)
    ppermute x2, starting transfers between devices, outer_swap(): lax.ppermute(block, 'lon', [(i, (i - 1) % count if i % 2 == 0 else (i + 1...  9.3 us
    pallas_call x1, Pallas kernels, late(): pl.pallas_call(functools.partial(late_kernel, near=near, cap=cap), out_sh...  3.32 us
    ppermute x1, waiting for transfers between devices, half_away(): lax.ppermute(block, 'lon', [(i, (i + count // 2) % count) for i in range(...  2.69 us
    pallas_call x1, Pallas kernels, body_sums(): pl.pallas_call(functools.partial(body_kernel, steps=steps), out_shape=jax...  2.41 us
    pallas_call x1, Pallas kernels, early(): pl.pallas_call(functools.partial(early_kernel, near=near, cap=cap), out_s...  2.12 us
    pallas_call x2, Pallas kernels, picked(): pl.pallas_call(kernel, out_shape=(shape,) * outputs, in_specs=[VMEM] * (1...  1.09 us
    pallas_call x1, Pallas kernels, folded(): pl.pallas_call(fold_kernel, grid=(1,), out_shape=jax.ShapeDtypeStruct((co...  0.93 us
  transfers between devices with their start and end apart: 5, of which 2 were waited for; matrix products, arithmetic and copies ran while one was open for 0% of the time, Pallas kernels for 39%

profile of v2, /device:TPU:0, one launch (start us, length us, event | category | flops | bytes accessed | tf_op | source)
XLA Modules:
  0.0 22.9 jit_solution(17231663270975941061)
XLA Ops:
  0.0 5.4 %collective-permute-start = (s32[3,256]{1,0:T(4,128)}, s32[3,256]{1,0:T(4,128)S(1)}, u32[]{:S(2)}, u32[]{:S(2)}) collective-permute-start(s32[3,256]{1,0:T(4,128)} %own_hbm.1), channel_id=1, source_target_pairs={{0,15},{1,2},{2,1},{3,4},{4,3},{5,6},{6,5},{7,8},{8,7},{9,10},{10,... | collective-permute-start | bytes 9224 | tf_op jit(solution)/shard_map/ppermute | solution.py:37
  5.4 0.0 collective-permute-start.2
  5.4 2.1 %shard_map.64 = (bf16[450,1024]{1,0:T(8,128)(2,1)S(1)}, s32[16,2048]{1,0:T(8,128)S(1)}, f32[16,2048]{1,0:T(8,128)S(1)}, s32[1,2048]{1,0:T(1,128)S(1)}, s32[3,256...) custom-call(bf16[450,1024]{1,0:T(8,128)(2,1)} %bitcast.7, s32[16,2048]{1,0:T(8,128)} %bitcast.8, f32[16,2048]{1,0:T(8,128)} %bitcast.9, ...), custom_call_target="tpu_custom_call" | custom-call | tf_op jit(solution)/shard_map/pallas_call | solution.py:98
  7.6 0.0 collective-permute-done.asked_ref
  7.6 0.4 %shard_map.65 = bf16[450,256]{1,0:T(8,128)(2,1)S(1)} custom-call(bf16[450,1024]{1,0:T(8,128)(2,1)S(1)} %get-tuple-element.15.grad_ref, s32[3,256]{1,0:T(4,128)S(1)} %collective-permute-done.asked_ref), custom_call_target="tpu_custom_call" | custom-call | tf_op jit(solution)/shard_map/pallas_call | solution.py:145
  8.0 3.9 %collective-permute-start.1 = (bf16[450,256]{1,0:T(8,128)(2,1)S(1)}, bf16[450,256]{1,0:T(8,128)(2,1)S(1)}, u32[]{:S(2)}, u32[]{:S(2)}) collective-permute-start(bf16[450,256]{1,0:T(8,128)(2,1)S(1)} %shard_map.65), channel_id=1, source_target_pairs={{0,15},{1,2},{2,1},{3,4},{4,3},{5,6},{6,5},{7,8},{8,7},{9,10},{10,... | collective-permute-start | bytes 691208 | tf_op jit(solution)/shard_map/ppermute | solution.py:37
  11.9 0.0 collective-permute-done.2.asked_ref
  11.9 0.7 %shard_map.66 = (bf16[450,256]{1,0:T(8,128)(2,1)S(1)}, bf16[450,256]{1,0:T(8,128)(2,1)S(1)}) custom-call(bf16[450,1024]{1,0:T(8,128)(2,1)S(1)} %get-tuple-element.15.grad_ref, s32[3,256]{1,0:T(4,128)S(1)} %collective-permute-done.2.asked_ref, s32[3,256]{1,0:T(4,128)S(1)} %get-tuple-element.16.own_ref), custom_call_target="tpu_custom_call" | custom-call | tf_op jit(solution)/shard_map/pallas_call | solution.py:145
  12.6 0.1 collective-permute-start.3
  12.6 3.3 %shard_map.67.late_ref = bf16[768,1536]{1,0:T(8,128)(2,1)S(1)} custom-call(s32[16,2048]{1,0:T(8,128)S(1)} %get-tuple-element.19.pos_ref, f32[16,2048]{1,0:T(8,128)S(1)} %get-tuple-element.20.weight_ref, s32[1,2048]{1,0:T(1,128)S(1)} %get-tuple-element.21.count_ref), custom_call_target="tpu_custom_call" | custom-call | flops 37748736 | bytes 2359296 | tf_op jit(solution)/shard_map/pallas_call | solution.py:114
  16.0 0.4 %collective-permute-done.1.outer_ref = bf16[450,256]{1,0:T(8,128)(2,1)S(1)} collective-permute-done((bf16[450,256]{1,0:T(8,128)(2,1)S(1)}, bf16[450,256]{1,0:T(8,128)(2,1)S(1)}, u32[]{:S(2)}, u32[]{:S(2)}) %collective-permute-start.1) | collective-permute-done | bytes 230432 | tf_op jit(solution)/shard_map/ppermute | solution.py:37
  16.4 0.0 collective-permute-done.3.inner_ref
  16.4 0.4 %shard_map.69 = (f32[480,128]{1,0:T(8,128)S(1)}, bf16[240,128]{1,0:T(8,128)(2,1)S(1)}) custom-call(bf16[450,256]{1,0:T(8,128)(2,1)S(1)} %collective-permute-done.1.outer_ref, bf16[450,256]{1,0:T(8,128)(2,1)S(1)} %get-tuple-element.17.own_ref, bf16[450,256]{1,0:T(8,128)(2,1)S(1)} %collective-permute-done.3.inner_ref, ...), custom_call_target="tpu_custom_call" | custom-call | tf_op jit(solution)/shard_map/pallas_call | solution.py:176
  16.8 0.0 copy-start
  16.8 0.1 collective-permute-start.4
  16.8 2.4 %shard_map.68.whole_ref = bf16[450,2048]{1,0:T(8,128)(2,1)} custom-call(bf16[450,256]{1,0:T(8,128)(2,1)S(1)} %collective-permute-done.1.outer_ref, bf16[450,256]{1,0:T(8,128)(2,1)S(1)} %get-tuple-element.17.own_ref, bf16[450,256]{1,0:T(8,128)(2,1)S(1)} %collective-permute-done.3.inner_ref, bf16[768,1536]{1,0:T(8,128)(2,1)S(1)} %shard_map.67.late_ref, ...), custom_call_target="tpu_custom_call" | custom-call | flops 1415577600 | bytes 1843200 | tf_op jit(solution)/shard_map/pallas_call | solution.py:203
  19.3 2.7 %collective-permute-done.4.mirror_ref = bf16[240,128]{1,0:T(8,128)(2,1)S(1)} collective-permute-done((bf16[240,128]{1,0:T(8,128)(2,1)S(1)}, bf16[240,128]{1,0:T(8,128)(2,1)S(1)}, u32[]{:S(2)}, u32[]{:S(2)}) %collective-permute-start.4) | collective-permute-done | bytes 61472 | tf_op jit(solution)/shard_map/ppermute | solution.py:42
  21.9 0.0 copy-done
  22.0 0.9 %shard_map.70 = bf16[450,2048]{1,0:T(8,128)(2,1)} custom-call(bf16[450,2048]{1,0:T(8,128)(2,1)} %shard_map.68.whole_ref, f32[480,128]{1,0:T(8,128)S(1)} %get-tuple-element.23.sum_ref, bf16[240,128]{1,0:T(8,128)(2,1)S(1)} %collective-permute-done.4.mirror_ref, s32[1,64]{1,0:T(1,128)S(1)} %bitcast.6), custom_call_target="tpu_custom_call", output_to_operand_aliasing={{}: (0, {})} | custom-call | tf_op jit(solution)/shard_map/pallas_call | solution.py:231
Async XLA Ops:
  0.0 7.6 %collective-permute-start = (s32[3,256]{1,0:T(4,128)}, s32[3,256]{1,0:T(4,128)S(1)}, u32[]{:S(2)}, u32[]{:S(2)}) collective-permute-start(s32[3,256]{1,0:T(4,128)} %own_hbm.1), channel_id=1, source_target_pairs={{0,15},{1,2},{2,1},{3,4},{4,3},{5,6},{6,5},{7,8},{8,7},{9,10},{10,... | collective-permute-start | bytes 9224 | tf_op jit(solution)/shard_map/ppermute | solution.py:37
  5.4 6.4 %collective-permute-start.2 = (s32[3,256]{1,0:T(4,128)}, s32[3,256]{1,0:T(4,128)S(1)}, u32[]{:S(2)}, u32[]{:S(2)}) collective-permute-start(s32[3,256]{1,0:T(4,128)} %own_hbm.1), channel_id=1, source_target_pairs={{0,1},{1,0},{2,3},{3,2},{4,5},{5,4},{6,7},{7,6},{8,9},{9,8},{10,11... | collective-permute-start | bytes 9224 | tf_op jit(solution)/shard_map/ppermute | solution.py:32
  8.0 8.4 %collective-permute-start.1 = (bf16[450,256]{1,0:T(8,128)(2,1)S(1)}, bf16[450,256]{1,0:T(8,128)(2,1)S(1)}, u32[]{:S(2)}, u32[]{:S(2)}) collective-permute-start(bf16[450,256]{1,0:T(8,128)(2,1)S(1)} %shard_map.65), channel_id=1, source_target_pairs={{0,15},{1,2},{2,1},{3,4},{4,3},{5,6},{6,5},{7,8},{8,7},{9,10},{10,... | collective-permute-start | bytes 691208 | tf_op jit(solution)/shard_map/ppermute | solution.py:37
  12.6 3.8 %collective-permute-start.3 = (bf16[450,256]{1,0:T(8,128)(2,1)S(1)}, bf16[450,256]{1,0:T(8,128)(2,1)S(1)}, u32[]{:S(2)}, u32[]{:S(2)}) collective-permute-start(bf16[450,256]{1,0:T(8,128)(2,1)S(1)} %get-tuple-element.18), channel_id=1, source_target_pairs={{0,1},{1,0},{2,3},{3,2},{4,5},{5,4},{6,7},{7,6},{8,9},{9,8},{10,11... | collective-permute-start | bytes 691208 | tf_op jit(solution)/shard_map/ppermute | solution.py:32
  16.8 5.2 %copy-start = (s32[64]{0:T(128)S(1)}, s32[64]{0:T(128)}, u32[]{:S(2)}) copy-start(s32[64]{0:T(128)} %param.11) | copy-start | bytes 772
  16.8 5.2 %collective-permute-start.4 = (bf16[240,128]{1,0:T(8,128)(2,1)S(1)}, bf16[240,128]{1,0:T(8,128)(2,1)S(1)}, u32[]{:S(2)}, u32[]{:S(2)}) collective-permute-start(bf16[240,128]{1,0:T(8,128)(2,1)S(1)} %get-tuple-element.24), channel_id=1, source_target_pairs={{0,8},{1,9},{2,10},{3,11},{4,12},{5,13},{6,14},{7,15},{8,0},{9,1},... | collective-permute-start | bytes 184328 | tf_op jit(solution)/shard_map/ppermute | solution.py:42

commit v3 on v2

v3 whole, which is shorter than its diff:
```python
import functools
import math

import jax
import jax.numpy as jnp
from jax import lax
from jax.experimental import pallas as pl
from jax.experimental.pallas import tpu as pltpu
from jax.sharding import PartitionSpec as P

LANES = 128
PACK = 16
MIB = 2**20
VMEM = pl.BlockSpec(memory_space=pltpu.VMEM)
HBM = pl.BlockSpec(memory_space=pltpu.HBM)


def even_place():
    return lax.rem(lax.axis_index("lon"), 2) == 0


def row_ids(shape):
    return lax.broadcasted_iota(jnp.int32, shape, 0)


def lane_ids(shape):
    return lax.broadcasted_iota(jnp.int32, shape, 1)


def outer_place(place, count):
    return (place - 1) % count if place % 2 == 0 else (place + 1) % count


def inner_swap(block):
    count = lax.axis_size("lon")
    return lax.ppermute(block, "lon", [(i, i ^ 1) for i in range(count)])


def outer_swap(block):
    count = lax.axis_size("lon")
    return lax.ppermute(block, "lon", [(i, outer_place(i, count)) for i in range(count)])


def half_away(block):
    count = lax.axis_size("lon")
    return lax.ppermute(block, "lon", [(i, (i + count // 2) % count) for i in range(count)])


def half_away_of_outer(block):
    count = lax.axis_size("lon")
    return lax.ppermute(block, "lon", [(i, (outer_place(i, count) + count // 2) % count) for i in range(count)])


def in_hbm(block):
    return pltpu.with_memory_space_constraint(block, pltpu.HBM)


def merged_weights(pos, weight, count):
    valid = row_ids(pos.shape) < count
    masked = jnp.where(valid, weight, jnp.float32(0.0))
    scale = masked / jnp.sum(masked, axis=0, keepdims=True)
    scale = scale.astype(jnp.bfloat16).astype(jnp.float32)
    merged = jnp.zeros(pos.shape, jnp.float32)
    for k in range(pos.shape[0]):
        merged += jnp.where(pos == pos[k : k + 1], scale[k : k + 1], jnp.float32(0.0))
    return merged


def spread_rows(rows, dtype):
    return [jnp.broadcast_to(rows[k : k + 1], (PACK, LANES)).astype(dtype) for k in range(rows.shape[0])]


def fill_piece(w_ref, first, lanes, count, place, spread):
    for group in range(count // PACK):
        acc = jnp.zeros((PACK, LANES), jnp.bfloat16)
        for k in range(len(place)):
            acc = jnp.where(place[k] == jnp.int16(group * PACK), spread[k], acc)
        w_ref[pl.ds(first + group * PACK, PACK), lanes] = acc


def fill_tiles(pos_ref, weight_ref, count_ref, w_ref, first, tiles, near, cap):
    even = even_place()
    row = row_ids((PACK, LANES)).astype(jnp.int16)

    def one_tile(tile, carry):
        taken = pl.ds(pl.multiple_of((first + tile) * LANES, LANES), LANES)
        given = pl.ds(pl.multiple_of(tile * LANES, LANES), LANES)
        pos = pos_ref[:, taken]
        spread = spread_rows(merged_weights(pos, weight_ref[:, taken], count_ref[:, taken]), jnp.bfloat16)
        turned = jnp.where(even, pos, pos + cap * (near - 1) - 2 * cap * lax.div(pos, cap))
        place = [x - row for x in spread_rows(turned, jnp.int16)]
        fill_piece(w_ref, 0, given, near * cap, place, spread)
        return carry

    lax.fori_loop(0, tiles, one_tile, 0, unroll=math.gcd(tiles, 3))


def ask_kernel(pos_hbm, weight_hbm, count_hbm, wanted_hbm, ask_ref, near_ref, pos_ref, weight_ref, count_ref, wanted_ref, sems):
    slots, cells = pos_hbm.shape
    near, cap = wanted_hbm.shape
    last = pl.ds(cells - LANES, LANES)
    pairs = ((pos_hbm.at[:, last], pos_ref), (weight_hbm.at[:, last], weight_ref), (count_hbm.at[:, last], count_ref), (wanted_hbm, wanted_ref))
    copies = [pltpu.make_async_copy(source, target, sems.at[i]) for i, (source, target) in enumerate(pairs)]
    for copy in copies:
        copy.start()
    for copy in copies:
        copy.wait()
    pos, even = pos_ref[...], even_place()
    local = pos - jnp.where(even, 0, (near - 1) * cap)
    local = jnp.where((local >= 0) & (local < cap), local, -1)
    wanted = jnp.where(even, wanted_ref[0:1, :], wanted_ref[near - 1 : near, :])
    for i in range(near):
        near_ref[i] = jnp.broadcast_to(wanted_ref[i : i + 1, :], (PACK, cap))
    ask_ref[0:slots, 0:LANES] = local.astype(jnp.float32)
    ask_ref[0:slots, LANES : 2 * LANES] = merged_weights(pos, weight_ref[...], count_ref[...])
    ask_ref[slots:, :] = jnp.broadcast_to(wanted, (ask_ref.shape[0] - slots, cap)).astype(jnp.float32)


def ask(pos, weight, count, wanted):
    slots, cap = pos.shape[0], wanted.shape[1]
    tile = (slots, LANES)
    return pl.pallas_call(
        ask_kernel,
        out_shape=(jax.ShapeDtypeStruct((slots + 8, cap), jnp.float32), jax.ShapeDtypeStruct((wanted.shape[0], PACK, cap), jnp.int32)),
        in_specs=[HBM] * 4,
        out_specs=(VMEM,) * 2,
        scratch_shapes=[
            pltpu.VMEM(tile, jnp.int32),
            pltpu.VMEM(tile, jnp.float32),
            pltpu.VMEM((1, LANES), jnp.int32),
            pltpu.VMEM(wanted.shape, jnp.int32),
            pltpu.SemaphoreType.DMA((4,)),
        ],
        compiler_params=pltpu.CompilerParams(vmem_limit_bytes=16 * MIB),
    )(*[in_hbm(x) for x in (pos, weight, count, wanted)])


def load_kernel(*refs):
    count = (len(refs) - 1) // 2
    copies = [pltpu.make_async_copy(refs[i], refs[count + i], refs[-1].at[i]) for i in range(count)]
    for copy in copies:
        copy.start()
    for copy in copies:
        copy.wait()


def loaded(*arrays):
    return pl.pallas_call(
        load_kernel,
        out_shape=tuple(jax.ShapeDtypeStruct(x.shape, x.dtype) for x in arrays),
        in_specs=[HBM] * len(arrays),
        out_specs=(VMEM,) * len(arrays),
        scratch_shapes=[pltpu.SemaphoreType.DMA((len(arrays),))],
        compiler_params=pltpu.CompilerParams(vmem_limit_bytes=16 * MIB),
    )(*[in_hbm(x) for x in arrays])


def late_kernel(pos_ref, weight_ref, count_ref, w_ref, *, near, cap):
    fill_tiles(pos_ref, weight_ref, count_ref, w_ref, 0, w_ref.shape[1] // LANES, near, cap)


def late(pos, weight, count, near, cap):
    slots, cells = pos.shape[0], pos.shape[1] - LANES
    return pl.pallas_call(
        functools.partial(late_kernel, near=near, cap=cap),
        out_shape=jax.ShapeDtypeStruct((near * cap, cells), jnp.bfloat16),
        in_specs=[VMEM] * 3,
        out_specs=VMEM,
        compiler_params=pltpu.CompilerParams(vmem_limit_bytes=16 * MIB),
        cost_estimate=pl.CostEstimate(flops=near * cap * cells * slots * 2, bytes_accessed=near * cap * cells * 2, transcendentals=0),
    )(pos, weight, count)


def chosen(grad, wanted):
    hit = row_ids((grad.shape[1], wanted.shape[1])) == wanted
    onehot = jnp.where(hit, jnp.float32(1.0), jnp.float32(0.0)).astype(jnp.bfloat16)
    return jnp.dot(grad, onehot, preferred_element_type=jnp.float32).astype(jnp.bfloat16)


def outer_pick_kernel(grad_ref, asked_ref, out_ref):
    rows = asked_ref.shape[0]
    out_ref[...] = chosen(grad_ref[...], asked_ref[rows - 1 : rows, :].astype(jnp.int32))


def inner_pick_kernel(grad_ref, asked_ref, own_ref, out_ref, own_out):
    near = asked_ref.shape[0]
    wanted = jnp.where(even_place(), asked_ref[0, 0:1, :], asked_ref[near - 1, 0:1, :])
    out_ref[...] = chosen(grad_ref[...], wanted)
    own_out[...] = chosen(grad_ref[...], own_ref[near // 2, 0:1, :])


def picked(kernel, outputs, grad, *asked):
    shape = jax.ShapeDtypeStruct((grad.shape[0], asked[0].shape[-1]), grad.dtype)
    return pl.pallas_call(
        kernel,
        out_shape=(shape,) * outputs,
        in_specs=[VMEM] * (1 + len(asked)),
        out_specs=(VMEM,) * outputs,
        compiler_params=pltpu.CompilerParams(vmem_limit_bytes=16 * MIB),
    )(grad, *asked)


def half_rows(cols):
    return -(-cols // (2 * PACK)) * PACK


def pack_fold(total, edge_ref, sum_ref):
    cols, half = total.shape[0], edge_ref.shape[0]
    tail = cols // 8 * 8
    sum_ref[pl.ds(tail, 2 * half - tail), :] = jnp.zeros((2 * half - tail, LANES), jnp.float32)
    sum_ref[0:cols, :] = total
    upper = pltpu.roll(sum_ref[0:half, :], LANES // 2, 1)
    packed = jnp.where(lane_ids((half, LANES)) < LANES // 2, upper, sum_ref[half : 2 * half, :])
    edge_ref[...] = packed.astype(jnp.bfloat16)


def near_fold_kernel(pos_ref, weight_ref, count_ref, own_ref, inner_ref, w_ref, edge_ref, sum_ref, *, near, cap):
    fill_tiles(pos_ref, weight_ref, count_ref, w_ref, pos_ref.shape[1] // LANES - 1, 1, near, cap)
    total = jnp.dot(own_ref[...], w_ref[cap : 2 * cap, :], preferred_element_type=jnp.float32)
    total += jnp.dot(inner_ref[...], w_ref[2 * cap : 3 * cap, :], preferred_element_type=jnp.float32)
    pack_fold(total, edge_ref, sum_ref)


def near_fold(pos, weight, count, own, inner, near):
    cols, cap = own.shape
    half = half_rows(cols)
    return pl.pallas_call(
        functools.partial(near_fold_kernel, near=near, cap=cap),
        out_shape=(jax.ShapeDtypeStruct((near * cap, LANES), jnp.bfloat16), jax.ShapeDtypeStruct((half, LANES), jnp.bfloat16)),
        in_specs=[VMEM] * 5,
        out_specs=(VMEM,) * 2,
        scratch_shapes=[pltpu.VMEM((2 * half, LANES), jnp.float32)],
        compiler_params=pltpu.CompilerParams(vmem_limit_bytes=16 * MIB),
    )(pos, weight, count, own, inner)


def far_fold_kernel(asked_ref, rows_ref, edge_ref, w_ref, sum_ref):
    slots, cap = asked_ref.shape[0] - 8, rows_ref.shape[1]
    row = row_ids((PACK, LANES)).astype(jnp.int16)
    place = [x - row for x in spread_rows(asked_ref[0:slots, 0:LANES].astype(jnp.int32), jnp.int16)]
    fill_piece(w_ref, 0, pl.ds(0, LANES), cap, place, spread_rows(asked_ref[0:slots, LANES : 2 * LANES], jnp.bfloat16))
    pack_fold(jnp.dot(rows_ref[...], w_ref[...], preferred_element_type=jnp.float32), edge_ref, sum_ref)


def far_fold(asked, rows):
    cols, cap = rows.shape
    half = half_rows(cols)
    return pl.pallas_call(
        far_fold_kernel,
        out_shape=jax.ShapeDtypeStruct((half, LANES), jnp.bfloat16),
        in_specs=[VMEM] * 2,
        out_specs=VMEM,
        scratch_shapes=[pltpu.VMEM((cap, LANES), jnp.bfloat16), pltpu.VMEM((2 * half, LANES), jnp.float32)],
        compiler_params=pltpu.CompilerParams(vmem_limit_bytes=16 * MIB),
    )(asked, rows)


def mixed(parts, w_ref, lanes):
    cap = parts[0].shape[1]
    acc = None
    for i, part in enumerate(parts):
        term = jnp.dot(part[...], w_ref[pl.ds(i * cap, cap), lanes], preferred_element_type=jnp.float32)
        acc = term if acc is None else acc + term
    return acc


def unpack_fold(mirrors, src_ref, cols):
    fold = src_ref.shape[1]
    unused = jnp.full((1, LANES - fold), -1, jnp.int32)
    halves = []
    for shift in (0, LANES // 2):
        source = jnp.concatenate([unused, src_ref[...] + shift], axis=1)
        hit = row_ids((LANES, LANES)) == source
        onehot = jnp.where(hit, jnp.float32(1.0), jnp.float32(0.0)).astype(jnp.bfloat16)
        halves.append(sum(jnp.dot(m[...], onehot, preferred_element_type=jnp.float32) for m in mirrors))
    return jnp.concatenate(halves, axis=0)[0:cols]


def body_kernel(outer_ref, own_ref, inner_ref, late_ref, last_ref, near_ref, far_ref, src_ref, out_hbm, buffer, sems, *, steps):
    parts = (outer_ref, own_ref, inner_ref)
    copies = []
    for i, (start, width) in enumerate(steps):
        lanes = pl.ds(start, width)
        if start < late_ref.shape[1]:
            total = mixed(parts, late_ref, lanes)
        else:
            total = mixed(parts, last_ref, pl.ds(0, width)) + unpack_fold((near_ref, far_ref), src_ref, own_ref.shape[0])
        buffer[:, lanes] = total.astype(jnp.bfloat16)
        copies.append(pltpu.make_async_copy(buffer.at[:, lanes], out_hbm.at[:, lanes], sems.at[i]))
        copies[-1].start()
    for copy in copies:
        copy.wait()


def body_sums(outer, own, inner, late_w, last_w, near_mirror, far_mirror, fold_src):
    cols, ahead = own.shape[0], late_w.shape[1]
    cells = ahead + LANES
    steps = [(start, min(4 * LANES, ahead - start)) for start in range(0, ahead, 4 * LANES)] + [(ahead, LANES)]
    return pl.pallas_call(
        functools.partial(body_kernel, steps=steps),
        out_shape=jax.ShapeDtypeStruct((cols, cells), jnp.bfloat16),
        in_specs=[VMEM] * 8,
        out_specs=HBM,
        scratch_shapes=[pltpu.VMEM((cols, cells), jnp.bfloat16), pltpu.SemaphoreType.DMA((len(steps),))],
        compiler_params=pltpu.CompilerParams(vmem_limit_bytes=24 * MIB),
        cost_estimate=pl.CostEstimate(flops=2 * cols * late_w.shape[0] * cells, bytes_accessed=cols * cells * 2, transcendentals=0),
    )(outer, own, inner, late_w, last_w, near_mirror, far_mirror, fold_src)


def local(analysis_grad, requests, slot_pos, slot_weight, slot_count, fold_src):
    near, cap = requests.shape
    places, raw, counts = slot_pos.T, slot_weight.T, slot_count[None, :]
    for_asking, own_asks = ask(places, raw, counts, requests)
    asked_inner = inner_swap(own_asks)
    asked_outer = outer_swap(for_asking)
    grad, pos, weight, count = loaded(analysis_grad.T, places, raw, counts)
    for_inner, own = picked(inner_pick_kernel, 2, grad, asked_inner, own_asks)
    asked_outer, for_inner = lax.optimization_barrier((asked_outer, for_inner))
    inner = inner_swap(for_inner)
    (for_outer,) = picked(outer_pick_kernel, 1, grad, asked_outer)
    outer = outer_swap(for_outer)
    last_w, near_edge = near_fold(pos, weight, count, own, inner, near)
    near_mirror = half_away(near_edge)
    far_mirror = half_away_of_outer(far_fold(asked_outer, for_outer))
    late_w = late(pos, weight, count, near, cap)
    return body_sums(outer, own, inner, late_w, last_w, near_mirror, far_mirror, fold_src[None, :]).T


def solution(mesh):
    in_specs = (
        P(("members", "lon"), None),
        P("lon", None),
        P("lon", None),
        P("lon", None),
        P("lon"),
        P("lon"),
    )
    out_specs = P(("members", "lon"), None)
    return jax.shard_map(local, mesh=mesh, in_specs=in_specs, out_specs=out_specs, check_vma=False)
```

time: 23 us -> 24.1 us (1.048)
  starting transfers between devices: 9.45 us -> 11.4 us
  waiting for transfers between devices: 3.11 us -> 1.53 us
  Pallas kernels: 10.2 us -> 10.9 us
    ppermute x1, waiting for transfers between devices: 2.69 us -> 0.01 us  [half_away(): lax.ppermute(block, 'lon', [(i, (i + count // 2) % count) for i in range(...]
    ppermute x2 -> x3, waiting for transfers between devices: 0.42 us -> 1.52 us  [the longest x1 1.52 us: half_away_of_outer(): lax.ppermute(block, 'lon', [(i, (outer_place(i, count) + count // 2) % co...]
    ppermute x1, starting transfers between devices: 0.07 us -> 1.15 us  [half_away(): lax.ppermute(block, 'lon', [(i, (i + count // 2) % count) for i in range(...]
    pallas_call x1, Pallas kernels: 3.32 us -> 3.85 us  [late(): pl.pallas_call(functools.partial(late_kernel, near=near, cap=cap), out_sh...]
    ppermute x2, starting transfers between devices: 0.07 us -> 0.59 us  [inner_swap(): return lax.ppermute(block, 'lon', [(i, i ^ 1) for i in range(count)])]
    pallas_call x1, Pallas kernels: 2.41 us -> 2.92 us  [body_sums(): pl.pallas_call(functools.partial(body_kernel, steps=steps), out_shape=jax...]
    ppermute x2 -> x3, starting transfers between devices: 9.3 us -> 9.71 us  [the longest x2 9.64 us: outer_swap(): lax.ppermute(block, 'lon', [(i, outer_place(i, count)) for i in range(cou...]
    pallas_call x3 -> x4, Pallas kernels: 3.41 us -> 3.03 us  [the longest x1 1.26 us: loaded(): pl.pallas_call(load_kernel, out_shape=tuple((jax.ShapeDtypeStruct(x.shape...]
  transfers between devices with their start and end apart: 5 -> 6, of which waited for: 2 -> 1; matrix products, arithmetic and copies ran while one was open for 0% -> 0% of each run, Pallas kernels for 39% -> 30%
where the time goes in v3:
time: 24.1 us; the launch traced here: 24 us
  starting transfers between devices  11.4 us (47%)
  Pallas kernels  10.9 us (45%)
  waiting for transfers between devices  1.53 us (6%)
    ppermute x2, starting transfers between devices, outer_swap(): lax.ppermute(block, 'lon', [(i, outer_place(i, count)) for i in range(cou...  9.64 us
    pallas_call x1, Pallas kernels, late(): pl.pallas_call(functools.partial(late_kernel, near=near, cap=cap), out_sh...  3.85 us
    pallas_call x1, Pallas kernels, body_sums(): pl.pallas_call(functools.partial(body_kernel, steps=steps), out_shape=jax...  2.92 us
    ppermute x1, waiting for transfers between devices, half_away_of_outer(): lax.ppermute(block, 'lon', [(i, (outer_place(i, count) + count // 2) % co...  1.52 us
    pallas_call x1, Pallas kernels, loaded(): pl.pallas_call(load_kernel, out_shape=tuple((jax.ShapeDtypeStruct(x.shape...  1.26 us
    ppermute x1, starting transfers between devices, half_away(): lax.ppermute(block, 'lon', [(i, (i + count // 2) % count) for i in range(...  1.15 us
    pallas_call x2, Pallas kernels, picked(): pl.pallas_call(kernel, out_shape=(shape,) * outputs, in_specs=[VMEM] * (1...  1.08 us
    pallas_call x1, Pallas kernels, ask(): pl.pallas_call(ask_kernel, out_shape=(jax.ShapeDtypeStruct((slots + 8, ca...  0.81 us
  transfers between devices with their start and end apart: 6, of which 1 were waited for; matrix products, arithmetic and copies ran while one was open for 0% of the time, Pallas kernels for 30%

profile of v3, /device:TPU:0, one launch (start us, length us, event | category | flops | bytes accessed | tf_op | source)
XLA Modules:
  0.0 24.0 jit_solution(5217779192069274123)
XLA Ops:
  0.0 0.8 %shard_map.65 = (f32[24,256]{1,0:T(8,128)S(1)}, s32[3,16,256]{2,1,0:T(8,128)S(1)}) custom-call(s32[16,2048]{1,0:T(8,128)} %bitcast.8, f32[16,2048]{1,0:T(8,128)} %bitcast.10, s32[1,2048]{1,0:T(1,128)} %bitcast.12, s32[3,256]{1,0:T(4,128)} %wanted_hbm.1), custom_call_target="tpu_custom_call" | custom-call | tf_op jit(solution)/shard_map/pallas_call | solution.py:122
  0.8 0.5 %collective-permute-start.1 = (s32[3,16,256]{2,1,0:T(8,128)S(1)}, s32[3,16,256]{2,1,0:T(8,128)S(1)}, u32[]{:S(2)}, u32[]{:S(2)}) collective-permute-start(s32[3,16,256]{2,1,0:T(8,128)S(1)} %get-tuple-element.19.own_ref), channel_id=1, source_target_pairs={{0,1},{1,0},{2,3},{3,2},{4,5},{5,4},{6,7},{7,6},{8,9},{9,8},{10,11... | collective-permute-start | bytes 147464 | tf_op jit(solution)/shard_map/ppermute | solution.py:36
  1.3 5.7 %collective-permute-start = (f32[24,256]{1,0:T(8,128)S(1)}, f32[24,256]{1,0:T(8,128)S(1)}, u32[]{:S(2)}, u32[]{:S(2)}) collective-permute-start(f32[24,256]{1,0:T(8,128)S(1)} %get-tuple-element.18), channel_id=1, source_target_pairs={{0,15},{1,2},{2,1},{3,4},{4,3},{5,6},{6,5},{7,8},{8,7},{9,10},{10,... | collective-permute-start | bytes 73736 | tf_op jit(solution)/shard_map/ppermute | solution.py:41
  7.0 1.3 %shard_map.64 = (bf16[450,1024]{1,0:T(8,128)(2,1)S(1)}, s32[16,2048]{1,0:T(8,128)S(1)}, f32[16,2048]{1,0:T(8,128)S(1)}, s32[1,2048]{1,0:T(1,128)S(1)}) custom-call(bf16[450,1024]{1,0:T(8,128)(2,1)} %bitcast.7, s32[16,2048]{1,0:T(8,128)} %bitcast.9, f32[16,2048]{1,0:T(8,128)} %bitcast.11, s32[1,2048]{1,0:T(1,128)} %bitcast.13), custom_call_target="tpu_custom_call" | custom-call | tf_op jit(solution)/shard_map/pallas_call | solution.py:148
  8.3 0.0 collective-permute-done.1.asked_ref
  8.3 0.7 %shard_map.66 = (bf16[450,256]{1,0:T(8,128)(2,1)S(1)}, bf16[450,256]{1,0:T(8,128)(2,1)S(1)}) custom-call(bf16[450,1024]{1,0:T(8,128)(2,1)S(1)} %get-tuple-element.17.grad_ref, s32[3,16,256]{2,1,0:T(8,128)S(1)} %collective-permute-done.1.asked_ref, s32[3,16,256]{2,1,0:T(8,128)S(1)} %get-tuple-element.19.own_ref), custom_call_target="tpu_custom_call" | custom-call | tf_op jit(solution)/shard_map/pallas_call | solution.py:194
  8.9 0.0 copy-start
  9.0 0.0 collective-permute-done.asked_ref
  9.0 0.1 collective-permute-start.3
  9.1 0.4 %shard_map.67.rows_ref = bf16[450,256]{1,0:T(8,128)(2,1)S(1)} custom-call(bf16[450,1024]{1,0:T(8,128)(2,1)S(1)} %get-tuple-element.17.grad_ref, f32[24,256]{1,0:T(8,128)S(1)} %collective-permute-done.asked_ref), custom_call_target="tpu_custom_call" | custom-call | tf_op jit(solution)/shard_map/pallas_call | solution.py:194
  9.5 4.0 %collective-permute-start.2 = (bf16[450,256]{1,0:T(8,128)(2,1)S(1)}, bf16[450,256]{1,0:T(8,128)(2,1)S(1)}, u32[]{:S(2)}, u32[]{:S(2)}) collective-permute-start(bf16[450,256]{1,0:T(8,128)(2,1)S(1)} %shard_map.67.rows_ref), channel_id=1, source_target_pairs={{0,15},{1,2},{2,1},{3,4},{4,3},{5,6},{6,5},{7,8},{8,7},{9,10},{10,... | collective-permute-start | bytes 691208 | tf_op jit(solution)/shard_map/ppermute | solution.py:41
  13.4 0.4 %shard_map.70 = bf16[240,128]{1,0:T(8,128)(2,1)S(1)} custom-call(f32[24,256]{1,0:T(8,128)S(1)} %collective-permute-done.asked_ref, bf16[450,256]{1,0:T(8,128)(2,1)S(1)} %shard_map.67.rows_ref), custom_call_target="tpu_custom_call" | custom-call | tf_op jit(solution)/shard_map/pallas_call | solution.py:248
  13.8 0.1 collective-permute-start.5
  13.9 0.0 collective-permute-done.3.inner_ref
  13.9 0.6 %shard_map.69 = (bf16[768,128]{1,0:T(8,128)(2,1)S(1)}, bf16[240,128]{1,0:T(8,128)(2,1)S(1)}) custom-call(s32[16,2048]{1,0:T(8,128)S(1)} %get-tuple-element.24.pos_ref, f32[16,2048]{1,0:T(8,128)S(1)} %get-tuple-element.25.weight_ref, s32[1,2048]{1,0:T(1,128)S(1)} %get-tuple-element.26.count_ref, bf16[450,256]{1,0:T(8,128)(2,1)S(1)} %get-tuple-element.22.own_ref, ...), custom_call_target="tpu_custom_call" | custom-call | tf_op jit(solution)/shard_map/pallas_call | solution.py:227
  14.5 1.1 %collective-permute-start.4 = (bf16[240,128]{1,0:T(8,128)(2,1)S(1)}, bf16[240,128]{1,0:T(8,128)(2,1)S(1)}, u32[]{:S(2)}, u32[]{:S(2)}) collective-permute-start(bf16[240,128]{1,0:T(8,128)(2,1)S(1)} %get-tuple-element.28), channel_id=1, source_target_pairs={{0,8},{1,9},{2,10},{3,11},{4,12},{5,13},{6,14},{7,15},{8,0},{9,1},... | collective-permute-start | bytes 184328 | tf_op jit(solution)/shard_map/ppermute | solution.py:46
  15.6 3.8 %shard_map.68.late_ref = bf16[768,1920]{1,0:T(8,128)(2,1)S(1)} custom-call(s32[16,2048]{1,0:T(8,128)S(1)} %get-tuple-element.24.pos_ref, f32[16,2048]{1,0:T(8,128)S(1)} %get-tuple-element.25.weight_ref, s32[1,2048]{1,0:T(1,128)S(1)} %get-tuple-element.26.count_ref), custom_call_target="tpu_custom_call" | custom-call | flops 47185920 | bytes 2949120 | tf_op jit(solution)/shard_map/pallas_call | solution.py:164
  19.5 1.5 %collective-permute-done.5.far_ref = bf16[240,128]{1,0:T(8,128)(2,1)S(1)} collective-permute-done((bf16[240,128]{1,0:T(8,128)(2,1)S(1)}, bf16[240,128]{1,0:T(8,128)(2,1)S(1)}, u32[]{:S(2)}, u32[]{:S(2)}) %collective-permute-start.5) | collective-permute-done | bytes 61472 | tf_op jit(solution)/shard_map/ppermute | solution.py:51
  21.0 0.0 collective-permute-done.2.outer_ref
  21.0 0.0 collective-permute-done.4.near_ref
  21.0 0.0 copy-done
  21.0 2.9 %shard_map.71 = bf16[450,2048]{1,0:T(8,128)(2,1)} custom-call(bf16[450,256]{1,0:T(8,128)(2,1)S(1)} %collective-permute-done.2.outer_ref, bf16[450,256]{1,0:T(8,128)(2,1)S(1)} %get-tuple-element.22.own_ref, bf16[450,256]{1,0:T(8,128)(2,1)S(1)} %collective-permute-done.3.inner_ref, bf16[768,1920]{1,0:T(8,128)(2,1)S(1)} %shard_map.68.late_ref, ...), custom_call_target="tpu_custom_call" | custom-call | flops 1415577600 | bytes 1843200 | tf_op jit(solution)/shard_map/pallas_call | solution.py:299
Async XLA Ops:
  0.8 7.5 %collective-permute-start.1 = (s32[3,16,256]{2,1,0:T(8,128)S(1)}, s32[3,16,256]{2,1,0:T(8,128)S(1)}, u32[]{:S(2)}, u32[]{:S(2)}) collective-permute-start(s32[3,16,256]{2,1,0:T(8,128)S(1)} %get-tuple-element.19.own_ref), channel_id=1, source_target_pairs={{0,1},{1,0},{2,3},{3,2},{4,5},{5,4},{6,7},{7,6},{8,9},{9,8},{10,11... | collective-permute-start | bytes 147464 | tf_op jit(solution)/shard_map/ppermute | solution.py:36
  1.3 7.6 %collective-permute-start = (f32[24,256]{1,0:T(8,128)S(1)}, f32[24,256]{1,0:T(8,128)S(1)}, u32[]{:S(2)}, u32[]{:S(2)}) collective-permute-start(f32[24,256]{1,0:T(8,128)S(1)} %get-tuple-element.18), channel_id=1, source_target_pairs={{0,15},{1,2},{2,1},{3,4},{4,3},{5,6},{6,5},{7,8},{8,7},{9,10},{10,... | collective-permute-start | bytes 73736 | tf_op jit(solution)/shard_map/ppermute | solution.py:41
  8.9 12.1 %copy-start = (s32[64]{0:T(128)S(1)}, s32[64]{0:T(128)}, u32[]{:S(2)}) copy-start(s32[64]{0:T(128)} %param.11) | copy-start | bytes 772
  9.0 4.9 %collective-permute-start.3 = (bf16[450,256]{1,0:T(8,128)(2,1)S(1)}, bf16[450,256]{1,0:T(8,128)(2,1)S(1)}, u32[]{:S(2)}, u32[]{:S(2)}) collective-permute-start(bf16[450,256]{1,0:T(8,128)(2,1)S(1)} %get-tuple-element.23), channel_id=1, source_target_pairs={{0,1},{1,0},{2,3},{3,2},{4,5},{5,4},{6,7},{7,6},{8,9},{9,8},{10,11... | collective-permute-start | bytes 691208 | tf_op jit(solution)/shard_map/ppermute | solution.py:36
  9.5 11.5 %collective-permute-start.2 = (bf16[450,256]{1,0:T(8,128)(2,1)S(1)}, bf16[450,256]{1,0:T(8,128)(2,1)S(1)}, u32[]{:S(2)}, u32[]{:S(2)}) collective-permute-start(bf16[450,256]{1,0:T(8,128)(2,1)S(1)} %shard_map.67.rows_ref), channel_id=1, source_target_pairs={{0,15},{1,2},{2,1},{3,4},{4,3},{5,6},{6,5},{7,8},{8,7},{9,10},{10,... | collective-permute-start | bytes 691208 | tf_op jit(solution)/shard_map/ppermute | solution.py:41
  13.8 7.2 %collective-permute-start.5 = (bf16[240,128]{1,0:T(8,128)(2,1)S(1)}, bf16[240,128]{1,0:T(8,128)(2,1)S(1)}, u32[]{:S(2)}, u32[]{:S(2)}) collective-permute-start(bf16[240,128]{1,0:T(8,128)(2,1)S(1)} %shard_map.70), channel_id=1, source_target_pairs={{0,7},{1,10},{2,9},{3,12},{4,11},{5,14},{6,13},{7,0},{8,15},{9,2},... | collective-permute-start | bytes 184328 | tf_op jit(solution)/shard_map/ppermute | solution.py:51
  14.5 6.5 %collective-permute-start.4 = (bf16[240,128]{1,0:T(8,128)(2,1)S(1)}, bf16[240,128]{1,0:T(8,128)(2,1)S(1)}, u32[]{:S(2)}, u32[]{:S(2)}) collective-permute-start(bf16[240,128]{1,0:T(8,128)(2,1)S(1)} %get-tuple-element.28), channel_id=1, source_target_pairs={{0,8},{1,9},{2,10},{3,11},{4,12},{5,13},{6,14},{7,15},{8,0},{9,1},... | collective-permute-start | bytes 184328 | tf_op jit(solution)/shard_map/ppermute | solution.py:46

commit v4 on v3

v4 whole, which is shorter than its diff:
```python
import functools
import math

import jax
import jax.numpy as jnp
from jax import lax
from jax.experimental import pallas as pl
from jax.experimental.pallas import tpu as pltpu
from jax.sharding import PartitionSpec as P

LANES = 128
PACK = 16
MIB = 2**20
FLOPS_PER_MICRO = 10**9
EARLY_TILES = 8
IPICK = 0
OPICK = 3
LOAD = 0
WA = 0
FOLD = 1
VMEM = pl.BlockSpec(memory_space=pltpu.VMEM)
HBM = pl.BlockSpec(memory_space=pltpu.HBM)


def lasting(micros):
    return pl.CostEstimate(flops=int(micros * FLOPS_PER_MICRO), bytes_accessed=0, transcendentals=0)


def even_place():
    return lax.rem(lax.axis_index("lon"), 2) == 0


def row_ids(shape):
    return lax.broadcasted_iota(jnp.int32, shape, 0)


def lane_ids(shape):
    return lax.broadcasted_iota(jnp.int32, shape, 1)


def outer_place(place, count):
    return (place - 1) % count if place % 2 == 0 else (place + 1) % count


def inner_swap(block):
    count = lax.axis_size("lon")
    return lax.ppermute(block, "lon", [(i, i ^ 1) for i in range(count)])


def outer_swap(block):
    count = lax.axis_size("lon")
    return lax.ppermute(block, "lon", [(i, outer_place(i, count)) for i in range(count)])


def half_away(block):
    count = lax.axis_size("lon")
    return lax.ppermute(block, "lon", [(i, (i + count // 2) % count) for i in range(count)])


def half_away_of_outer(block):
    count = lax.axis_size("lon")
    return lax.ppermute(block, "lon", [(i, (outer_place(i, count) + count // 2) % count) for i in range(count)])


def in_hbm(block):
    return pltpu.with_memory_space_constraint(block, pltpu.HBM)


def merged_weights(pos, weight, count):
    valid = row_ids(pos.shape) < count
    masked = jnp.where(valid, weight, jnp.float32(0.0))
    scale = masked / jnp.sum(masked, axis=0, keepdims=True)
    scale = scale.astype(jnp.bfloat16).astype(jnp.float32)
    merged = jnp.zeros(pos.shape, jnp.float32)
    for k in range(pos.shape[0]):
        merged += jnp.where(pos == pos[k : k + 1], scale[k : k + 1], jnp.float32(0.0))
    return merged


def spread_rows(rows, dtype):
    return [jnp.broadcast_to(rows[k : k + 1], (PACK, LANES)).astype(dtype) for k in range(rows.shape[0])]


def fill_piece(w_ref, first, lanes, count, place, spread):
    for group in range(count // PACK):
        acc = jnp.zeros((PACK, LANES), jnp.bfloat16)
        for k in range(len(place)):
            acc = jnp.where(place[k] == jnp.int16(group * PACK), spread[k], acc)
        w_ref[pl.ds(first + group * PACK, PACK), lanes] = acc


def fill_tiles(pos_ref, weight_ref, count_ref, w_ref, first, tiles, near, cap):
    even = even_place()
    row = row_ids((PACK, LANES)).astype(jnp.int16)

    def one_tile(tile, carry):
        taken = pl.ds(pl.multiple_of((first + tile) * LANES, LANES), LANES)
        given = pl.ds(pl.multiple_of(tile * LANES, LANES), LANES)
        pos = pos_ref[:, taken]
        spread = spread_rows(merged_weights(pos, weight_ref[:, taken], count_ref[:, taken]), jnp.bfloat16)
        turned = jnp.where(even, pos, pos + cap * (near - 1) - 2 * cap * lax.div(pos, cap))
        place = [x - row for x in spread_rows(turned, jnp.int16)]
        fill_piece(w_ref, 0, given, near * cap, place, spread)
        return carry

    lax.fori_loop(0, tiles, one_tile, 0, unroll=math.gcd(tiles, 3))


def load_kernel(grad_hbm, pos_hbm, weight_hbm, count_hbm, own_hbm, grad_ref, pos_ref, weight_ref, count_ref, own_ref, info_ref, sems, *, near, cap):
    pairs = ((pos_hbm, pos_ref), (weight_hbm, weight_ref), (count_hbm, count_ref), (own_hbm, own_ref), (grad_hbm, grad_ref))
    copies = [pltpu.make_async_copy(source, target, sems.at[i]) for i, (source, target) in enumerate(pairs)]
    for copy in copies:
        copy.start()
    for copy in copies[:3]:
        copy.wait()
    slots, cells = pos_ref.shape
    last = pl.ds(cells - LANES, LANES)
    pos = pos_ref[:, last]
    local = pos - jnp.where(even_place(), 0, (near - 1) * cap)
    local = jnp.where((local >= 0) & (local < cap), local, -1)
    info_ref[0:slots, :] = local.astype(jnp.float32)
    info_ref[slots : 2 * slots, :] = merged_weights(pos, weight_ref[:, last], count_ref[:, last])
    for copy in copies[3:]:
        copy.wait()


def loaded(grad, pos, weight, count, own):
    near, cap = own.shape
    arrays = (grad, pos, weight, count, own)
    held = [jax.ShapeDtypeStruct(x.shape, x.dtype) for x in arrays]
    return pl.pallas_call(
        functools.partial(load_kernel, near=near, cap=cap),
        out_shape=(*held, jax.ShapeDtypeStruct((2 * pos.shape[0], LANES), jnp.float32)),
        in_specs=[HBM] * 5,
        out_specs=(VMEM,) * 6,
        scratch_shapes=[pltpu.SemaphoreType.DMA((5,))],
        compiler_params=pltpu.CompilerParams(vmem_limit_bytes=16 * MIB),
        cost_estimate=lasting(LOAD),
    )(*[in_hbm(x) for x in arrays])


def weights_kernel(pos_ref, weight_ref, count_ref, w_ref, *, first, near, cap):
    fill_tiles(pos_ref, weight_ref, count_ref, w_ref, first, w_ref.shape[1] // LANES, near, cap)


def dense_weights(pos, weight, count, near, cap, first, tiles, micros):
    return pl.pallas_call(
        functools.partial(weights_kernel, first=first, near=near, cap=cap),
        out_shape=jax.ShapeDtypeStruct((near * cap, tiles * LANES), jnp.bfloat16),
        in_specs=[VMEM] * 3,
        out_specs=VMEM,
        compiler_params=pltpu.CompilerParams(vmem_limit_bytes=16 * MIB),
        cost_estimate=lasting(micros),
    )(pos, weight, count)


def chosen(grad, wanted):
    hit = row_ids((grad.shape[1], wanted.shape[1])) == wanted
    onehot = jnp.where(hit, jnp.float32(1.0), jnp.float32(0.0)).astype(jnp.bfloat16)
    return jnp.dot(grad, onehot, preferred_element_type=jnp.float32).astype(jnp.bfloat16)


def outer_pick_kernel(grad_ref, asked_ref, out_ref):
    near = asked_ref.shape[0]
    wanted = jnp.where(even_place(), asked_ref[near - 1 : near, :], asked_ref[0:1, :])
    out_ref[...] = chosen(grad_ref[...], wanted)


def inner_pick_kernel(grad_ref, asked_ref, own_ref, out_ref, own_out):
    near = asked_ref.shape[0]
    wanted = jnp.where(even_place(), asked_ref[0:1, :], asked_ref[near - 1 : near, :])
    out_ref[...] = chosen(grad_ref[...], wanted)
    own_out[...] = chosen(grad_ref[...], own_ref[near // 2 : near // 2 + 1, :])


def picked(kernel, outputs, micros, grad, *asked):
    shape = jax.ShapeDtypeStruct((grad.shape[0], asked[0].shape[1]), grad.dtype)
    return pl.pallas_call(
        kernel,
        out_shape=(shape,) * outputs,
        in_specs=[VMEM] * (1 + len(asked)),
        out_specs=(VMEM,) * outputs,
        compiler_params=pltpu.CompilerParams(vmem_limit_bytes=16 * MIB),
        cost_estimate=lasting(micros),
    )(grad, *asked)


def half_rows(cols):
    return -(-cols // (2 * PACK)) * PACK


def pack_fold(total, edge_ref, sum_ref):
    cols, half = total.shape[0], edge_ref.shape[0]
    tail = cols // 8 * 8
    sum_ref[pl.ds(tail, 2 * half - tail), :] = jnp.zeros((2 * half - tail, LANES), jnp.float32)
    sum_ref[0:cols, :] = total
    upper = pltpu.roll(sum_ref[0:half, :], LANES // 2, 1)
    packed = jnp.where(lane_ids((half, LANES)) < LANES // 2, upper, sum_ref[half : 2 * half, :])
    edge_ref[...] = packed.astype(jnp.bfloat16)


def near_fold_kernel(pos_ref, weight_ref, count_ref, own_ref, inner_ref, w_ref, edge_ref, sum_ref, *, near, cap):
    fill_tiles(pos_ref, weight_ref, count_ref, w_ref, pos_ref.shape[1] // LANES - 1, 1, near, cap)
    total = jnp.dot(own_ref[...], w_ref[cap : 2 * cap, :], preferred_element_type=jnp.float32)
    total += jnp.dot(inner_ref[...], w_ref[2 * cap : 3 * cap, :], preferred_element_type=jnp.float32)
    pack_fold(total, edge_ref, sum_ref)


def near_fold(pos, weight, count, own, inner, near):
    cols, cap = own.shape
    half = half_rows(cols)
    return pl.pallas_call(
        functools.partial(near_fold_kernel, near=near, cap=cap),
        out_shape=(jax.ShapeDtypeStruct((near * cap, LANES), jnp.bfloat16), jax.ShapeDtypeStruct((half, LANES), jnp.bfloat16)),
        in_specs=[VMEM] * 5,
        out_specs=(VMEM,) * 2,
        scratch_shapes=[pltpu.VMEM((2 * half, LANES), jnp.float32)],
        compiler_params=pltpu.CompilerParams(vmem_limit_bytes=16 * MIB),
        cost_estimate=lasting(FOLD),
    )(pos, weight, count, own, inner)


def far_fold_kernel(info_ref, rows_ref, edge_ref, w_ref, sum_ref):
    slots, cap = info_ref.shape[0] // 2, rows_ref.shape[1]
    row = row_ids((PACK, LANES)).astype(jnp.int16)
    place = [x - row for x in spread_rows(info_ref[0:slots, :].astype(jnp.int32), jnp.int16)]
    fill_piece(w_ref, 0, pl.ds(0, LANES), cap, place, spread_rows(info_ref[slots:, :], jnp.bfloat16))
    pack_fold(jnp.dot(rows_ref[...], w_ref[...], preferred_element_type=jnp.float32), edge_ref, sum_ref)


def far_fold(info, rows):
    cols, cap = rows.shape
    half = half_rows(cols)
    return pl.pallas_call(
        far_fold_kernel,
        out_shape=jax.ShapeDtypeStruct((half, LANES), jnp.bfloat16),
        in_specs=[VMEM] * 2,
        out_specs=VMEM,
        scratch_shapes=[pltpu.VMEM((cap, LANES), jnp.bfloat16), pltpu.VMEM((2 * half, LANES), jnp.float32)],
        compiler_params=pltpu.CompilerParams(vmem_limit_bytes=16 * MIB),
        cost_estimate=lasting(FOLD),
    )(info, rows)


def mixed(parts, w_ref, lanes):
    cap = parts[0].shape[1]
    acc = None
    for i, part in enumerate(parts):
        term = jnp.dot(part[...], w_ref[pl.ds(i * cap, cap), lanes], preferred_element_type=jnp.float32)
        acc = term if acc is None else acc + term
    return acc


def unpack_fold(mirrors, src_ref, cols):
    fold = src_ref.shape[1]
    unused = jnp.full((1, LANES - fold), -1, jnp.int32)
    halves = []
    for shift in (0, LANES // 2):
        source = jnp.concatenate([unused, src_ref[...] + shift], axis=1)
        hit = row_ids((LANES, LANES)) == source
        onehot = jnp.where(hit, jnp.float32(1.0), jnp.float32(0.0)).astype(jnp.bfloat16)
        halves.append(sum(jnp.dot(m[...], onehot, preferred_element_type=jnp.float32) for m in mirrors))
    return jnp.concatenate(halves, axis=0)[0:cols]


def body_kernel(outer_ref, own_ref, inner_ref, early_ref, late_ref, last_ref, near_ref, far_ref, src_ref, out_hbm, buffer, sems, *, width):
    parts = (outer_ref, own_ref, inner_ref)
    copies, start = [], 0
    for w_ref in (early_ref, late_ref, last_ref):
        for inside in range(0, w_ref.shape[1], width):
            taken = min(width, w_ref.shape[1] - inside)
            total = mixed(parts, w_ref, pl.ds(inside, taken))
            if w_ref is last_ref:
                total += unpack_fold((near_ref, far_ref), src_ref, own_ref.shape[0])
            lanes = pl.ds(start, taken)
            buffer[:, lanes] = total.astype(jnp.bfloat16)
            copies.append(pltpu.make_async_copy(buffer.at[:, lanes], out_hbm.at[:, lanes], sems.at[len(copies)]))
            copies[-1].start()
            start += taken
    for copy in copies:
        copy.wait()


def body_sums(outer, own, inner, dense, mirrors, fold_src):
    cols, width = own.shape[0], 4 * LANES
    cells = sum(w.shape[1] for w in dense)
    steps = sum(-(-w.shape[1] // width) for w in dense)
    return pl.pallas_call(
        functools.partial(body_kernel, width=width),
        out_shape=jax.ShapeDtypeStruct((cols, cells), jnp.bfloat16),
        in_specs=[VMEM] * 9,
        out_specs=HBM,
        scratch_shapes=[pltpu.VMEM((cols, cells), jnp.bfloat16), pltpu.SemaphoreType.DMA((steps,))],
        compiler_params=pltpu.CompilerParams(vmem_limit_bytes=24 * MIB),
        cost_estimate=lasting(2.5),
    )(outer, own, inner, *dense, *mirrors, fold_src)


def local(analysis_grad, requests, slot_pos, slot_weight, slot_count, fold_src):
    near, cap = requests.shape
    tiles = slot_pos.shape[0] // LANES
    asked_inner = inner_swap(requests)
    asked_outer = outer_swap(requests)
    grad, pos, weight, count, own_asks, info = loaded(analysis_grad.T, slot_pos.T, slot_weight.T, slot_count[None, :], requests)
    info = outer_swap(info)
    for_inner, own = picked(inner_pick_kernel, 2, IPICK, grad, asked_inner, own_asks)
    early_w = dense_weights(pos, weight, count, near, cap, 0, EARLY_TILES, WA)
    asked_outer, for_inner, early_w = lax.optimization_barrier((asked_outer, for_inner, early_w))
    inner = inner_swap(for_inner)
    (for_outer,) = picked(outer_pick_kernel, 1, OPICK, grad, asked_outer)
    outer = outer_swap(for_outer)
    last_w, near_edge = near_fold(pos, weight, count, own, inner, near)
    near_mirror = half_away(near_edge)
    far_mirror = half_away_of_outer(far_fold(info, for_outer))
    late_w = dense_weights(pos, weight, count, near, cap, EARLY_TILES, tiles - EARLY_TILES - 1, FOLD)
    return body_sums(outer, own, inner, (early_w, late_w, last_w), (near_mirror, far_mirror), fold_src[None, :]).T


def solution(mesh):
    in_specs = (
        P(("members", "lon"), None),
        P("lon", None),
        P("lon", None),
        P("lon", None),
        P("lon"),
        P("lon"),
    )
    out_specs = P(("members", "lon"), None)
    return jax.shard_map(local, mesh=mesh, in_specs=in_specs, out_specs=out_specs, check_vma=False)
```

time: 24.1 us -> 25.6 us (1.062)
  waiting for transfers between devices: 1.53 us -> 3.51 us
  Pallas kernels: 10.9 us -> 10.4 us
    ppermute x1, waiting for transfers between devices: 1.52 us -> 3.49 us  [half_away_of_outer(): lax.ppermute(block, 'lon', [(i, (outer_place(i, count) + count // 2) % co...]
    ppermute x2 -> x3, starting transfers between devices: 9.64 us -> 10.2 us  [outer_swap(): lax.ppermute(block, 'lon', [(i, outer_place(i, count)) for i in range(cou...]
    ppermute x1, starting transfers between devices: 1.15 us -> 0.62 us  [half_away(): lax.ppermute(block, 'lon', [(i, (i + count // 2) % count) for i in range(...]
    pallas_call x4, Pallas kernels: 8.84 us -> 8.33 us  [the longest x2 4 us: dense_weights(): pl.pallas_call(functools.partial(weights_kernel, first=first, near=near,...]
  transfers between devices with their start and end apart: 6 -> 7, of which waited for: 1 -> 1; matrix products, arithmetic and copies ran while one was open for 0% -> 0% of each run, Pallas kernels for 30% -> 29%
where the time goes in v4:
time: 25.6 us; the launch traced here: 25.4 us
  starting transfers between devices  11.4 us (45%)
  Pallas kernels  10.4 us (41%)
  waiting for transfers between devices  3.51 us (14%)
    ppermute x3, starting transfers between devices, outer_swap(): lax.ppermute(block, 'lon', [(i, outer_place(i, count)) for i in range(cou...  10.2 us
    pallas_call x2, Pallas kernels, dense_weights(): pl.pallas_call(functools.partial(weights_kernel, first=first, near=near,...  4 us
    ppermute x1, waiting for transfers between devices, half_away_of_outer(): lax.ppermute(block, 'lon', [(i, (outer_place(i, count) + count // 2) % co...  3.49 us
    pallas_call x1, Pallas kernels, body_sums(): pl.pallas_call(functools.partial(body_kernel, width=width), out_shape=jax...  2.93 us
    pallas_call x1, Pallas kernels, loaded(): pl.pallas_call(functools.partial(load_kernel, near=near, cap=cap), out_sh...  1.4 us
    pallas_call x2, Pallas kernels, picked(): pl.pallas_call(kernel, out_shape=(shape,) * outputs, in_specs=[VMEM] * (1...  1.09 us
    ppermute x1, starting transfers between devices, half_away(): lax.ppermute(block, 'lon', [(i, (i + count // 2) % count) for i in range(...  0.62 us
    pallas_call x1, Pallas kernels, near_fold(): pl.pallas_call(functools.partial(near_fold_kernel, near=near, cap=cap), o...  0.59 us
  transfers between devices with their start and end apart: 7, of which 1 were waited for; matrix products, arithmetic and copies ran while one was open for 0% of the time, Pallas kernels for 29%

profile of v4, /device:TPU:0, one launch (start us, length us, event | category | flops | bytes accessed | tf_op | source)
XLA Modules:
  0.0 25.4 jit_solution(12996440495675578950)
XLA Ops:
  0.0 0.5 %collective-permute-start.1 = (s32[3,256]{1,0:T(4,128)}, s32[3,256]{1,0:T(4,128)S(1)}, u32[]{:S(2)}, u32[]{:S(2)}) collective-permute-start(s32[3,256]{1,0:T(4,128)} %own_hbm.1), channel_id=1, source_target_pairs={{0,1},{1,0},{2,3},{3,2},{4,5},{5,4},{6,7},{7,6},{8,9},{9,8},{10,11... | collective-permute-start | bytes 9224 | tf_op jit(solution)/shard_map/ppermute | solution.py:47
  0.5 5.7 %collective-permute-start = (s32[3,256]{1,0:T(4,128)}, s32[3,256]{1,0:T(4,128)S(1)}, u32[]{:S(2)}, u32[]{:S(2)}) collective-permute-start(s32[3,256]{1,0:T(4,128)} %own_hbm.1), channel_id=1, source_target_pairs={{0,15},{1,2},{2,1},{3,4},{4,3},{5,6},{6,5},{7,8},{8,7},{9,10},{10,... | collective-permute-start | bytes 9224 | tf_op jit(solution)/shard_map/ppermute | solution.py:52
  6.1 1.4 %shard_map.64 = (bf16[450,1024]{1,0:T(8,128)(2,1)S(1)}, s32[16,2048]{1,0:T(8,128)S(1)}, f32[16,2048]{1,0:T(8,128)S(1)}, s32[1,2048]{1,0:T(1,128)S(1)}, s32[3,256]{1,0:T(4,128)S(1)}, /*index=5*/f32[32,128]{1,0:T(8,128)S(1)}) custom-call(bf16[450,1024]{1,0:T(8,128)(2,1)} %bitcast.7, s32[16,2048]{1,0:T(8,128)} %bitcast.8, f32[16,2048]{1,0:T(8,128)} %bitcast.9, ...), custom_call_target="tpu_custom_call" | custom-call | tf_op jit(solution)/shard_map/pallas_call | solution.py:131
  7.5 0.1 collective-permute-start.5
  7.6 2.1 %shard_map.66.early_ref = bf16[768,1024]{1,0:T(8,128)(2,1)S(1)} custom-call(s32[16,2048]{1,0:T(8,128)S(1)} %get-tuple-element.21.pos_ref, f32[16,2048]{1,0:T(8,128)S(1)} %get-tuple-element.22.weight_ref, s32[1,2048]{1,0:T(1,128)S(1)} %get-tuple-element.23.count_ref), custom_call_target="tpu_custom_call" | custom-call | tf_op jit(solution)/shard_map/pallas_call | solution.py:147
  9.8 0.0 collective-permute-done.1.asked_ref
  9.8 0.7 %shard_map.65 = (bf16[450,256]{1,0:T(8,128)(2,1)S(1)}, bf16[450,256]{1,0:T(8,128)(2,1)S(1)}) custom-call(bf16[450,1024]{1,0:T(8,128)(2,1)S(1)} %get-tuple-element.18.grad_ref, s32[3,256]{1,0:T(4,128)S(1)} %collective-permute-done.1.asked_ref, s32[3,256]{1,0:T(4,128)S(1)} %get-tuple-element.19.own_ref), custom_call_target="tpu_custom_call" | custom-call | tf_op jit(solution)/shard_map/pallas_call | solution.py:178
  10.4 0.0 collective-permute-done.asked_ref
  10.4 0.1 collective-permute-start.3
  10.5 0.4 %shard_map.67.rows_ref = bf16[450,256]{1,0:T(8,128)(2,1)S(1)} custom-call(bf16[450,1024]{1,0:T(8,128)(2,1)S(1)} %get-tuple-element.18.grad_ref, s32[3,256]{1,0:T(4,128)S(1)} %collective-permute-done.asked_ref), custom_call_target="tpu_custom_call" | custom-call | flops 3000000000 | tf_op jit(solution)/shard_map/pallas_call | solution.py:178
  11.0 4.5 %collective-permute-start.2 = (bf16[450,256]{1,0:T(8,128)(2,1)S(1)}, bf16[450,256]{1,0:T(8,128)(2,1)S(1)}, u32[]{:S(2)}, u32[]{:S(2)}) collective-permute-start(bf16[450,256]{1,0:T(8,128)(2,1)S(1)} %shard_map.67.rows_ref), channel_id=1, source_target_pairs={{0,15},{1,2},{2,1},{3,4},{4,3},{5,6},{6,5},{7,8},{8,7},{9,10},{10,... | collective-permute-start | bytes 691208 | tf_op jit(solution)/shard_map/ppermute | solution.py:52
  15.4 0.0 collective-permute-done.5.info_ref
  15.4 0.4 %shard_map.70 = bf16[240,128]{1,0:T(8,128)(2,1)S(1)} custom-call(f32[32,128]{1,0:T(8,128)S(1)} %collective-permute-done.5.info_ref, bf16[450,256]{1,0:T(8,128)(2,1)S(1)} %shard_map.67.rows_ref), custom_call_target="tpu_custom_call" | custom-call | flops 1000000000 | tf_op jit(solution)/shard_map/pallas_call | solution.py:234
  15.8 0.1 collective-permute-start.6
  15.9 0.0 collective-permute-done.3.inner_ref
  15.9 0.6 %shard_map.69 = (bf16[768,128]{1,0:T(8,128)(2,1)S(1)}, bf16[240,128]{1,0:T(8,128)(2,1)S(1)}) custom-call(s32[16,2048]{1,0:T(8,128)S(1)} %get-tuple-element.21.pos_ref, f32[16,2048]{1,0:T(8,128)S(1)} %get-tuple-element.22.weight_ref, s32[1,2048]{1,0:T(1,128)S(1)} %get-tuple-element.23.count_ref, bf16[450,256]{1,0:T(8,128)(2,1)S(1)} %get-tuple-element.25.own_ref, ...), custom_call_target="tpu_custom_call" | custom-call | flops 1000000000 | tf_op jit(solution)/shard_map/pallas_call | solution.py:212
  16.5 0.0 copy-start
  16.5 0.6 %collective-permute-start.4 = (bf16[240,128]{1,0:T(8,128)(2,1)S(1)}, bf16[240,128]{1,0:T(8,128)(2,1)S(1)}, u32[]{:S(2)}, u32[]{:S(2)}) collective-permute-start(bf16[240,128]{1,0:T(8,128)(2,1)S(1)} %get-tuple-element.29), channel_id=1, source_target_pairs={{0,8},{1,9},{2,10},{3,11},{4,12},{5,13},{6,14},{7,15},{8,0},{9,1},... | collective-permute-start | bytes 184328 | tf_op jit(solution)/shard_map/ppermute | solution.py:57
  17.1 1.9 %shard_map.68.late_ref = bf16[768,896]{1,0:T(8,128)(2,1)S(1)} custom-call(s32[16,2048]{1,0:T(8,128)S(1)} %get-tuple-element.21.pos_ref, f32[16,2048]{1,0:T(8,128)S(1)} %get-tuple-element.22.weight_ref, s32[1,2048]{1,0:T(1,128)S(1)} %get-tuple-element.23.count_ref), custom_call_target="tpu_custom_call" | custom-call | flops 1000000000 | tf_op jit(solution)/shard_map/pallas_call | solution.py:147
  19.0 3.5 %collective-permute-done.6.far_ref = bf16[240,128]{1,0:T(8,128)(2,1)S(1)} collective-permute-done((bf16[240,128]{1,0:T(8,128)(2,1)S(1)}, bf16[240,128]{1,0:T(8,128)(2,1)S(1)}, u32[]{:S(2)}, u32[]{:S(2)}) %collective-permute-start.6) | collective-permute-done | bytes 61472 | tf_op jit(solution)/shard_map/ppermute | solution.py:62
  22.5 0.0 collective-permute-done.2.outer_ref
  22.5 0.0 collective-permute-done.4.near_ref
  22.5 0.0 copy-done
  22.5 2.9 %shard_map.71 = bf16[450,2048]{1,0:T(8,128)(2,1)} custom-call(bf16[450,256]{1,0:T(8,128)(2,1)S(1)} %collective-permute-done.2.outer_ref, bf16[450,256]{1,0:T(8,128)(2,1)S(1)} %get-tuple-element.25.own_ref, bf16[450,256]{1,0:T(8,128)(2,1)S(1)} %collective-permute-done.3.inner_ref, bf16[768,1024]{1,0:T(8,128)(2,1)S(1)} %shard_map.66.early_ref, ...), custom_call_target="tpu_custom_call" | custom-call | flops 2500000000 | tf_op jit(solution)/shard_map/pallas_call | solution.py:288
Async XLA Ops:
  0.0 9.8 %collective-permute-start.1 = (s32[3,256]{1,0:T(4,128)}, s32[3,256]{1,0:T(4,128)S(1)}, u32[]{:S(2)}, u32[]{:S(2)}) collective-permute-start(s32[3,256]{1,0:T(4,128)} %own_hbm.1), channel_id=1, source_target_pairs={{0,1},{1,0},{2,3},{3,2},{4,5},{5,4},{6,7},{7,6},{8,9},{9,8},{10,11... | collective-permute-start | bytes 9224 | tf_op jit(solution)/shard_map/ppermute | solution.py:47
  0.5 10.0 %collective-permute-start = (s32[3,256]{1,0:T(4,128)}, s32[3,256]{1,0:T(4,128)S(1)}, u32[]{:S(2)}, u32[]{:S(2)}) collective-permute-start(s32[3,256]{1,0:T(4,128)} %own_hbm.1), channel_id=1, source_target_pairs={{0,15},{1,2},{2,1},{3,4},{4,3},{5,6},{6,5},{7,8},{8,7},{9,10},{10,... | collective-permute-start | bytes 9224 | tf_op jit(solution)/shard_map/ppermute | solution.py:52
  7.5 7.9 %collective-permute-start.5 = (f32[32,128]{1,0:T(8,128)S(1)}, f32[32,128]{1,0:T(8,128)S(1)}, u32[]{:S(2)}, u32[]{:S(2)}) collective-permute-start(f32[32,128]{1,0:T(8,128)S(1)} %get-tuple-element.30), channel_id=1, source_target_pairs={{0,15},{1,2},{2,1},{3,4},{4,3},{5,6},{6,5},{7,8},{8,7},{9,10},{10,... | collective-permute-start | bytes 49160 | tf_op jit(solution)/shard_map/ppermute | solution.py:52
  10.4 5.5 %collective-permute-start.3 = (bf16[450,256]{1,0:T(8,128)(2,1)S(1)}, bf16[450,256]{1,0:T(8,128)(2,1)S(1)}, u32[]{:S(2)}, u32[]{:S(2)}) collective-permute-start(bf16[450,256]{1,0:T(8,128)(2,1)S(1)} %get-tuple-element.26), channel_id=1, source_target_pairs={{0,1},{1,0},{2,3},{3,2},{4,5},{5,4},{6,7},{7,6},{8,9},{9,8},{10,11... | collective-permute-start | bytes 691208 | tf_op jit(solution)/shard_map/ppermute | solution.py:47
  11.0 11.5 %collective-permute-start.2 = (bf16[450,256]{1,0:T(8,128)(2,1)S(1)}, bf16[450,256]{1,0:T(8,128)(2,1)S(1)}, u32[]{:S(2)}, u32[]{:S(2)}) collective-permute-start(bf16[450,256]{1,0:T(8,128)(2,1)S(1)} %shard_map.67.rows_ref), channel_id=1, source_target_pairs={{0,15},{1,2},{2,1},{3,4},{4,3},{5,6},{6,5},{7,8},{8,7},{9,10},{10,... | collective-permute-start | bytes 691208 | tf_op jit(solution)/shard_map/ppermute | solution.py:52
  15.8 6.7 %collective-permute-start.6 = (bf16[240,128]{1,0:T(8,128)(2,1)S(1)}, bf16[240,128]{1,0:T(8,128)(2,1)S(1)}, u32[]{:S(2)}, u32[]{:S(2)}) collective-permute-start(bf16[240,128]{1,0:T(8,128)(2,1)S(1)} %shard_map.70), channel_id=1, source_target_pairs={{0,7},{1,10},{2,9},{3,12},{4,11},{5,14},{6,13},{7,0},{8,15},{9,2},... | collective-permute-start | bytes 184328 | tf_op jit(solution)/shard_map/ppermute | solution.py:62
  16.5 6.0 %copy-start = (s32[64]{0:T(128)S(1)}, s32[64]{0:T(128)}, u32[]{:S(2)}) copy-start(s32[64]{0:T(128)} %param.11) | copy-start | bytes 772
  16.5 6.0 %collective-permute-start.4 = (bf16[240,128]{1,0:T(8,128)(2,1)S(1)}, bf16[240,128]{1,0:T(8,128)(2,1)S(1)}, u32[]{:S(2)}, u32[]{:S(2)}) collective-permute-start(bf16[240,128]{1,0:T(8,128)(2,1)S(1)} %get-tuple-element.29), channel_id=1, source_target_pairs={{0,8},{1,9},{2,10},{3,11},{4,12},{5,13},{6,14},{7,15},{8,0},{9,1},... | collective-permute-start | bytes 184328 | tf_op jit(solution)/shard_map/ppermute | solution.py:57

commit v5 on v2

v5 whole, which is shorter than its diff:
```python
import functools
import math

import jax
import jax.numpy as jnp
from jax import lax
from jax.experimental import pallas as pl
from jax.experimental.pallas import tpu as pltpu
from jax.sharding import PartitionSpec as P

LANES = 128
PACK = 16
MID_TILES = 12
MIB = 2**20
FLOPS_PER_MICRO = 10**9
OPICK = 3
IPICK = 0
LOAD = 0
MID = 30
REST = 1
EDGE = 1
BODY = 1
VMEM = pl.BlockSpec(memory_space=pltpu.VMEM)
HBM = pl.BlockSpec(memory_space=pltpu.HBM)
ANY = pl.BlockSpec(memory_space=pl.ANY)


def lasting(micros):
    return pl.CostEstimate(flops=int(micros * FLOPS_PER_MICRO), bytes_accessed=0, transcendentals=0)


def row_ids(shape):
    return lax.broadcasted_iota(jnp.int32, shape, 0)


def lane_ids(shape):
    return lax.broadcasted_iota(jnp.int32, shape, 1)


def sent(block, target):
    count = lax.axis_size("lon")
    return lax.ppermute(block, "lon", [(i, target(i, count)) for i in range(count)])


def inner_place(place, count):
    return place ^ 1


def outer_place(place, count):
    return (place - 1) % count if place % 2 == 0 else (place + 1) % count


def half_place(place, count):
    return (place + count // 2) % count


def is_even():
    return lax.rem(lax.axis_index("lon"), 2) == 0


def in_hbm(block):
    return pltpu.with_memory_space_constraint(block, pltpu.HBM)


def merged_weights(pos, weight, count):
    valid = row_ids(pos.shape) < count
    masked = jnp.where(valid, weight, jnp.float32(0.0))
    scale = masked / jnp.sum(masked, axis=0, keepdims=True)
    scale = scale.astype(jnp.bfloat16).astype(jnp.float32)
    merged = jnp.zeros(pos.shape, jnp.float32)
    for k in range(pos.shape[0]):
        merged += jnp.where(pos == pos[k : k + 1], scale[k : k + 1], jnp.float32(0.0))
    return merged


def spread_rows(rows, dtype):
    return [jnp.broadcast_to(rows[k : k + 1], (PACK, LANES)).astype(dtype) for k in range(rows.shape[0])]


def fill_piece(w_ref, first, lanes, count, place, spread):
    for group in range(count // PACK):
        acc = jnp.zeros((PACK, LANES), jnp.bfloat16)
        for k in range(len(place)):
            acc = jnp.where(place[k] == jnp.int16(group * PACK), spread[k], acc)
        w_ref[pl.ds(first + group * PACK, PACK), lanes] = acc


def fill_tiles(pos_ref, weight_ref, count_ref, w_ref, first, tiles, near, cap):
    even = is_even()
    row = row_ids((PACK, LANES)).astype(jnp.int16)

    def one_tile(tile, carry):
        taken = pl.ds(pl.multiple_of((first + tile) * LANES, LANES), LANES)
        given = pl.ds(pl.multiple_of(tile * LANES, LANES), LANES)
        pos = pos_ref[:, taken]
        spread = spread_rows(merged_weights(pos, weight_ref[:, taken], count_ref[:, taken]), jnp.bfloat16)
        turned = jnp.where(even, pos, pos + cap * (near - 1) - 2 * cap * lax.div(pos, cap))
        place = [x - row for x in spread_rows(turned, jnp.int16)]
        fill_piece(w_ref, 0, given, near * cap, place, spread)
        return carry

    lax.fori_loop(0, tiles, one_tile, 0, unroll=math.gcd(tiles, 3))


def load_kernel(*refs):
    count = (len(refs) - 1) // 2
    copies = [pltpu.make_async_copy(refs[i], refs[count + i], refs[-1].at[i]) for i in range(count)]
    for copy in copies:
        copy.start()
    for copy in copies:
        copy.wait()


def loaded(*arrays):
    return pl.pallas_call(
        load_kernel,
        out_shape=tuple(jax.ShapeDtypeStruct(x.shape, x.dtype) for x in arrays),
        in_specs=[HBM] * len(arrays),
        out_specs=(VMEM,) * len(arrays),
        scratch_shapes=[pltpu.SemaphoreType.DMA((len(arrays),))],
        compiler_params=pltpu.CompilerParams(vmem_limit_bytes=16 * MIB),
        cost_estimate=lasting(LOAD),
    )(*[in_hbm(x) for x in arrays])


def weights_kernel(after_ref, pos_ref, weight_ref, count_ref, w_ref, *, first, near, cap):
    del after_ref
    fill_tiles(pos_ref, weight_ref, count_ref, w_ref, first, w_ref.shape[1] // LANES, near, cap)


def dense_weights(after, pos, weight, count, near, cap, first, tiles, micros):
    return pl.pallas_call(
        functools.partial(weights_kernel, first=first, near=near, cap=cap),
        out_shape=jax.ShapeDtypeStruct((near * cap, tiles * LANES), jnp.bfloat16),
        in_specs=[ANY] + [VMEM] * 3,
        out_specs=VMEM,
        compiler_params=pltpu.CompilerParams(vmem_limit_bytes=16 * MIB),
        cost_estimate=lasting(micros),
    )(after, pos, weight, count)


def chosen(grad, wanted):
    hit = row_ids((grad.shape[1], wanted.shape[1])) == wanted
    onehot = jnp.where(hit, jnp.float32(1.0), jnp.float32(0.0)).astype(jnp.bfloat16)
    return jnp.dot(grad, onehot, preferred_element_type=jnp.float32).astype(jnp.bfloat16)


def outer_pick_kernel(grad_ref, asked_ref, out_ref):
    near = asked_ref.shape[0]
    wanted = jnp.where(is_even(), asked_ref[near - 1 : near, :], asked_ref[0:1, :])
    out_ref[...] = chosen(grad_ref[...], wanted)


def inner_pick_kernel(grad_ref, asked_ref, own_ref, after_ref, out_ref, own_out):
    del after_ref
    near = asked_ref.shape[0]
    wanted = jnp.where(is_even(), asked_ref[0:1, :], asked_ref[near - 1 : near, :])
    out_ref[...] = chosen(grad_ref[...], wanted)
    own_out[...] = chosen(grad_ref[...], own_ref[near // 2 : near // 2 + 1, :])


def picked(kernel, outputs, micros, grad, *asked):
    shape = jax.ShapeDtypeStruct((grad.shape[0], asked[0].shape[1]), grad.dtype)
    return pl.pallas_call(
        kernel,
        out_shape=(shape,) * outputs,
        in_specs=[VMEM] * min(len(asked) + 1, 3) + [ANY] * max(len(asked) - 2, 0),
        out_specs=(VMEM,) * outputs,
        compiler_params=pltpu.CompilerParams(vmem_limit_bytes=16 * MIB),
        cost_estimate=lasting(micros),
    )(grad, *asked)


def mixed(parts, w_ref, lanes):
    cap = parts[0].shape[1]
    acc = None
    for i, part in enumerate(parts):
        term = jnp.dot(part[...], w_ref[pl.ds(i * cap, cap), lanes], preferred_element_type=jnp.float32)
        acc = term if acc is None else acc + term
    return acc


def edge_kernel(outer_ref, own_ref, inner_ref, w_ref, sum_ref, edge_ref):
    cells, cols, half = w_ref.shape[1], own_ref.shape[0], edge_ref.shape[0]
    total = mixed((outer_ref, own_ref, inner_ref), w_ref, pl.ds(cells - LANES, LANES))
    tail = cols // 8 * 8
    sum_ref[pl.ds(tail, 2 * half - tail), :] = jnp.zeros((2 * half - tail, LANES), jnp.float32)
    sum_ref[0:cols, :] = total
    upper = pltpu.roll(sum_ref[0:half, :], LANES // 2, 1)
    packed = jnp.where(lane_ids((half, LANES)) < LANES // 2, upper, sum_ref[half : 2 * half, :])
    edge_ref[...] = packed.astype(jnp.bfloat16)


def edge_sums(outer, own, inner, dense):
    cols = own.shape[0]
    half = -(-cols // (2 * PACK)) * PACK
    return pl.pallas_call(
        edge_kernel,
        out_shape=(jax.ShapeDtypeStruct((2 * half, LANES), jnp.float32), jax.ShapeDtypeStruct((half, LANES), jnp.bfloat16)),
        in_specs=[VMEM] * 4,
        out_specs=(VMEM,) * 2,
        compiler_params=pltpu.CompilerParams(vmem_limit_bytes=16 * MIB),
        cost_estimate=lasting(EDGE),
    )(outer, own, inner, dense)


def body_kernel(outer_ref, own_ref, inner_ref, late_ref, early_ref, out_hbm, buffer, sems, *, steps):
    for i, (start, width) in enumerate(steps):
        ahead = late_ref.shape[1]
        w_ref, inside = (late_ref, start) if start < ahead else (early_ref, start - ahead)
        buffer[:, pl.ds(start, width)] = mixed((outer_ref, own_ref, inner_ref), w_ref, pl.ds(inside, width)).astype(jnp.bfloat16)
        pltpu.make_async_copy(buffer.at[:, pl.ds(start, width)], out_hbm.at[:, pl.ds(start, width)], sems.at[i]).start()
    for i, (start, width) in enumerate(steps):
        pltpu.make_async_copy(buffer.at[:, pl.ds(start, width)], out_hbm.at[:, pl.ds(start, width)], sems.at[i]).wait()


def cuts(first, last, width):
    return [(start, min(width, last - start)) for start in range(first, last, width)]


def body_sums(outer, own, inner, late_w, early_w):
    cols, ahead = own.shape[0], late_w.shape[1]
    cells = ahead + early_w.shape[1]
    steps = cuts(0, ahead, 4 * LANES) + cuts(ahead, cells - LANES, 4 * LANES)
    return pl.pallas_call(
        functools.partial(body_kernel, steps=steps),
        out_shape=jax.ShapeDtypeStruct((cols, cells), jnp.bfloat16),
        in_specs=[VMEM] * 5,
        out_specs=HBM,
        scratch_shapes=[pltpu.VMEM((cols, cells), jnp.bfloat16), pltpu.SemaphoreType.DMA((len(steps),))],
        compiler_params=pltpu.CompilerParams(vmem_limit_bytes=24 * MIB),
        cost_estimate=lasting(BODY),
    )(outer, own, inner, late_w, early_w)


def fold_kernel(whole_ref, sum_ref, mirror_ref, src_ref, out_ref):
    del whole_ref
    cols, half, fold = out_ref.shape[0], mirror_ref.shape[0], src_ref.shape[1]
    unused = jnp.full((1, LANES - fold), -1, jnp.int32)
    others = []
    for shift in (0, LANES // 2):
        source = jnp.concatenate([unused, src_ref[...] + shift], axis=1)
        hit = row_ids((LANES, LANES)) == source
        onehot = jnp.where(hit, jnp.float32(1.0), jnp.float32(0.0)).astype(jnp.bfloat16)
        others.append(jnp.dot(mirror_ref[...], onehot, preferred_element_type=jnp.float32))
    other = jnp.concatenate(others, axis=0)[0:cols]
    out_ref[...] = (sum_ref[0:cols, :] + other).astype(jnp.bfloat16)


def folded(whole, sums, mirror, fold_src):
    cols, cells = whole.shape
    last = cells // LANES - 1
    return pl.pallas_call(
        fold_kernel,
        grid=(1,),
        out_shape=jax.ShapeDtypeStruct((cols, cells), jnp.bfloat16),
        in_specs=[HBM, VMEM, VMEM, VMEM],
        out_specs=pl.BlockSpec((cols, LANES), lambda i: (0, last)),
        input_output_aliases={0: 0},
        compiler_params=pltpu.CompilerParams(vmem_limit_bytes=8 * MIB),
    )(whole, sums, mirror, fold_src)


def local(analysis_grad, requests, slot_pos, slot_weight, slot_count, fold_src):
    near, cap = requests.shape
    tiles = slot_pos.shape[0] // LANES
    rest = tiles - MID_TILES
    asked_inner = sent(requests, inner_place)
    asked_outer = sent(requests, outer_place)
    grad, pos, weight, count, own_asks = loaded(analysis_grad.T, slot_pos.T, slot_weight.T, slot_count[None, :], requests)
    (for_outer,) = picked(outer_pick_kernel, 1, OPICK, grad, asked_outer)
    outer = sent(for_outer, outer_place)
    for_inner, own = picked(inner_pick_kernel, 2, IPICK, grad, asked_inner, own_asks, for_outer)
    inner = sent(for_inner, inner_place)
    mid_w = dense_weights(for_inner, pos, weight, count, near, cap, rest, MID_TILES, MID)
    sums, edge = edge_sums(outer, own, inner, mid_w)
    mirror = sent(edge, half_place)
    rest_w = dense_weights(sums, pos, weight, count, near, cap, 0, rest, REST)
    whole = body_sums(outer, own, inner, rest_w, mid_w)
    return folded(whole, sums, mirror, fold_src[None, :]).T


def solution(mesh):
    in_specs = (
        P(("members", "lon"), None),
        P("lon", None),
        P("lon", None),
        P("lon", None),
        P("lon"),
        P("lon"),
    )
    out_specs = P(("members", "lon"), None)
    return jax.shard_map(local, mesh=mesh, in_specs=in_specs, out_specs=out_specs, check_vma=False)
```

time: 23 us -> 22.6 us (0.983)
  waiting for transfers between devices: 3.11 us -> 2.05 us
  starting transfers between devices: 9.45 us -> 10.1 us
    ppermute x5, waiting for transfers between devices: 3.11 us -> 2.05 us  [sent(): lax.ppermute(block, 'lon', [(i, target(i, count)) for i in range(count)])]
    ppermute x5, starting transfers between devices: 9.45 us -> 10.1 us  [sent(): lax.ppermute(block, 'lon', [(i, target(i, count)) for i in range(count)])]
    pallas_call x4 -> x5, Pallas kernels: 6.53 us -> 6.51 us  [the longest x2 4.16 us: dense_weights(): pl.pallas_call(functools.partial(weights_kernel, first=first, near=near,...]
  transfers between devices with their start and end apart: 5 -> 5, of which waited for: 2 -> 2; matrix products, arithmetic and copies ran while one was open for 0% -> 0% of each run, Pallas kernels for 39% -> 40%
where the time goes in v5:
time: 22.6 us; the launch traced here: 22.4 us
  Pallas kernels  10.2 us (45%)
  starting transfers between devices  10.1 us (45%)
  waiting for transfers between devices  2.05 us (9%)
    ppermute x5, starting transfers between devices, sent(): lax.ppermute(block, 'lon', [(i, target(i, count)) for i in range(count)])  10.1 us
    pallas_call x2, Pallas kernels, dense_weights(): pl.pallas_call(functools.partial(weights_kernel, first=first, near=near,...  4.16 us
    pallas_call x1, Pallas kernels, body_sums(): pl.pallas_call(functools.partial(body_kernel, steps=steps), out_shape=jax...  2.41 us
    ppermute x5, waiting for transfers between devices, sent(): lax.ppermute(block, 'lon', [(i, target(i, count)) for i in range(count)])  2.05 us
    pallas_call x1, Pallas kernels, loaded(): pl.pallas_call(load_kernel, out_shape=tuple((jax.ShapeDtypeStruct(x.shape...  1.27 us
    pallas_call x2, Pallas kernels, picked(): pl.pallas_call(kernel, out_shape=(shape,) * outputs, in_specs=[VMEM] * mi...  1.08 us
    pallas_call x1, Pallas kernels, folded(): pl.pallas_call(fold_kernel, grid=(1,), out_shape=jax.ShapeDtypeStruct((co...  0.93 us
  transfers between devices with their start and end apart: 5, of which 2 were waited for; matrix products, arithmetic and copies ran while one was open for 0% of the time, Pallas kernels for 40%

profile of v5, /device:TPU:0, one launch (start us, length us, event | category | flops | bytes accessed | tf_op | source)
XLA Modules:
  0.0 22.4 jit_solution(814610914872792005)
XLA Ops:
  0.0 5.4 %collective-permute-start = (s32[3,256]{1,0:T(4,128)}, s32[3,256]{1,0:T(4,128)S(1)}, u32[]{:S(2)}, u32[]{:S(2)}) collective-permute-start(s32[3,256]{1,0:T(4,128)} %refs_4_.1), channel_id=1, source_target_pairs={{0,15},{1,2},{2,1},{3,4},{4,3},{5,6},{6,5},{7,8},{8,7},{9,10},{10,... | collective-permute-start | bytes 9224 | tf_op jit(solution)/shard_map/ppermute | solution.py:42
  5.4 0.0 collective-permute-start.2
  5.4 1.3 %shard_map.64 = (bf16[450,1024]{1,0:T(8,128)(2,1)S(1)}, s32[16,2048]{1,0:T(8,128)S(1)}, f32[16,2048]{1,0:T(8,128)S(1)}, s32[1,2048]{1,0:T(1,128)S(1)}, s32[3,256]{1,0:T(4,128)S(1)}) custom-call(bf16[450,1024]{1,0:T(8,128)(2,1)} %bitcast.7, s32[16,2048]{1,0:T(8,128)} %bitcast.8, f32[16,2048]{1,0:T(8,128)} %bitcast.9, s32[1,2048]{1,0:T(1,128)} %bitcast.10, ...), custom_call_target="tpu_custom_call" | custom-call | tf_op jit(solution)/shard_map/pallas_call | solution.py:115
  6.7 0.3 %collective-permute-done.asked_ref = s32[3,256]{1,0:T(4,128)S(1)} collective-permute-done((s32[3,256]{1,0:T(4,128)}, s32[3,256]{1,0:T(4,128)S(1)}, u32[]{:S(2)}, u32[]{:S(2)}) %collective-permute-start) | collective-permute-done | bytes 3104 | tf_op jit(solution)/shard_map/ppermute | solution.py:42
  7.0 0.4 %shard_map.65.after_ref = bf16[450,256]{1,0:T(8,128)(2,1)S(1)} custom-call(bf16[450,1024]{1,0:T(8,128)(2,1)S(1)} %get-tuple-element.14.grad_ref, s32[3,256]{1,0:T(4,128)S(1)} %collective-permute-done.asked_ref), custom_call_target="tpu_custom_call" | custom-call | flops 3000000000 | tf_op jit(solution)/shard_map/pallas_call | solution.py:164
  7.4 4.5 %collective-permute-start.1 = (bf16[450,256]{1,0:T(8,128)(2,1)S(1)}, bf16[450,256]{1,0:T(8,128)(2,1)S(1)}, u32[]{:S(2)}, u32[]{:S(2)}) collective-permute-start(bf16[450,256]{1,0:T(8,128)(2,1)S(1)} %shard_map.65.after_ref), channel_id=1, source_target_pairs={{0,15},{1,2},{2,1},{3,4},{4,3},{5,6},{6,5},{7,8},{8,7},{9,10},{10,... | collective-permute-start | bytes 691208 | tf_op jit(solution)/shard_map/ppermute | solution.py:42
  11.9 0.0 collective-permute-done.2.asked_ref
  11.9 0.7 %shard_map.66 = (bf16[450,256]{1,0:T(8,128)(2,1)S(1)}, bf16[450,256]{1,0:T(8,128)(2,1)S(1)}) custom-call(bf16[450,1024]{1,0:T(8,128)(2,1)S(1)} %get-tuple-element.14.grad_ref, s32[3,256]{1,0:T(4,128)S(1)} %collective-permute-done.2.asked_ref, s32[3,256]{1,0:T(4,128)S(1)} %get-tuple-element.15.own_ref, bf16[450,256]{1,0:T(8,128)(2,1)S(1)} %shard_map.65.after_ref), custom_call_target="tpu_custom_call" | custom-call | tf_op jit(solution)/shard_map/pallas_call | solution.py:164
  12.5 0.1 collective-permute-start.3
  12.6 3.1 %shard_map.67.w_ref.early_ref = bf16[768,1536]{1,0:T(8,128)(2,1)S(1)} custom-call(bf16[450,256]{1,0:T(8,128)(2,1)S(1)} %get-tuple-element.17.after_ref, s32[16,2048]{1,0:T(8,128)S(1)} %get-tuple-element.18.pos_ref, f32[16,2048]{1,0:T(8,128)S(1)} %get-tuple-element.19.weight_ref, s32[1,2048]{1,0:T(1,128)S(1)} %get-tuple-element.20.count_ref), custom_call_target="tpu_custom_call" | custom-call | flops 30000001024 | tf_op jit(solution)/shard_map/pallas_call | solution.py:132
  15.7 0.0 collective-permute-done.3.inner_ref
  15.7 0.0 collective-permute-done.1.outer_ref
  15.8 0.4 %shard_map.68 = (f32[480,128]{1,0:T(8,128)S(1)}, bf16[240,128]{1,0:T(8,128)(2,1)S(1)}) custom-call(bf16[450,256]{1,0:T(8,128)(2,1)S(1)} %collective-permute-done.1.outer_ref, bf16[450,256]{1,0:T(8,128)(2,1)S(1)} %get-tuple-element.16.own_ref, bf16[450,256]{1,0:T(8,128)(2,1)S(1)} %collective-permute-done.3.inner_ref, ...), custom_call_target="tpu_custom_call" | custom-call | flops 1000000000 | tf_op jit(solution)/shard_map/pallas_call | solution.py:197
  16.1 0.1 collective-permute-start.4
  16.2 1.1 %shard_map.69.late_ref = bf16[768,512]{1,0:T(8,128)(2,1)S(1)} custom-call(f32[480,128]{1,0:T(8,128)S(1)} %get-tuple-element.21.after_ref.sum_ref, s32[16,2048]{1,0:T(8,128)S(1)} %get-tuple-element.18.pos_ref, f32[16,2048]{1,0:T(8,128)S(1)} %get-tuple-element.19.weight_ref, s32[1,2048]{1,0:T(1,128)S(1)} %get-tuple-element.20.count_ref), custom_call_target="tpu_custom_call" | custom-call | flops 1000000000 | tf_op jit(solution)/shard_map/pallas_call | solution.py:132
  17.3 0.0 copy-start
  17.3 2.4 %shard_map.70.whole_ref = bf16[450,2048]{1,0:T(8,128)(2,1)} custom-call(bf16[450,256]{1,0:T(8,128)(2,1)S(1)} %collective-permute-done.1.outer_ref, bf16[450,256]{1,0:T(8,128)(2,1)S(1)} %get-tuple-element.16.own_ref, bf16[450,256]{1,0:T(8,128)(2,1)S(1)} %collective-permute-done.3.inner_ref, bf16[768,512]{1,0:T(8,128)(2,1)S(1)} %shard_map.69.late_ref, ...), custom_call_target="tpu_custom_call" | custom-call | flops 1000000000 | tf_op jit(solution)/shard_map/pallas_call | solution.py:225
  19.7 1.7 %collective-permute-done.4.mirror_ref = bf16[240,128]{1,0:T(8,128)(2,1)S(1)} collective-permute-done((bf16[240,128]{1,0:T(8,128)(2,1)S(1)}, bf16[240,128]{1,0:T(8,128)(2,1)S(1)}, u32[]{:S(2)}, u32[]{:S(2)}) %collective-permute-start.4) | collective-permute-done | bytes 61472 | tf_op jit(solution)/shard_map/ppermute | solution.py:42
  21.5 0.0 copy-done
  21.5 0.9 %shard_map.71 = bf16[450,2048]{1,0:T(8,128)(2,1)} custom-call(bf16[450,2048]{1,0:T(8,128)(2,1)} %shard_map.70.whole_ref, f32[480,128]{1,0:T(8,128)S(1)} %get-tuple-element.21.after_ref.sum_ref, bf16[240,128]{1,0:T(8,128)(2,1)S(1)} %collective-permute-done.4.mirror_ref, s32[1,64]{1,0:T(1,128)S(1)} %bitcast.6), custom_call_target="tpu_custom_call", output_to_operand_aliasing={{}: (0, {})} | custom-call | tf_op jit(solution)/shard_map/pallas_call | solution.py:253
Async XLA Ops:
  0.0 7.0 %collective-permute-start = (s32[3,256]{1,0:T(4,128)}, s32[3,256]{1,0:T(4,128)S(1)}, u32[]{:S(2)}, u32[]{:S(2)}) collective-permute-start(s32[3,256]{1,0:T(4,128)} %refs_4_.1), channel_id=1, source_target_pairs={{0,15},{1,2},{2,1},{3,4},{4,3},{5,6},{6,5},{7,8},{8,7},{9,10},{10,... | collective-permute-start | bytes 9224 | tf_op jit(solution)/shard_map/ppermute | solution.py:42
  5.4 6.4 %collective-permute-start.2 = (s32[3,256]{1,0:T(4,128)}, s32[3,256]{1,0:T(4,128)S(1)}, u32[]{:S(2)}, u32[]{:S(2)}) collective-permute-start(s32[3,256]{1,0:T(4,128)} %refs_4_.1), channel_id=1, source_target_pairs={{0,1},{1,0},{2,3},{3,2},{4,5},{5,4},{6,7},{7,6},{8,9},{9,8},{10,11... | collective-permute-start | bytes 9224 | tf_op jit(solution)/shard_map/ppermute | solution.py:42
  7.4 8.4 %collective-permute-start.1 = (bf16[450,256]{1,0:T(8,128)(2,1)S(1)}, bf16[450,256]{1,0:T(8,128)(2,1)S(1)}, u32[]{:S(2)}, u32[]{:S(2)}) collective-permute-start(bf16[450,256]{1,0:T(8,128)(2,1)S(1)} %shard_map.65.after_ref), channel_id=1, source_target_pairs={{0,15},{1,2},{2,1},{3,4},{4,3},{5,6},{6,5},{7,8},{8,7},{9,10},{10,... | collective-permute-start | bytes 691208 | tf_op jit(solution)/shard_map/ppermute | solution.py:42
  12.5 3.2 %collective-permute-start.3 = (bf16[450,256]{1,0:T(8,128)(2,1)S(1)}, bf16[450,256]{1,0:T(8,128)(2,1)S(1)}, u32[]{:S(2)}, u32[]{:S(2)}) collective-permute-start(bf16[450,256]{1,0:T(8,128)(2,1)S(1)} %get-tuple-element.17.after_ref), channel_id=1, source_target_pairs={{0,1},{1,0},{2,3},{3,2},{4,5},{5,4},{6,7},{7,6},{8,9},{9,8},{10,11... | collective-permute-start | bytes 691208 | tf_op jit(solution)/shard_map/ppermute | solution.py:42
  16.1 5.3 %collective-permute-start.4 = (bf16[240,128]{1,0:T(8,128)(2,1)S(1)}, bf16[240,128]{1,0:T(8,128)(2,1)S(1)}, u32[]{:S(2)}, u32[]{:S(2)}) collective-permute-start(bf16[240,128]{1,0:T(8,128)(2,1)S(1)} %get-tuple-element.22), channel_id=1, source_target_pairs={{0,8},{1,9},{2,10},{3,11},{4,12},{5,13},{6,14},{7,15},{8,0},{9,1},... | collective-permute-start | bytes 184328 | tf_op jit(solution)/shard_map/ppermute | solution.py:42
  17.3 4.2 %copy-start = (s32[64]{0:T(128)S(1)}, s32[64]{0:T(128)}, u32[]{:S(2)}) copy-start(s32[64]{0:T(128)} %param.11) | copy-start | bytes 772

commit v6 on v5

--- a/solution.py
+++ b/solution.py
@@ -1,5 +1,4 @@
 import functools
-import math
 
 import jax
 import jax.numpy as jnp
@@ -10,14 +9,13 @@
 
 LANES = 128
 PACK = 16
-MID_TILES = 12
+MID_TILES = 10
 MIB = 2**20
 FLOPS_PER_MICRO = 10**9
 OPICK = 3
 IPICK = 0
 LOAD = 0
 MID = 30
-REST = 1
 EDGE = 1
 BODY = 1
 VMEM = pl.BlockSpec(memory_space=pltpu.VMEM)
@@ -85,21 +83,23 @@
         w_ref[pl.ds(first + group * PACK, PACK), lanes] = acc
 
 
+def fill_tile(pos_ref, weight_ref, count_ref, w_ref, source, target, near, cap):
+    taken, given = pl.ds(source, LANES), pl.ds(target, LANES)
+    row = row_ids((PACK, LANES)).astype(jnp.int16)
+    pos = pos_ref[:, taken]
+    spread = spread_rows(merged_weights(pos, weight_ref[:, taken], count_ref[:, taken]), jnp.bfloat16)
+    turned = jnp.where(is_even(), pos, pos + cap * (near - 1) - 2 * cap * lax.div(pos, cap))
+    place = [x - row for x in spread_rows(turned, jnp.int16)]
+    fill_piece(w_ref, 0, given, near * cap, place, spread)
+
+
 def fill_tiles(pos_ref, weight_ref, count_ref, w_ref, first, tiles, near, cap):
-    even = is_even()
-    row = row_ids((PACK, LANES)).astype(jnp.int16)
-
     def one_tile(tile, carry):
-        taken = pl.ds(pl.multiple_of((first + tile) * LANES, LANES), LANES)
-        given = pl.ds(pl.multiple_of(tile * LANES, LANES), LANES)
-        pos = pos_ref[:, taken]
-        spread = spread_rows(merged_weights(pos, weight_ref[:, taken], count_ref[:, taken]), jnp.bfloat16)
-        turned = jnp.where(even, pos, pos + cap * (near - 1) - 2 * cap * lax.div(pos, cap))
-        place = [x - row for x in spread_rows(turned, jnp.int16)]
-        fill_piece(w_ref, 0, given, near * cap, place, spread)
+        source, target = pl.multiple_of((first + tile) * LANES, LANES), pl.multiple_of(tile * LANES, LANES)
+        fill_tile(pos_ref, weight_ref, count_ref, w_ref, source, target, near, cap)
         return carry
 
-    lax.fori_loop(0, tiles, one_tile, 0, unroll=math.gcd(tiles, 3))
+    lax.fori_loop(0, tiles, one_tile, 0, unroll=2 - tiles % 2)
 
 
 def load_kernel(*refs):
@@ -180,9 +180,27 @@
     return acc
 
 
-def edge_kernel(outer_ref, own_ref, inner_ref, w_ref, sum_ref, edge_ref):
-    cells, cols, half = w_ref.shape[1], own_ref.shape[0], edge_ref.shape[0]
-    total = mixed((outer_ref, own_ref, inner_ref), w_ref, pl.ds(cells - LANES, LANES))
+def part_kernel(own_ref, inner_ref, w_ref, part_ref):
+    cells, cap = w_ref.shape[1], own_ref.shape[1]
+    last = pl.ds(cells - LANES, LANES)
+    part = jnp.dot(own_ref[...], w_ref[cap : 2 * cap, last], preferred_element_type=jnp.float32)
+    part_ref[...] = part + jnp.dot(inner_ref[...], w_ref[2 * cap : 3 * cap, last], preferred_element_type=jnp.float32)
+
+
+def part_sums(own, inner, dense):
+    return pl.pallas_call(
+        part_kernel,
+        out_shape=jax.ShapeDtypeStruct((own.shape[0], LANES), jnp.float32),
+        in_specs=[VMEM] * 3,
+        out_specs=VMEM,
+        compiler_params=pltpu.CompilerParams(vmem_limit_bytes=16 * MIB),
+        cost_estimate=lasting(EDGE),
+    )(own, inner, dense)
+
+
+def edge_kernel(outer_ref, part_ref, w_ref, sum_ref, edge_ref):
+    cells, cols, half, cap = w_ref.shape[1], part_ref.shape[0], edge_ref.shape[0], outer_ref.shape[1]
+    total = part_ref[...] + jnp.dot(outer_ref[...], w_ref[0:cap, pl.ds(cells - LANES, LANES)], preferred_element_type=jnp.float32)
     tail = cols // 8 * 8
     sum_ref[pl.ds(tail, 2 * half - tail), :] = jnp.zeros((2 * half - tail, LANES), jnp.float32)
     sum_ref[0:cols, :] = total
@@ -191,59 +209,67 @@
     edge_ref[...] = packed.astype(jnp.bfloat16)
 
 
-def edge_sums(outer, own, inner, dense):
-    cols = own.shape[0]
+def edge_sums(outer, part, dense):
+    cols = part.shape[0]
     half = -(-cols // (2 * PACK)) * PACK
     return pl.pallas_call(
         edge_kernel,
         out_shape=(jax.ShapeDtypeStruct((2 * half, LANES), jnp.float32), jax.ShapeDtypeStruct((half, LANES), jnp.bfloat16)),
-        in_specs=[VMEM] * 4,
+        in_specs=[VMEM] * 3,
         out_specs=(VMEM,) * 2,
         compiler_params=pltpu.CompilerParams(vmem_limit_bytes=16 * MIB),
         cost_estimate=lasting(EDGE),
-    )(outer, own, inner, dense)
-
-
-def body_kernel(outer_ref, own_ref, inner_ref, late_ref, early_ref, out_hbm, buffer, sems, *, steps):
-    for i, (start, width) in enumerate(steps):
-        ahead = late_ref.shape[1]
-        w_ref, inside = (late_ref, start) if start < ahead else (early_ref, start - ahead)
-        buffer[:, pl.ds(start, width)] = mixed((outer_ref, own_ref, inner_ref), w_ref, pl.ds(inside, width)).astype(jnp.bfloat16)
-        pltpu.make_async_copy(buffer.at[:, pl.ds(start, width)], out_hbm.at[:, pl.ds(start, width)], sems.at[i]).start()
-    for i, (start, width) in enumerate(steps):
-        pltpu.make_async_copy(buffer.at[:, pl.ds(start, width)], out_hbm.at[:, pl.ds(start, width)], sems.at[i]).wait()
+    )(outer, part, dense)
+
+
+def body_kernel(outer_ref, own_ref, inner_ref, pos_ref, weight_ref, count_ref, mid_ref, after_ref, out_hbm, buffer, rest_ref, sems, *, width):
+    del after_ref
+    parts = (outer_ref, own_ref, inner_ref)
+    near, cap = len(parts), own_ref.shape[1]
+    ahead, cells = rest_ref.shape[1], out_hbm.shape[1]
+    spans = cuts(ahead, cells - LANES, width) + cuts(0, ahead, width)
+    early = len(cuts(ahead, cells - LANES, width))
+    tiles, copies = list(range(0, ahead, LANES)), []
+    for i, (start, taken) in enumerate(spans):
+        w_ref, inside = (rest_ref, start) if start < ahead else (mid_ref, start - ahead)
+        lanes = pl.ds(start, taken)
+        buffer[:, lanes] = mixed(parts, w_ref, pl.ds(inside, taken)).astype(jnp.bfloat16)
+        copies.append(pltpu.make_async_copy(buffer.at[:, lanes], out_hbm.at[:, lanes], sems.at[i]))
+        copies[-1].start()
+        for tile in tiles[len(tiles) * i // early : len(tiles) * (i + 1) // early] if i < early else ():
+            fill_tile(pos_ref, weight_ref, count_ref, rest_ref, tile, tile, near, cap)
+    for copy in copies:
+        copy.wait()
 
 
 def cuts(first, last, width):
     return [(start, min(width, last - start)) for start in range(first, last, width)]
 
 
-def body_sums(outer, own, inner, late_w, early_w):
-    cols, ahead = own.shape[0], late_w.shape[1]
-    cells = ahead + early_w.shape[1]
-    steps = cuts(0, ahead, 4 * LANES) + cuts(ahead, cells - LANES, 4 * LANES)
-    return pl.pallas_call(
-        functools.partial(body_kernel, steps=steps),
+def body_sums(outer, own, inner, pos, weight, count, mid_w, after):
+    cols, width = own.shape[0], 2 * LANES
+    cells, kept = pos.shape[1], pos.shape[1] - mid_w.shape[1]
+    steps = len(cuts(kept, cells - LANES, width)) + len(cuts(0, kept, width))
+    return pl.pallas_call(
+        functools.partial(body_kernel, width=width),
         out_shape=jax.ShapeDtypeStruct((cols, cells), jnp.bfloat16),
-        in_specs=[VMEM] * 5,
+        in_specs=[VMEM] * 7 + [ANY],
         out_specs=HBM,
-        scratch_shapes=[pltpu.VMEM((cols, cells), jnp.bfloat16), pltpu.SemaphoreType.DMA((len(steps),))],
+        scratch_shapes=[pltpu.VMEM((cols, cells), jnp.bfloat16), pltpu.VMEM((mid_w.shape[0], kept), jnp.bfloat16), pltpu.SemaphoreType.DMA((steps,))],
         compiler_params=pltpu.CompilerParams(vmem_limit_bytes=24 * MIB),
         cost_estimate=lasting(BODY),
-    )(outer, own, inner, late_w, early_w)
+    )(outer, own, inner, pos, weight, count, mid_w, after)
 
 
 def fold_kernel(whole_ref, sum_ref, mirror_ref, src_ref, out_ref):
     del whole_ref
     cols, half, fold = out_ref.shape[0], mirror_ref.shape[0], src_ref.shape[1]
     unused = jnp.full((1, LANES - fold), -1, jnp.int32)
-    others = []
-    for shift in (0, LANES // 2):
-        source = jnp.concatenate([unused, src_ref[...] + shift], axis=1)
-        hit = row_ids((LANES, LANES)) == source
-        onehot = jnp.where(hit, jnp.float32(1.0), jnp.float32(0.0)).astype(jnp.bfloat16)
-        others.append(jnp.dot(mirror_ref[...], onehot, preferred_element_type=jnp.float32))
-    other = jnp.concatenate(others, axis=0)[0:cols]
+    sources = [jnp.concatenate([unused, src_ref[...] + shift], axis=1) for shift in (0, LANES // 2)]
+    hit = row_ids((LANES, 2 * LANES)) == jnp.concatenate(sources, axis=1)
+    onehot = jnp.where(hit, jnp.float32(1.0), jnp.float32(0.0)).astype(jnp.bfloat16)
+    both = jnp.dot(mirror_ref[...], onehot, preferred_element_type=jnp.float32)
+    other = jnp.concatenate([both[:, :LANES], both[:, LANES:]], axis=0)[0:cols]
     out_ref[...] = (sum_ref[0:cols, :] + other).astype(jnp.bfloat16)
 
 
@@ -273,10 +299,9 @@
     for_inner, own = picked(inner_pick_kernel, 2, IPICK, grad, asked_inner, own_asks, for_outer)
     inner = sent(for_inner, inner_place)
     mid_w = dense_weights(for_inner, pos, weight, count, near, cap, rest, MID_TILES, MID)
-    sums, edge = edge_sums(outer, own, inner, mid_w)
+    sums, edge = edge_sums(outer, part_sums(own, inner, mid_w), mid_w)
     mirror = sent(edge, half_place)
-    rest_w = dense_weights(sums, pos, weight, count, near, cap, 0, rest, REST)
-    whole = body_sums(outer, own, inner, rest_w, mid_w)
+    whole = body_sums(outer, own, inner, pos, weight, count, mid_w, sums)
     return folded(whole, sums, mirror, fold_src[None, :]).T
 
 

time: 22.6 us -> 22.3 us (0.987)
  waiting for transfers between devices: 2.05 us -> 1.65 us
    pallas_call x1 -> x2, Pallas kernels: 2.41 us -> 4.23 us  [the longest x1 3.96 us: body_sums(): pl.pallas_call(functools.partial(body_kernel, width=width), out_shape=jax...]
    pallas_call x2 -> x1, Pallas kernels: 4.16 us -> 2.59 us  [dense_weights(): pl.pallas_call(functools.partial(weights_kernel, first=first, near=near,...]
    ppermute x5, waiting for transfers between devices: 2.05 us -> 1.65 us  [sent(): lax.ppermute(block, 'lon', [(i, target(i, count)) for i in range(count)])]
  transfers between devices with their start and end apart: 5 -> 5, of which waited for: 2 -> 3; matrix products, arithmetic and copies ran while one was open for 0% -> 0% of each run, Pallas kernels for 40% -> 42%
where the time goes in v6:
time: 22.3 us; the launch traced here: 22.1 us
  Pallas kernels  10.4 us (47%)
  starting transfers between devices  10.1 us (45%)
  waiting for transfers between devices  1.65 us (7%)
    ppermute x5, starting transfers between devices, sent(): lax.ppermute(block, 'lon', [(i, target(i, count)) for i in range(count)])  10.1 us
    pallas_call x1, Pallas kernels, body_sums(): pl.pallas_call(functools.partial(body_kernel, width=width), out_shape=jax...  3.96 us
    pallas_call x1, Pallas kernels, dense_weights(): pl.pallas_call(functools.partial(weights_kernel, first=first, near=near,...  2.59 us
    ppermute x5, waiting for transfers between devices, sent(): lax.ppermute(block, 'lon', [(i, target(i, count)) for i in range(count)])  1.65 us
    pallas_call x1, Pallas kernels, loaded(): pl.pallas_call(load_kernel, out_shape=tuple((jax.ShapeDtypeStruct(x.shape...  1.27 us
    pallas_call x2, Pallas kernels, picked(): pl.pallas_call(kernel, out_shape=(shape,) * outputs, in_specs=[VMEM] * mi...  1.08 us
    pallas_call x1, Pallas kernels, folded(): pl.pallas_call(fold_kernel, grid=(1,), out_shape=jax.ShapeDtypeStruct((co...  0.9 us
  transfers between devices with their start and end apart: 5, of which 3 were waited for; matrix products, arithmetic and copies ran while one was open for 0% of the time, Pallas kernels for 42%

profile of v6, /device:TPU:0, one launch (start us, length us, event | category | flops | bytes accessed | tf_op | source)
XLA Modules:
  0.0 22.1 jit_solution(16479627649667861708)
XLA Ops:
  0.0 5.4 %collective-permute-start = (s32[3,256]{1,0:T(4,128)}, s32[3,256]{1,0:T(4,128)S(1)}, u32[]{:S(2)}, u32[]{:S(2)}) collective-permute-start(s32[3,256]{1,0:T(4,128)} %refs_4_.1), channel_id=1, source_target_pairs={{0,15},{1,2},{2,1},{3,4},{4,3},{5,6},{6,5},{7,8},{8,7},{9,10},{10,... | collective-permute-start | bytes 9224 | tf_op jit(solution)/shard_map/ppermute | solution.py:40
  5.4 0.0 collective-permute-start.2
  5.4 1.3 %shard_map.64 = (bf16[450,1024]{1,0:T(8,128)(2,1)S(1)}, s32[16,2048]{1,0:T(8,128)S(1)}, f32[16,2048]{1,0:T(8,128)S(1)}, s32[1,2048]{1,0:T(1,128)S(1)}, s32[3,256]{1,0:T(4,128)S(1)}) custom-call(bf16[450,1024]{1,0:T(8,128)(2,1)} %bitcast.7, s32[16,2048]{1,0:T(8,128)} %bitcast.8, f32[16,2048]{1,0:T(8,128)} %bitcast.9, s32[1,2048]{1,0:T(1,128)} %bitcast.10, ...), custom_call_target="tpu_custom_call" | custom-call | tf_op jit(solution)/shard_map/pallas_call | solution.py:115
  6.7 0.3 %collective-permute-done.asked_ref = s32[3,256]{1,0:T(4,128)S(1)} collective-permute-done((s32[3,256]{1,0:T(4,128)}, s32[3,256]{1,0:T(4,128)S(1)}, u32[]{:S(2)}, u32[]{:S(2)}) %collective-permute-start) | collective-permute-done | bytes 3104 | tf_op jit(solution)/shard_map/ppermute | solution.py:40
  7.0 0.4 %shard_map.65.after_ref = bf16[450,256]{1,0:T(8,128)(2,1)S(1)} custom-call(bf16[450,1024]{1,0:T(8,128)(2,1)S(1)} %get-tuple-element.14.grad_ref, s32[3,256]{1,0:T(4,128)S(1)} %collective-permute-done.asked_ref), custom_call_target="tpu_custom_call" | custom-call | flops 3000000000 | tf_op jit(solution)/shard_map/pallas_call | solution.py:164
  7.4 4.5 %collective-permute-start.1 = (bf16[450,256]{1,0:T(8,128)(2,1)S(1)}, bf16[450,256]{1,0:T(8,128)(2,1)S(1)}, u32[]{:S(2)}, u32[]{:S(2)}) collective-permute-start(bf16[450,256]{1,0:T(8,128)(2,1)S(1)} %shard_map.65.after_ref), channel_id=1, source_target_pairs={{0,15},{1,2},{2,1},{3,4},{4,3},{5,6},{6,5},{7,8},{8,7},{9,10},{10,... | collective-permute-start | bytes 691208 | tf_op jit(solution)/shard_map/ppermute | solution.py:40
  11.9 0.0 collective-permute-done.2.asked_ref
  11.9 0.7 %shard_map.66 = (bf16[450,256]{1,0:T(8,128)(2,1)S(1)}, bf16[450,256]{1,0:T(8,128)(2,1)S(1)}) custom-call(bf16[450,1024]{1,0:T(8,128)(2,1)S(1)} %get-tuple-element.14.grad_ref, s32[3,256]{1,0:T(4,128)S(1)} %collective-permute-done.2.asked_ref, s32[3,256]{1,0:T(4,128)S(1)} %get-tuple-element.15.own_ref, bf16[450,256]{1,0:T(8,128)(2,1)S(1)} %shard_map.65.after_ref), custom_call_target="tpu_custom_call" | custom-call | tf_op jit(solution)/shard_map/pallas_call | solution.py:164
  12.5 0.1 collective-permute-start.3
  12.6 2.6 %shard_map.67.w_ref.mid_ref = bf16[768,1280]{1,0:T(8,128)(2,1)S(1)} custom-call(bf16[450,256]{1,0:T(8,128)(2,1)S(1)} %get-tuple-element.17.after_ref, s32[16,2048]{1,0:T(8,128)S(1)} %get-tuple-element.18.pos_ref, f32[16,2048]{1,0:T(8,128)S(1)} %get-tuple-element.19.weight_ref, s32[1,2048]{1,0:T(1,128)S(1)} %get-tuple-element.20.count_ref), custom_call_target="tpu_custom_call" | custom-call | flops 30000001024 | tf_op jit(solution)/shard_map/pallas_call | solution.py:132
  15.2 0.0 collective-permute-done.3.inner_ref
  15.2 0.3 %shard_map.68.part_ref = f32[450,128]{1,0:T(8,128)S(1)} custom-call(bf16[450,256]{1,0:T(8,128)(2,1)S(1)} %get-tuple-element.16.own_ref, bf16[450,256]{1,0:T(8,128)(2,1)S(1)} %collective-permute-done.3.inner_ref, bf16[768,1280]{1,0:T(8,128)(2,1)S(1)} %shard_map.67.w_ref.mid_ref), custom_call_target="tpu_custom_call" | custom-call | flops 1000000000 | tf_op jit(solution)/shard_map/pallas_call | solution.py:191
  15.5 0.3 %collective-permute-done.1.outer_ref = bf16[450,256]{1,0:T(8,128)(2,1)S(1)} collective-permute-done((bf16[450,256]{1,0:T(8,128)(2,1)S(1)}, bf16[450,256]{1,0:T(8,128)(2,1)S(1)}, u32[]{:S(2)}, u32[]{:S(2)}) %collective-permute-start.1) | collective-permute-done | bytes 230432 | tf_op jit(solution)/shard_map/ppermute | solution.py:40
  15.8 0.3 %shard_map.69 = (f32[480,128]{1,0:T(8,128)S(1)}, bf16[240,128]{1,0:T(8,128)(2,1)S(1)}) custom-call(bf16[450,256]{1,0:T(8,128)(2,1)S(1)} %collective-permute-done.1.outer_ref, f32[450,128]{1,0:T(8,128)S(1)} %shard_map.68.part_ref, bf16[768,1280]{1,0:T(8,128)(2,1)S(1)} %shard_map.67.w_ref.mid_ref), custom_call_target="tpu_custom_call" | custom-call | flops 1000000000 | tf_op jit(solution)/shard_map/pallas_call | solution.py:215
  16.1 0.1 collective-permute-start.4
  16.1 0.0 copy-start
  16.2 4.0 %shard_map.70.whole_ref = bf16[450,2048]{1,0:T(8,128)(2,1)} custom-call(bf16[450,256]{1,0:T(8,128)(2,1)S(1)} %collective-permute-done.1.outer_ref, bf16[450,256]{1,0:T(8,128)(2,1)S(1)} %get-tuple-element.16.own_ref, bf16[450,256]{1,0:T(8,128)(2,1)S(1)} %collective-permute-done.3.inner_ref, s32[16,2048]{1,0:T(8,128)S(1)} %get-tuple-element.18.pos_ref, ...), custom_call_target="tpu_custom_call" | custom-call | flops 1000000000 | tf_op jit(solution)/shard_map/pallas_call | solution.py:253
  20.1 1.1 %collective-permute-done.4.mirror_ref = bf16[240,128]{1,0:T(8,128)(2,1)S(1)} collective-permute-done((bf16[240,128]{1,0:T(8,128)(2,1)S(1)}, bf16[240,128]{1,0:T(8,128)(2,1)S(1)}, u32[]{:S(2)}, u32[]{:S(2)}) %collective-permute-start.4) | collective-permute-done | bytes 61472 | tf_op jit(solution)/shard_map/ppermute | solution.py:40
  21.2 0.0 copy-done
  21.2 0.9 %shard_map.71 = bf16[450,2048]{1,0:T(8,128)(2,1)} custom-call(bf16[450,2048]{1,0:T(8,128)(2,1)} %shard_map.70.whole_ref, f32[480,128]{1,0:T(8,128)S(1)} %get-tuple-element.21.after_ref.sum_ref, bf16[240,128]{1,0:T(8,128)(2,1)S(1)} %collective-permute-done.4.mirror_ref, s32[1,64]{1,0:T(1,128)S(1)} %bitcast.6), custom_call_target="tpu_custom_call", output_to_operand_aliasing={{}: (0, {})} | custom-call | tf_op jit(solution)/shard_map/pallas_call | solution.py:279
Async XLA Ops:
  0.0 7.0 %collective-permute-start = (s32[3,256]{1,0:T(4,128)}, s32[3,256]{1,0:T(4,128)S(1)}, u32[]{:S(2)}, u32[]{:S(2)}) collective-permute-start(s32[3,256]{1,0:T(4,128)} %refs_4_.1), channel_id=1, source_target_pairs={{0,15},{1,2},{2,1},{3,4},{4,3},{5,6},{6,5},{7,8},{8,7},{9,10},{10,... | collective-permute-start | bytes 9224 | tf_op jit(solution)/shard_map/ppermute | solution.py:40
  5.4 6.4 %collective-permute-start.2 = (s32[3,256]{1,0:T(4,128)}, s32[3,256]{1,0:T(4,128)S(1)}, u32[]{:S(2)}, u32[]{:S(2)}) collective-permute-start(s32[3,256]{1,0:T(4,128)} %refs_4_.1), channel_id=1, source_target_pairs={{0,1},{1,0},{2,3},{3,2},{4,5},{5,4},{6,7},{7,6},{8,9},{9,8},{10,11... | collective-permute-start | bytes 9224 | tf_op jit(solution)/shard_map/ppermute | solution.py:40
  7.4 8.4 %collective-permute-start.1 = (bf16[450,256]{1,0:T(8,128)(2,1)S(1)}, bf16[450,256]{1,0:T(8,128)(2,1)S(1)}, u32[]{:S(2)}, u32[]{:S(2)}) collective-permute-start(bf16[450,256]{1,0:T(8,128)(2,1)S(1)} %shard_map.65.after_ref), channel_id=1, source_target_pairs={{0,15},{1,2},{2,1},{3,4},{4,3},{5,6},{6,5},{7,8},{8,7},{9,10},{10,... | collective-permute-start | bytes 691208 | tf_op jit(solution)/shard_map/ppermute | solution.py:40
  12.5 2.7 %collective-permute-start.3 = (bf16[450,256]{1,0:T(8,128)(2,1)S(1)}, bf16[450,256]{1,0:T(8,128)(2,1)S(1)}, u32[]{:S(2)}, u32[]{:S(2)}) collective-permute-start(bf16[450,256]{1,0:T(8,128)(2,1)S(1)} %get-tuple-element.17.after_ref), channel_id=1, source_target_pairs={{0,1},{1,0},{2,3},{3,2},{4,5},{5,4},{6,7},{7,6},{8,9},{9,8},{10,11... | collective-permute-start | bytes 691208 | tf_op jit(solution)/shard_map/ppermute | solution.py:40
  16.1 5.2 %collective-permute-start.4 = (bf16[240,128]{1,0:T(8,128)(2,1)S(1)}, bf16[240,128]{1,0:T(8,128)(2,1)S(1)}, u32[]{:S(2)}, u32[]{:S(2)}) collective-permute-start(bf16[240,128]{1,0:T(8,128)(2,1)S(1)} %get-tuple-element.22), channel_id=1, source_target_pairs={{0,8},{1,9},{2,10},{3,11},{4,12},{5,13},{6,14},{7,15},{8,0},{9,1},... | collective-permute-start | bytes 184328 | tf_op jit(solution)/shard_map/ppermute | solution.py:40
  16.1 5.1 %copy-start = (s32[64]{0:T(128)S(1)}, s32[64]{0:T(128)}, u32[]{:S(2)}) copy-start(s32[64]{0:T(128)} %param.11) | copy-start | bytes 772

commit v7 on v6

--- a/solution.py
+++ b/solution.py
@@ -247,7 +247,7 @@
 
 
 def body_sums(outer, own, inner, pos, weight, count, mid_w, after):
-    cols, width = own.shape[0], 2 * LANES
+    cols, width = own.shape[0], 4 * LANES
     cells, kept = pos.shape[1], pos.shape[1] - mid_w.shape[1]
     steps = len(cuts(kept, cells - LANES, width)) + len(cuts(0, kept, width))
     return pl.pallas_call(

time: 22.3 us -> 22.3 us (level)
  transfers between devices with their start and end apart: 5 -> 5, of which waited for: 3 -> 3; matrix products, arithmetic and copies ran while one was open for 0% -> 0% of each run, Pallas kernels for 42% -> 41%
where the time goes in v7:
time: 22.3 us; the launch traced here: 22.1 us
  Pallas kernels  10.3 us (46%)
  starting transfers between devices  10.1 us (45%)
  waiting for transfers between devices  1.74 us (8%)
    ppermute x5, starting transfers between devices, sent(): lax.ppermute(block, 'lon', [(i, target(i, count)) for i in range(count)])  10.1 us
    pallas_call x1, Pallas kernels, body_sums(): pl.pallas_call(functools.partial(body_kernel, width=width), out_shape=jax...  3.86 us
    pallas_call x1, Pallas kernels, dense_weights(): pl.pallas_call(functools.partial(weights_kernel, first=first, near=near,...  2.59 us
    ppermute x5, waiting for transfers between devices, sent(): lax.ppermute(block, 'lon', [(i, target(i, count)) for i in range(count)])  1.74 us
    pallas_call x1, Pallas kernels, loaded(): pl.pallas_call(load_kernel, out_shape=tuple((jax.ShapeDtypeStruct(x.shape...  1.27 us
    pallas_call x2, Pallas kernels, picked(): pl.pallas_call(kernel, out_shape=(shape,) * outputs, in_specs=[VMEM] * mi...  1.08 us
    pallas_call x1, Pallas kernels, folded(): pl.pallas_call(fold_kernel, grid=(1,), out_shape=jax.ShapeDtypeStruct((co...  0.9 us
  transfers between devices with their start and end apart: 5, of which 3 were waited for; matrix products, arithmetic and copies ran while one was open for 0% of the time, Pallas kernels for 41%

profile of v7, /device:TPU:0, one launch (start us, length us, event | category | flops | bytes accessed | tf_op | source)
XLA Modules:
  0.0 22.1 jit_solution(16946548295263392709)
XLA Ops:
  0.0 5.4 %collective-permute-start = (s32[3,256]{1,0:T(4,128)}, s32[3,256]{1,0:T(4,128)S(1)}, u32[]{:S(2)}, u32[]{:S(2)}) collective-permute-start(s32[3,256]{1,0:T(4,128)} %refs_4_.1), channel_id=1, source_target_pairs={{0,15},{1,2},{2,1},{3,4},{4,3},{5,6},{6,5},{7,8},{8,7},{9,10},{10,... | collective-permute-start | bytes 9224 | tf_op jit(solution)/shard_map/ppermute | solution.py:40
  5.4 0.0 collective-permute-start.2
  5.4 1.3 %shard_map.64 = (bf16[450,1024]{1,0:T(8,128)(2,1)S(1)}, s32[16,2048]{1,0:T(8,128)S(1)}, f32[16,2048]{1,0:T(8,128)S(1)}, s32[1,2048]{1,0:T(1,128)S(1)}, s32[3,256]{1,0:T(4,128)S(1)}) custom-call(bf16[450,1024]{1,0:T(8,128)(2,1)} %bitcast.7, s32[16,2048]{1,0:T(8,128)} %bitcast.8, f32[16,2048]{1,0:T(8,128)} %bitcast.9, s32[1,2048]{1,0:T(1,128)} %bitcast.10, ...), custom_call_target="tpu_custom_call" | custom-call | tf_op jit(solution)/shard_map/pallas_call | solution.py:115
  6.7 0.3 %collective-permute-done.asked_ref = s32[3,256]{1,0:T(4,128)S(1)} collective-permute-done((s32[3,256]{1,0:T(4,128)}, s32[3,256]{1,0:T(4,128)S(1)}, u32[]{:S(2)}, u32[]{:S(2)}) %collective-permute-start) | collective-permute-done | bytes 3104 | tf_op jit(solution)/shard_map/ppermute | solution.py:40
  7.0 0.4 %shard_map.65.after_ref = bf16[450,256]{1,0:T(8,128)(2,1)S(1)} custom-call(bf16[450,1024]{1,0:T(8,128)(2,1)S(1)} %get-tuple-element.14.grad_ref, s32[3,256]{1,0:T(4,128)S(1)} %collective-permute-done.asked_ref), custom_call_target="tpu_custom_call" | custom-call | flops 3000000000 | tf_op jit(solution)/shard_map/pallas_call | solution.py:164
  7.4 4.5 %collective-permute-start.1 = (bf16[450,256]{1,0:T(8,128)(2,1)S(1)}, bf16[450,256]{1,0:T(8,128)(2,1)S(1)}, u32[]{:S(2)}, u32[]{:S(2)}) collective-permute-start(bf16[450,256]{1,0:T(8,128)(2,1)S(1)} %shard_map.65.after_ref), channel_id=1, source_target_pairs={{0,15},{1,2},{2,1},{3,4},{4,3},{5,6},{6,5},{7,8},{8,7},{9,10},{10,... | collective-permute-start | bytes 691208 | tf_op jit(solution)/shard_map/ppermute | solution.py:40
  11.9 0.0 collective-permute-done.2.asked_ref
  11.9 0.7 %shard_map.66 = (bf16[450,256]{1,0:T(8,128)(2,1)S(1)}, bf16[450,256]{1,0:T(8,128)(2,1)S(1)}) custom-call(bf16[450,1024]{1,0:T(8,128)(2,1)S(1)} %get-tuple-element.14.grad_ref, s32[3,256]{1,0:T(4,128)S(1)} %collective-permute-done.2.asked_ref, s32[3,256]{1,0:T(4,128)S(1)} %get-tuple-element.15.own_ref, bf16[450,256]{1,0:T(8,128)(2,1)S(1)} %shard_map.65.after_ref), custom_call_target="tpu_custom_call" | custom-call | tf_op jit(solution)/shard_map/pallas_call | solution.py:164
  12.5 0.1 collective-permute-start.3
  12.6 2.6 %shard_map.67.w_ref.mid_ref = bf16[768,1280]{1,0:T(8,128)(2,1)S(1)} custom-call(bf16[450,256]{1,0:T(8,128)(2,1)S(1)} %get-tuple-element.17.after_ref, s32[16,2048]{1,0:T(8,128)S(1)} %get-tuple-element.18.pos_ref, f32[16,2048]{1,0:T(8,128)S(1)} %get-tuple-element.19.weight_ref, s32[1,2048]{1,0:T(1,128)S(1)} %get-tuple-element.20.count_ref), custom_call_target="tpu_custom_call" | custom-call | flops 30000001024 | tf_op jit(solution)/shard_map/pallas_call | solution.py:132
  15.2 0.0 collective-permute-done.3.inner_ref
  15.2 0.3 %shard_map.68.part_ref = f32[450,128]{1,0:T(8,128)S(1)} custom-call(bf16[450,256]{1,0:T(8,128)(2,1)S(1)} %get-tuple-element.16.own_ref, bf16[450,256]{1,0:T(8,128)(2,1)S(1)} %collective-permute-done.3.inner_ref, bf16[768,1280]{1,0:T(8,128)(2,1)S(1)} %shard_map.67.w_ref.mid_ref), custom_call_target="tpu_custom_call" | custom-call | flops 1000000000 | tf_op jit(solution)/shard_map/pallas_call | solution.py:191
  15.5 0.3 %collective-permute-done.1.outer_ref = bf16[450,256]{1,0:T(8,128)(2,1)S(1)} collective-permute-done((bf16[450,256]{1,0:T(8,128)(2,1)S(1)}, bf16[450,256]{1,0:T(8,128)(2,1)S(1)}, u32[]{:S(2)}, u32[]{:S(2)}) %collective-permute-start.1) | collective-permute-done | bytes 230432 | tf_op jit(solution)/shard_map/ppermute | solution.py:40
  15.8 0.3 %shard_map.69 = (f32[480,128]{1,0:T(8,128)S(1)}, bf16[240,128]{1,0:T(8,128)(2,1)S(1)}) custom-call(bf16[450,256]{1,0:T(8,128)(2,1)S(1)} %collective-permute-done.1.outer_ref, f32[450,128]{1,0:T(8,128)S(1)} %shard_map.68.part_ref, bf16[768,1280]{1,0:T(8,128)(2,1)S(1)} %shard_map.67.w_ref.mid_ref), custom_call_target="tpu_custom_call" | custom-call | flops 1000000000 | tf_op jit(solution)/shard_map/pallas_call | solution.py:215
  16.1 0.1 collective-permute-start.4
  16.1 0.0 copy-start
  16.2 3.9 %shard_map.70.whole_ref = bf16[450,2048]{1,0:T(8,128)(2,1)} custom-call(bf16[450,256]{1,0:T(8,128)(2,1)S(1)} %collective-permute-done.1.outer_ref, bf16[450,256]{1,0:T(8,128)(2,1)S(1)} %get-tuple-element.16.own_ref, bf16[450,256]{1,0:T(8,128)(2,1)S(1)} %collective-permute-done.3.inner_ref, s32[16,2048]{1,0:T(8,128)S(1)} %get-tuple-element.18.pos_ref, ...), custom_call_target="tpu_custom_call" | custom-call | flops 1000000000 | tf_op jit(solution)/shard_map/pallas_call | solution.py:253
  20.0 1.2 %collective-permute-done.4.mirror_ref = bf16[240,128]{1,0:T(8,128)(2,1)S(1)} collective-permute-done((bf16[240,128]{1,0:T(8,128)(2,1)S(1)}, bf16[240,128]{1,0:T(8,128)(2,1)S(1)}, u32[]{:S(2)}, u32[]{:S(2)}) %collective-permute-start.4) | collective-permute-done | bytes 61472 | tf_op jit(solution)/shard_map/ppermute | solution.py:40
  21.2 0.0 copy-done
  21.2 0.9 %shard_map.71 = bf16[450,2048]{1,0:T(8,128)(2,1)} custom-call(bf16[450,2048]{1,0:T(8,128)(2,1)} %shard_map.70.whole_ref, f32[480,128]{1,0:T(8,128)S(1)} %get-tuple-element.21.after_ref.sum_ref, bf16[240,128]{1,0:T(8,128)(2,1)S(1)} %collective-permute-done.4.mirror_ref, s32[1,64]{1,0:T(1,128)S(1)} %bitcast.6), custom_call_target="tpu_custom_call", output_to_operand_aliasing={{}: (0, {})} | custom-call | tf_op jit(solution)/shard_map/pallas_call | solution.py:279
Async XLA Ops:
  0.0 7.0 %collective-permute-start = (s32[3,256]{1,0:T(4,128)}, s32[3,256]{1,0:T(4,128)S(1)}, u32[]{:S(2)}, u32[]{:S(2)}) collective-permute-start(s32[3,256]{1,0:T(4,128)} %refs_4_.1), channel_id=1, source_target_pairs={{0,15},{1,2},{2,1},{3,4},{4,3},{5,6},{6,5},{7,8},{8,7},{9,10},{10,... | collective-permute-start | bytes 9224 | tf_op jit(solution)/shard_map/ppermute | solution.py:40
  5.4 6.4 %collective-permute-start.2 = (s32[3,256]{1,0:T(4,128)}, s32[3,256]{1,0:T(4,128)S(1)}, u32[]{:S(2)}, u32[]{:S(2)}) collective-permute-start(s32[3,256]{1,0:T(4,128)} %refs_4_.1), channel_id=1, source_target_pairs={{0,1},{1,0},{2,3},{3,2},{4,5},{5,4},{6,7},{7,6},{8,9},{9,8},{10,11... | collective-permute-start | bytes 9224 | tf_op jit(solution)/shard_map/ppermute | solution.py:40
  7.4 8.4 %collective-permute-start.1 = (bf16[450,256]{1,0:T(8,128)(2,1)S(1)}, bf16[450,256]{1,0:T(8,128)(2,1)S(1)}, u32[]{:S(2)}, u32[]{:S(2)}) collective-permute-start(bf16[450,256]{1,0:T(8,128)(2,1)S(1)} %shard_map.65.after_ref), channel_id=1, source_target_pairs={{0,15},{1,2},{2,1},{3,4},{4,3},{5,6},{6,5},{7,8},{8,7},{9,10},{10,... | collective-permute-start | bytes 691208 | tf_op jit(solution)/shard_map/ppermute | solution.py:40
  12.5 2.7 %collective-permute-start.3 = (bf16[450,256]{1,0:T(8,128)(2,1)S(1)}, bf16[450,256]{1,0:T(8,128)(2,1)S(1)}, u32[]{:S(2)}, u32[]{:S(2)}) collective-permute-start(bf16[450,256]{1,0:T(8,128)(2,1)S(1)} %get-tuple-element.17.after_ref), channel_id=1, source_target_pairs={{0,1},{1,0},{2,3},{3,2},{4,5},{5,4},{6,7},{7,6},{8,9},{9,8},{10,11... | collective-permute-start | bytes 691208 | tf_op jit(solution)/shard_map/ppermute | solution.py:40
  16.1 5.2 %collective-permute-start.4 = (bf16[240,128]{1,0:T(8,128)(2,1)S(1)}, bf16[240,128]{1,0:T(8,128)(2,1)S(1)}, u32[]{:S(2)}, u32[]{:S(2)}) collective-permute-start(bf16[240,128]{1,0:T(8,128)(2,1)S(1)} %get-tuple-element.22), channel_id=1, source_target_pairs={{0,8},{1,9},{2,10},{3,11},{4,12},{5,13},{6,14},{7,15},{8,0},{9,1},... | collective-permute-start | bytes 184328 | tf_op jit(solution)/shard_map/ppermute | solution.py:40
  16.1 5.1 %copy-start = (s32[64]{0:T(128)S(1)}, s32[64]{0:T(128)}, u32[]{:S(2)}) copy-start(s32[64]{0:T(128)} %param.11) | copy-start | bytes 772

commit v8 on v7

--- a/solution.py
+++ b/solution.py
@@ -201,11 +201,10 @@
 def edge_kernel(outer_ref, part_ref, w_ref, sum_ref, edge_ref):
     cells, cols, half, cap = w_ref.shape[1], part_ref.shape[0], edge_ref.shape[0], outer_ref.shape[1]
     total = part_ref[...] + jnp.dot(outer_ref[...], w_ref[0:cap, pl.ds(cells - LANES, LANES)], preferred_element_type=jnp.float32)
-    tail = cols // 8 * 8
-    sum_ref[pl.ds(tail, 2 * half - tail), :] = jnp.zeros((2 * half - tail, LANES), jnp.float32)
-    sum_ref[0:cols, :] = total
-    upper = pltpu.roll(sum_ref[0:half, :], LANES // 2, 1)
-    packed = jnp.where(lane_ids((half, LANES)) < LANES // 2, upper, sum_ref[half : 2 * half, :])
+    sum_ref[...] = total
+    upper = pltpu.roll(total[0:half], LANES // 2, 1)
+    lower = jnp.concatenate([total[half:cols], jnp.zeros((2 * half - cols, LANES), jnp.float32)], axis=0)
+    packed = jnp.where(lane_ids((half, LANES)) < LANES // 2, upper, lower)
     edge_ref[...] = packed.astype(jnp.bfloat16)
 
 
@@ -214,7 +213,7 @@
     half = -(-cols // (2 * PACK)) * PACK
     return pl.pallas_call(
         edge_kernel,
-        out_shape=(jax.ShapeDtypeStruct((2 * half, LANES), jnp.float32), jax.ShapeDtypeStruct((half, LANES), jnp.bfloat16)),
+        out_shape=(jax.ShapeDtypeStruct((cols, LANES), jnp.float32), jax.ShapeDtypeStruct((half, LANES), jnp.bfloat16)),
         in_specs=[VMEM] * 3,
         out_specs=(VMEM,) * 2,
         compiler_params=pltpu.CompilerParams(vmem_limit_bytes=16 * MIB),
@@ -270,7 +269,7 @@
     onehot = jnp.where(hit, jnp.float32(1.0), jnp.float32(0.0)).astype(jnp.bfloat16)
     both = jnp.dot(mirror_ref[...], onehot, preferred_element_type=jnp.float32)
     other = jnp.concatenate([both[:, :LANES], both[:, LANES:]], axis=0)[0:cols]
-    out_ref[...] = (sum_ref[0:cols, :] + other).astype(jnp.bfloat16)
+    out_ref[...] = (sum_ref[...] + other).astype(jnp.bfloat16)
 
 
 def folded(whole, sums, mirror, fold_src):

time: 22.3 us -> 22.3 us (level)
  no operation moved by 1% of the time
where the time goes in v8:
time: 22.3 us; the launch traced here: 22.1 us
  Pallas kernels  10.3 us (46%)
  starting transfers between devices  10.1 us (45%)
  waiting for transfers between devices  1.74 us (8%)
    ppermute x5, starting transfers between devices, sent(): lax.ppermute(block, 'lon', [(i, target(i, count)) for i in range(count)])  10.1 us
    pallas_call x1, Pallas kernels, body_sums(): pl.pallas_call(functools.partial(body_kernel, width=width), out_shape=jax...  3.87 us
    pallas_call x1, Pallas kernels, dense_weights(): pl.pallas_call(functools.partial(weights_kernel, first=first, near=near,...  2.59 us
    ppermute x5, waiting for transfers between devices, sent(): lax.ppermute(block, 'lon', [(i, target(i, count)) for i in range(count)])  1.74 us
    pallas_call x1, Pallas kernels, loaded(): pl.pallas_call(load_kernel, out_shape=tuple((jax.ShapeDtypeStruct(x.shape...  1.27 us
    pallas_call x2, Pallas kernels, picked(): pl.pallas_call(kernel, out_shape=(shape,) * outputs, in_specs=[VMEM] * mi...  1.08 us
    pallas_call x1, Pallas kernels, folded(): pl.pallas_call(fold_kernel, grid=(1,), out_shape=jax.ShapeDtypeStruct((co...  0.9 us
  transfers between devices with their start and end apart: 5, of which 3 were waited for; matrix products, arithmetic and copies ran while one was open for 0% of the time, Pallas kernels for 41%

profile of v8, /device:TPU:0, one launch (start us, length us, event | category | flops | bytes accessed | tf_op | source)
XLA Modules:
  0.0 22.1 jit_solution(11759533947592631896)
XLA Ops:
  0.0 5.4 %collective-permute-start = (s32[3,256]{1,0:T(4,128)}, s32[3,256]{1,0:T(4,128)S(1)}, u32[]{:S(2)}, u32[]{:S(2)}) collective-permute-start(s32[3,256]{1,0:T(4,128)} %refs_4_.1), channel_id=1, source_target_pairs={{0,15},{1,2},{2,1},{3,4},{4,3},{5,6},{6,5},{7,8},{8,7},{9,10},{10,... | collective-permute-start | bytes 9224 | tf_op jit(solution)/shard_map/ppermute | solution.py:40
  5.4 0.0 collective-permute-start.2
  5.4 1.3 %shard_map.64 = (bf16[450,1024]{1,0:T(8,128)(2,1)S(1)}, s32[16,2048]{1,0:T(8,128)S(1)}, f32[16,2048]{1,0:T(8,128)S(1)}, s32[1,2048]{1,0:T(1,128)S(1)}, s32[3,256]{1,0:T(4,128)S(1)}) custom-call(bf16[450,1024]{1,0:T(8,128)(2,1)} %bitcast.7, s32[16,2048]{1,0:T(8,128)} %bitcast.8, f32[16,2048]{1,0:T(8,128)} %bitcast.9, s32[1,2048]{1,0:T(1,128)} %bitcast.10, ...), custom_call_target="tpu_custom_call" | custom-call | tf_op jit(solution)/shard_map/pallas_call | solution.py:115
  6.7 0.3 %collective-permute-done.asked_ref = s32[3,256]{1,0:T(4,128)S(1)} collective-permute-done((s32[3,256]{1,0:T(4,128)}, s32[3,256]{1,0:T(4,128)S(1)}, u32[]{:S(2)}, u32[]{:S(2)}) %collective-permute-start) | collective-permute-done | bytes 3104 | tf_op jit(solution)/shard_map/ppermute | solution.py:40
  7.0 0.4 %shard_map.65.after_ref = bf16[450,256]{1,0:T(8,128)(2,1)S(1)} custom-call(bf16[450,1024]{1,0:T(8,128)(2,1)S(1)} %get-tuple-element.14.grad_ref, s32[3,256]{1,0:T(4,128)S(1)} %collective-permute-done.asked_ref), custom_call_target="tpu_custom_call" | custom-call | flops 3000000000 | tf_op jit(solution)/shard_map/pallas_call | solution.py:164
  7.4 4.5 %collective-permute-start.1 = (bf16[450,256]{1,0:T(8,128)(2,1)S(1)}, bf16[450,256]{1,0:T(8,128)(2,1)S(1)}, u32[]{:S(2)}, u32[]{:S(2)}) collective-permute-start(bf16[450,256]{1,0:T(8,128)(2,1)S(1)} %shard_map.65.after_ref), channel_id=1, source_target_pairs={{0,15},{1,2},{2,1},{3,4},{4,3},{5,6},{6,5},{7,8},{8,7},{9,10},{10,... | collective-permute-start | bytes 691208 | tf_op jit(solution)/shard_map/ppermute | solution.py:40
  11.9 0.0 collective-permute-done.2.asked_ref
  11.9 0.7 %shard_map.66 = (bf16[450,256]{1,0:T(8,128)(2,1)S(1)}, bf16[450,256]{1,0:T(8,128)(2,1)S(1)}) custom-call(bf16[450,1024]{1,0:T(8,128)(2,1)S(1)} %get-tuple-element.14.grad_ref, s32[3,256]{1,0:T(4,128)S(1)} %collective-permute-done.2.asked_ref, s32[3,256]{1,0:T(4,128)S(1)} %get-tuple-element.15.own_ref, bf16[450,256]{1,0:T(8,128)(2,1)S(1)} %shard_map.65.after_ref), custom_call_target="tpu_custom_call" | custom-call | tf_op jit(solution)/shard_map/pallas_call | solution.py:164
  12.5 0.1 collective-permute-start.3
  12.6 2.6 %shard_map.67.w_ref.mid_ref = bf16[768,1280]{1,0:T(8,128)(2,1)S(1)} custom-call(bf16[450,256]{1,0:T(8,128)(2,1)S(1)} %get-tuple-element.17.after_ref, s32[16,2048]{1,0:T(8,128)S(1)} %get-tuple-element.18.pos_ref, f32[16,2048]{1,0:T(8,128)S(1)} %get-tuple-element.19.weight_ref, s32[1,2048]{1,0:T(1,128)S(1)} %get-tuple-element.20.count_ref), custom_call_target="tpu_custom_call" | custom-call | flops 30000001024 | tf_op jit(solution)/shard_map/pallas_call | solution.py:132
  15.2 0.0 collective-permute-done.3.inner_ref
  15.2 0.3 %shard_map.68.part_ref = f32[450,128]{1,0:T(8,128)S(1)} custom-call(bf16[450,256]{1,0:T(8,128)(2,1)S(1)} %get-tuple-element.16.own_ref, bf16[450,256]{1,0:T(8,128)(2,1)S(1)} %collective-permute-done.3.inner_ref, bf16[768,1280]{1,0:T(8,128)(2,1)S(1)} %shard_map.67.w_ref.mid_ref), custom_call_target="tpu_custom_call" | custom-call | flops 1000000000 | tf_op jit(solution)/shard_map/pallas_call | solution.py:191
  15.5 0.3 %collective-permute-done.1.outer_ref = bf16[450,256]{1,0:T(8,128)(2,1)S(1)} collective-permute-done((bf16[450,256]{1,0:T(8,128)(2,1)S(1)}, bf16[450,256]{1,0:T(8,128)(2,1)S(1)}, u32[]{:S(2)}, u32[]{:S(2)}) %collective-permute-start.1) | collective-permute-done | bytes 230432 | tf_op jit(solution)/shard_map/ppermute | solution.py:40
  15.8 0.3 %shard_map.69 = (f32[450,128]{1,0:T(8,128)S(1)}, bf16[240,128]{1,0:T(8,128)(2,1)S(1)}) custom-call(bf16[450,256]{1,0:T(8,128)(2,1)S(1)} %collective-permute-done.1.outer_ref, f32[450,128]{1,0:T(8,128)S(1)} %shard_map.68.part_ref, bf16[768,1280]{1,0:T(8,128)(2,1)S(1)} %shard_map.67.w_ref.mid_ref), custom_call_target="tpu_custom_call" | custom-call | flops 1000000000 | tf_op jit(solution)/shard_map/pallas_call | solution.py:214
  16.1 0.1 collective-permute-start.4
  16.1 0.0 copy-start
  16.2 3.9 %shard_map.70.whole_ref = bf16[450,2048]{1,0:T(8,128)(2,1)} custom-call(bf16[450,256]{1,0:T(8,128)(2,1)S(1)} %collective-permute-done.1.outer_ref, bf16[450,256]{1,0:T(8,128)(2,1)S(1)} %get-tuple-element.16.own_ref, bf16[450,256]{1,0:T(8,128)(2,1)S(1)} %collective-permute-done.3.inner_ref, s32[16,2048]{1,0:T(8,128)S(1)} %get-tuple-element.18.pos_ref, ...), custom_call_target="tpu_custom_call" | custom-call | flops 1000000000 | tf_op jit(solution)/shard_map/pallas_call | solution.py:252
  20.0 1.2 %collective-permute-done.4.mirror_ref = bf16[240,128]{1,0:T(8,128)(2,1)S(1)} collective-permute-done((bf16[240,128]{1,0:T(8,128)(2,1)S(1)}, bf16[240,128]{1,0:T(8,128)(2,1)S(1)}, u32[]{:S(2)}, u32[]{:S(2)}) %collective-permute-start.4) | collective-permute-done | bytes 61472 | tf_op jit(solution)/shard_map/ppermute | solution.py:40
  21.2 0.0 copy-done
  21.2 0.9 %shard_map.71 = bf16[450,2048]{1,0:T(8,128)(2,1)} custom-call(bf16[450,2048]{1,0:T(8,128)(2,1)} %shard_map.70.whole_ref, f32[450,128]{1,0:T(8,128)S(1)} %get-tuple-element.21.after_ref.sum_ref, bf16[240,128]{1,0:T(8,128)(2,1)S(1)} %collective-permute-done.4.mirror_ref, s32[1,64]{1,0:T(1,128)S(1)} %bitcast.6), custom_call_target="tpu_custom_call", output_to_operand_aliasing={{}: (0, {})} | custom-call | tf_op jit(solution)/shard_map/pallas_call | solution.py:278
Async XLA Ops:
  0.0 7.0 %collective-permute-start = (s32[3,256]{1,0:T(4,128)}, s32[3,256]{1,0:T(4,128)S(1)}, u32[]{:S(2)}, u32[]{:S(2)}) collective-permute-start(s32[3,256]{1,0:T(4,128)} %refs_4_.1), channel_id=1, source_target_pairs={{0,15},{1,2},{2,1},{3,4},{4,3},{5,6},{6,5},{7,8},{8,7},{9,10},{10,... | collective-permute-start | bytes 9224 | tf_op jit(solution)/shard_map/ppermute | solution.py:40
  5.4 6.4 %collective-permute-start.2 = (s32[3,256]{1,0:T(4,128)}, s32[3,256]{1,0:T(4,128)S(1)}, u32[]{:S(2)}, u32[]{:S(2)}) collective-permute-start(s32[3,256]{1,0:T(4,128)} %refs_4_.1), channel_id=1, source_target_pairs={{0,1},{1,0},{2,3},{3,2},{4,5},{5,4},{6,7},{7,6},{8,9},{9,8},{10,11... | collective-permute-start | bytes 9224 | tf_op jit(solution)/shard_map/ppermute | solution.py:40
  7.4 8.4 %collective-permute-start.1 = (bf16[450,256]{1,0:T(8,128)(2,1)S(1)}, bf16[450,256]{1,0:T(8,128)(2,1)S(1)}, u32[]{:S(2)}, u32[]{:S(2)}) collective-permute-start(bf16[450,256]{1,0:T(8,128)(2,1)S(1)} %shard_map.65.after_ref), channel_id=1, source_target_pairs={{0,15},{1,2},{2,1},{3,4},{4,3},{5,6},{6,5},{7,8},{8,7},{9,10},{10,... | collective-permute-start | bytes 691208 | tf_op jit(solution)/shard_map/ppermute | solution.py:40
  12.5 2.7 %collective-permute-start.3 = (bf16[450,256]{1,0:T(8,128)(2,1)S(1)}, bf16[450,256]{1,0:T(8,128)(2,1)S(1)}, u32[]{:S(2)}, u32[]{:S(2)}) collective-permute-start(bf16[450,256]{1,0:T(8,128)(2,1)S(1)} %get-tuple-element.17.after_ref), channel_id=1, source_target_pairs={{0,1},{1,0},{2,3},{3,2},{4,5},{5,4},{6,7},{7,6},{8,9},{9,8},{10,11... | collective-permute-start | bytes 691208 | tf_op jit(solution)/shard_map/ppermute | solution.py:40
  16.1 5.2 %collective-permute-start.4 = (bf16[240,128]{1,0:T(8,128)(2,1)S(1)}, bf16[240,128]{1,0:T(8,128)(2,1)S(1)}, u32[]{:S(2)}, u32[]{:S(2)}) collective-permute-start(bf16[240,128]{1,0:T(8,128)(2,1)S(1)} %get-tuple-element.22), channel_id=1, source_target_pairs={{0,8},{1,9},{2,10},{3,11},{4,12},{5,13},{6,14},{7,15},{8,0},{9,1},... | collective-permute-start | bytes 184328 | tf_op jit(solution)/shard_map/ppermute | solution.py:40
  16.1 5.1 %copy-start = (s32[64]{0:T(128)S(1)}, s32[64]{0:T(128)}, u32[]{:S(2)}) copy-start(s32[64]{0:T(128)} %param.11) | copy-start | bytes 772
